TPU v7x, 512 devices: a whole 4x8x8 slice. The times are simulated.
512 devices in a mesh: row: 8 (over y_lo, x), channel: 8 (over y_hi, core), sample: 8 (over z).
Axes of the slice: x: 4, y: 8 (y_hi: 4, y_lo: 2; y = y_hi * 2 + y_lo), z: 8, core: 2. Of those that a mesh axis runs over, the one named last changes fastest.
Arguments:
- features: bfloat16 [8, 48, 72, 2048], P('sample', 'row', None, 'channel'), may hold values from -6 to 6
- weights: bfloat16 [256, 3, 9, 2048], P('sample', None, None, 'channel'), may hold values from -0.046875 to 0.046875
- proj: bfloat16 [768, 256], replicated, may hold values from -0.21875 to 0.21875
- classify: bfloat16 [256, 3], replicated, may hold values from -0.375 to 0.375
- labels: int32 [8, 48, 72], P('sample', 'row'), may hold values from 0 to 2
Outputs:
- weight_grad: bfloat16 [256, 3, 9, 2048], P('sample', None, None, 'channel')
All inputs are finite; a program needn't handle non-finite values.
Results may differ from a plain program's by a relative error of at most 0.03.
Values may be sent and summed in bfloat16 or wider, within the bound.
No kernel may reach another device: no remote copies, remote signals or barrier semaphores. Data moves between devices by JAX's collectives and lax.ppermute only.
A program may use at most 64 MiB of HBM per device.

v0:
```python
import jax
import jax.numpy as jnp
from jax import lax
from jax.sharding import PartitionSpec as P


def passed_along(value, axis, by):
    devices = lax.axis_size(axis)
    pairs = [(i, i + by) for i in range(devices) if 0 <= i + by < devices]
    return lax.ppermute(value, axis, pairs)


def swish_grad(values):
    gate_value = jax.nn.sigmoid(values)
    return gate_value * (1.0 + values * (1.0 - gate_value))


def tail_grad(preact, proj, classify, flat_labels):
    pixel_count = preact.shape[0]
    activated = jax.nn.silu(preact).astype(jnp.bfloat16).reshape(pixel_count, -1)
    mixed_pre = jnp.dot(activated, proj, preferred_element_type=jnp.float32)
    hidden = jax.nn.silu(mixed_pre).astype(jnp.bfloat16)
    logits = jnp.dot(hidden, classify, preferred_element_type=jnp.float32)
    exp_logits = jnp.exp(logits)
    probabilities = exp_logits / jnp.sum(exp_logits, axis=1, keepdims=True)
    classes_row = jnp.arange(classify.shape[1], dtype=jnp.int32)
    onehot = (flat_labels[:, None] == classes_row[None, :]).astype(jnp.float32)
    dlogits = (probabilities - onehot).astype(jnp.bfloat16)
    grad_hidden = lax.dot_general(
        dlogits, classify, (((1,), (1,)), ((), ())), preferred_element_type=jnp.float32
    )
    grad_mixed = (grad_hidden * swish_grad(mixed_pre)).astype(jnp.bfloat16)
    grad_act = lax.dot_general(
        grad_mixed, proj, (((1,), (1,)), ((), ())), preferred_element_type=jnp.float32
    )
    return (grad_act.reshape(preact.shape) * swish_grad(preact)).astype(jnp.bfloat16)


def shards(features, weights, proj, classify, labels):
    sample_count, row_count, col_count, chan_count = features.shape
    dilation = 2 * row_count
    shifted = {}
    for offset in range(-3, 4):
        if offset == 0:
            shifted[offset] = features
        else:
            shifted[offset] = passed_along(features, "row", -2 * offset)

    def pick_tap(branch, tap_index):
        tap_row = tap_index // 3
        tap_col = tap_index % 3
        offset_cols = (branch + 1) * dilation * (tap_col - 1)
        source = shifted[(branch + 1) * (tap_row - 1)]
        if offset_cols > 0:
            moved = jnp.pad(
                source[:, :, offset_cols:, :], ((0, 0), (0, 0), (0, offset_cols), (0, 0))
            )
        elif offset_cols < 0:
            moved = jnp.pad(
                source[:, :, : col_count + offset_cols, :],
                ((0, 0), (0, 0), (-offset_cols, 0), (0, 0)),
            )
        else:
            moved = source
        return moved.reshape(-1, chan_count)

    def branch_pre(branch, kernels):
        running = None
        for tap_index in range(9):
            contrib = lax.dot_general(
                pick_tap(branch, tap_index),
                kernels[:, tap_index, :],
                (((1,), (1,)), ((), ())),
                preferred_element_type=jnp.float32,
            )
            running = contrib if running is None else running + contrib
        return running

    portion = lax.all_gather(weights, "sample", axis=0, tiled=True)
    partial_pre = jnp.stack([branch_pre(branch, portion[:, branch]) for branch in range(3)], axis=1)
    flat_labels = labels.reshape(-1)
    preact = lax.psum(partial_pre.astype(jnp.bfloat16), "channel").astype(jnp.float32)
    grad_pre = tail_grad(preact, proj, classify, flat_labels)
    grad_blocks = []
    for branch in range(3):
        for tap_index in range(9):
            grad_blocks.append(
                lax.dot_general(
                    grad_pre[:, branch, :],
                    pick_tap(branch, tap_index),
                    (((0,), (0,)), ((), ())),
                    preferred_element_type=jnp.float32,
                )
            )
    sample_summed = lax.psum_scatter(
        jnp.stack(grad_blocks, axis=1)
        .reshape(weights.shape[0] * lax.axis_size("sample"), 3, 9, chan_count)
        .astype(jnp.bfloat16),
        "sample",
        scatter_dimension=0,
        tiled=True,
    )
    row_summed = lax.psum(sample_summed, "row").astype(jnp.float32)
    return row_summed.astype(jnp.bfloat16)


def solution(mesh):
    in_specs = (
        P("sample", "row", None, "channel"),
        P("sample", None, None, "channel"),
        P(),
        P(),
        P("sample", "row", None),
    )
    out_specs = P("sample", None, None, "channel")
    return jax.shard_map(shards, mesh=mesh, in_specs=in_specs, out_specs=out_specs, check_vma=False)
```

profile of v0, /device:TPU:1, one launch (start us, length us, event | category | flops | bytes accessed | tf_op | source)
XLA Modules:
  0.0 331.0 jit_solution(8349586133848180792)
XLA Ops:
  7.3 5.5 %collective-permute-start = (bf16[1,6,72,256]{3,2,1,0:T(8,128)(2,1)}, bf16[1,6,72,256]{3,2,1,0:T(8,128)(2,1)S(1)}, u32[]{:S(2)}, u32[]{:S(2)}) collective-permute-start(bf16[1,6,72,256]{3,2,1,0:T(8,128)(2,1)} %param.5), channel_id=1, source_target_pairs={{0,128},{64,192},{128,256},{192,320},{256,384},{320,448},{1,129},{... | collective-permute-start | bytes 663560 | tf_op jit(solution)/shard_map/ppermute | solution.py:10
  12.8 1.3 collective-permute-start.1
  14.1 5.0 %collective-permute-start.2 = (bf16[1,6,72,256]{3,2,1,0:T(8,128)(2,1)}, bf16[1,6,72,256]{3,2,1,0:T(8,128)(2,1)S(1)}, u32[]{:S(2)}, u32[]{:S(2)}) collective-permute-start(bf16[1,6,72,256]{3,2,1,0:T(8,128)(2,1)} %param.5), channel_id=1, source_target_pairs={{0,256},{64,320},{128,384},{192,448},{1,257},{65,321},{129,385},{1... | collective-permute-start | bytes 663560 | tf_op jit(solution)/shard_map/ppermute | solution.py:10
  19.1 1.3 collective-permute-start.3
  20.4 5.6 %collective-permute-start.4 = (bf16[1,6,72,256]{3,2,1,0:T(8,128)(2,1)}, bf16[1,6,72,256]{3,2,1,0:T(8,128)(2,1)S(1)}, u32[]{:S(2)}, u32[]{:S(2)}) collective-permute-start(bf16[1,6,72,256]{3,2,1,0:T(8,128)(2,1)} %param.5), channel_id=1, source_target_pairs={{0,384},{64,448},{1,385},{65,449},{2,386},{66,450},{3,387},{67,451... | collective-permute-start | bytes 663560 | tf_op jit(solution)/shard_map/ppermute | solution.py:10
  26.0 1.1 fusion.112
  27.2 1.1 fusion.115
  31.2 1.3 collective-permute-start.5
  32.8 0.8 pad.82
  36.6 3.7 %collective-permute-done.5 = bf16[1,6,72,256]{3,2,1,0:T(8,128)(2,1)S(1)} collective-permute-done((bf16[1,6,72,256]{3,2,1,0:T(8,128)(2,1)S(1)}, bf16[1,6,72,256]{3,2,1,0:T(8,128)(2,1)S(1)}, u32[]{:S(2)}, u32[]{:S(2)}) %collective-permute-start.5) | collective-permute-done | bytes 221216 | tf_op jit(solution)/shard_map/ppermute | solution.py:10
  40.3 0.8 pad.95
  41.8 25.2 %all-gather.2.cloned.1.call-done = bf16[256,3,9,256]{3,0,2,1:T(8,128)(2,1)} async-done(((bf16[32,3,9,256]{3,0,2,1:T(8,128)(2,1)}), bf16[256,3,9,256]{3,0,2,1:T(8,128)(2,1)}) %all-gather.2.cloned.1.call-update) | async-done | bytes 3538960 | tf_op jit(solution)/shard_map/all_gather | solution.py:79
  67.1 2.2 slice_bitcast_fusion.2
  76.5 0.9 pad_maximum_fusion
  77.8 77.4 %all-reduce.21.cloned.1.call-done = bf16[432,3,256]{2,0,1:T(8,128)(2,1)} async-done(((bf16[432,3,256]{2,0,1:T(8,128)(2,1)}), bf16[432,3,256]{2,0,1:T(8,128)(2,1)}) %all-reduce.21.cloned.1.call-update) | async-done | bytes 663568 | tf_op jit(solution)/shard_map/psum | solution.py:82
  155.3 1.5 fusion.3
  157.7 1.8 fusion.24
  159.5 1.9 copy.8
  162.0 1.9 fusion.29
  163.9 0.9 fusion.31
  164.8 0.9 fusion.33
  165.8 0.9 fusion.35
  166.7 0.9 fusion.37
  167.7 0.9 fusion.39
  168.6 0.9 fusion.41
  169.5 0.9 fusion.43
  170.5 0.9 fusion.45
  171.4 0.9 fusion.47
  172.3 0.9 fusion.49
  173.3 0.9 fusion.51
  174.2 0.9 fusion.53
  175.1 0.9 fusion.55
  176.1 0.9 fusion.57
  177.0 0.9 fusion.59
  178.0 0.9 fusion.61
  178.9 0.9 fusion.63
  179.8 0.9 fusion.65
  180.8 0.9 fusion.67
  181.7 0.9 fusion.69
  182.6 0.9 fusion.71
  183.6 0.9 fusion.73
  184.5 0.9 fusion.75
  185.5 0.9 fusion.77
  186.4 0.9 fusion.79
  187.3 0.9 fusion.81
  188.3 52.4 %reduce-scatter.2.cloned.1.call-done = bf16[32,3,9,256]{3,0,2,1:T(8,128)(2,1)} async-done(((bf16[256,3,9,256]{3,0,2,1:T(8,128)(2,1)}), bf16[32,3,9,256]{3,0,2,1:T(8,128)(2,1)}) %reduce-scatter.2.cloned.1.call-update) | async-done | bytes 442384 | tf_op jit(solution)/shard_map/reduce_scatter | solution.py:95
  240.8 81.9 %all-reduce.23.cloned.1.call-done = bf16[32,3,9,256]{3,0,2,1:T(8,128)(2,1)} async-done(((bf16[32,3,9,256]{3,0,2,1:T(8,128)(2,1)}), bf16[32,3,9,256]{3,0,2,1:T(8,128)(2,1)}) %all-reduce.23.cloned.1.call-update) | async-done | bytes 442384 | tf_op jit(solution)/shard_map/psum | solution.py:103
  322.7 1.8 copy.38
  (157 shorter events, 16.4 us)
Async XLA Ops:
  6.5 150.5 %copy-start = (bf16[768,256]{1,0:T(8,128)(2,1)S(1)}, bf16[768,256]{1,0:T(8,128)(2,1)}, u32[]{:S(2)}) copy-start(bf16[768,256]{1,0:T(8,128)(2,1)} %param.7) | copy-start | bytes 1179652
  6.5 23.2 %copy-start.1 = (bf16[1,6,72,256]{3,2,1,0:T(8,128)(2,1)S(1)}, bf16[1,6,72,256]{3,2,1,0:T(8,128)(2,1)}, u32[]{:S(2)}) copy-start(bf16[1,6,72,256]{3,2,1,0:T(8,128)(2,1)} %param.5) | copy-start | bytes 663556
  6.5 60.5 %all-gather.2.cloned.1.call-start = ((), (), s32[]{:S(2)}) async-start(), calls=%async_computation.1 | async-start | bytes 3981312 | tf_op jit(solution)/shard_map/all_gather | solution.py:79
  7.3 148.0 %all-reduce.21.cloned.1.call-start = ((), (), s32[]{:S(2)}) async-start(), calls=%async_computation.2 | async-start | bytes 1327104 | tf_op jit(solution)/shard_map/psum | solution.py:82
  7.3 23.9 %collective-permute-start = (bf16[1,6,72,256]{3,2,1,0:T(8,128)(2,1)}, bf16[1,6,72,256]{3,2,1,0:T(8,128)(2,1)S(1)}, u32[]{:S(2)}, u32[]{:S(2)}) collective-permute-start(bf16[1,6,72,256]{3,2,1,0:T(8,128)(2,1)} %param.5), channel_id=1, source_target_pairs={{0,128},{64,192},{128,256},{192,320},{256,384},{320,448},{1,129},{... | collective-permute-start | bytes 663560 | tf_op jit(solution)/shard_map/ppermute | solution.py:10
  12.8 19.9 %collective-permute-start.1 = (bf16[1,6,72,256]{3,2,1,0:T(8,128)(2,1)}, bf16[1,6,72,256]{3,2,1,0:T(8,128)(2,1)S(1)}, u32[]{:S(2)}, u32[]{:S(2)}) collective-permute-start(bf16[1,6,72,256]{3,2,1,0:T(8,128)(2,1)} %param.5), channel_id=1, source_target_pairs={{128,0},{192,64},{256,128},{320,192},{384,256},{448,320},{129,1},{... | collective-permute-start | bytes 663560 | tf_op jit(solution)/shard_map/ppermute | solution.py:10
  14.1 19.4 %collective-permute-start.2 = (bf16[1,6,72,256]{3,2,1,0:T(8,128)(2,1)}, bf16[1,6,72,256]{3,2,1,0:T(8,128)(2,1)S(1)}, u32[]{:S(2)}, u32[]{:S(2)}) collective-permute-start(bf16[1,6,72,256]{3,2,1,0:T(8,128)(2,1)} %param.5), channel_id=1, source_target_pairs={{0,256},{64,320},{128,384},{192,448},{1,257},{65,321},{129,385},{1... | collective-permute-start | bytes 663560 | tf_op jit(solution)/shard_map/ppermute | solution.py:10
  19.1 15.3 %collective-permute-start.3 = (bf16[1,6,72,256]{3,2,1,0:T(8,128)(2,1)}, bf16[1,6,72,256]{3,2,1,0:T(8,128)(2,1)S(1)}, u32[]{:S(2)}, u32[]{:S(2)}) collective-permute-start(bf16[1,6,72,256]{3,2,1,0:T(8,128)(2,1)} %param.5), channel_id=1, source_target_pairs={{256,0},{320,64},{384,128},{448,192},{257,1},{321,65},{385,129},{4... | collective-permute-start | bytes 663560 | tf_op jit(solution)/shard_map/ppermute | solution.py:10
  20.4 15.4 %collective-permute-start.4 = (bf16[1,6,72,256]{3,2,1,0:T(8,128)(2,1)}, bf16[1,6,72,256]{3,2,1,0:T(8,128)(2,1)S(1)}, u32[]{:S(2)}, u32[]{:S(2)}) collective-permute-start(bf16[1,6,72,256]{3,2,1,0:T(8,128)(2,1)} %param.5), channel_id=1, source_target_pairs={{0,384},{64,448},{1,385},{65,449},{2,386},{66,450},{3,387},{67,451... | collective-permute-start | bytes 663560 | tf_op jit(solution)/shard_map/ppermute | solution.py:10
  27.1 42.4 %copy-start.14 = (bf16[1,6,72,256]{3,2,1,0:T(8,128)(2,1)}, bf16[1,6,72,256]{3,2,1,0:T(8,128)(2,1)S(1)}, u32[]{:S(2)}) copy-start(bf16[1,6,72,256]{3,2,1,0:T(8,128)(2,1)S(1)} %pad.80) | copy-start | bytes 663556
  27.2 47.7 %copy-start.12 = (bf16[1,6,72,256]{3,2,1,0:T(8,128)(2,1)}, bf16[1,6,72,256]{3,2,1,0:T(8,128)(2,1)S(1)}, u32[]{:S(2)}) copy-start(bf16[1,6,72,256]{3,2,1,0:T(8,128)(2,1)S(1)} %pad.81) | copy-start | bytes 663556
  31.2 9.1 %collective-permute-start.5 = (bf16[1,6,72,256]{3,2,1,0:T(8,128)(2,1)S(1)}, bf16[1,6,72,256]{3,2,1,0:T(8,128)(2,1)S(1)}, u32[]{:S(2)}, u32[]{:S(2)}) collective-permute-start(bf16[1,6,72,256]{3,2,1,0:T(8,128)(2,1)S(1)} %copy-done.1), channel_id=1, source_target_pairs={{384,0},{448,64},{385,1},{449,65},{386,2},{450,66},{387,3},{451,67... | collective-permute-start | bytes 663560 | tf_op jit(solution)/shard_map/ppermute | solution.py:10
  32.6 36.7 %copy-start.18 = (bf16[1,6,72,256]{3,2,1,0:T(8,128)(2,1)}, bf16[1,6,72,256]{3,2,1,0:T(8,128)(2,1)S(1)}, u32[]{:S(2)}) copy-start(bf16[1,6,72,256]{3,2,1,0:T(8,128)(2,1)S(1)} %pad.79) | copy-start | bytes 663556
  32.7 38.7 %copy-start.7 = (bf16[1,6,72,256]{3,2,1,0:T(8,128)(2,1)}, bf16[1,6,72,256]{3,2,1,0:T(8,128)(2,1)S(1)}, u32[]{:S(2)}) copy-start(bf16[1,6,72,256]{3,2,1,0:T(8,128)(2,1)S(1)} %pad.78) | copy-start | bytes 663556
  32.8 37.3 %copy-start.16 = (bf16[1,6,72,256]{3,2,1,0:T(8,128)(2,1)}, bf16[1,6,72,256]{3,2,1,0:T(8,128)(2,1)S(1)}, u32[]{:S(2)}) copy-start(bf16[1,6,72,256]{3,2,1,0:T(8,128)(2,1)S(1)} %pad.83) | copy-start | bytes 663556
  34.3 37.7 %copy-start.10 = (bf16[1,6,72,256]{3,2,1,0:T(8,128)(2,1)}, bf16[1,6,72,256]{3,2,1,0:T(8,128)(2,1)S(1)}, u32[]{:S(2)}) copy-start(bf16[1,6,72,256]{3,2,1,0:T(8,128)(2,1)S(1)} %pad.84) | copy-start | bytes 663556
  35.8 37.8 %copy-start.3 = (bf16[1,6,72,256]{3,2,1,0:T(8,128)(2,1)}, bf16[1,6,72,256]{3,2,1,0:T(8,128)(2,1)S(1)}, u32[]{:S(2)}) copy-start(bf16[1,6,72,256]{3,2,1,0:T(8,128)(2,1)S(1)} %collective-permute-done.4) | copy-start | bytes 663556
  36.6 37.2 %copy-start.8 = (bf16[1,6,72,256]{3,2,1,0:T(8,128)(2,1)}, bf16[1,6,72,256]{3,2,1,0:T(8,128)(2,1)S(1)}, u32[]{:S(2)}) copy-start(bf16[1,6,72,256]{3,2,1,0:T(8,128)(2,1)S(1)} %pad.90) | copy-start | bytes 663556
  40.3 34.3 %copy-start.5 = (bf16[1,6,72,256]{3,2,1,0:T(8,128)(2,1)}, bf16[1,6,72,256]{3,2,1,0:T(8,128)(2,1)S(1)}, u32[]{:S(2)}) copy-start(bf16[1,6,72,256]{3,2,1,0:T(8,128)(2,1)S(1)} %collective-permute-done.5) | copy-start | bytes 663556
  72.5 1.9 copy-start.28
  73.5 1.6 copy-start.24
  73.8 1.6 copy-start.20
  74.1 1.6 copy-start.36
  74.4 1.6 copy-start.40
  75.7 2.0 copy-start.42
  76.5 80.9 %copy-start.43 = (bf16[256,3]{0,1:T(4,128)(2,1)S(1)}, bf16[256,3]{0,1:T(4,128)(2,1)}, u32[]{:S(2)}) copy-start(bf16[256,3]{0,1:T(4,128)(2,1)} %param.8) | copy-start | bytes 4612
  77.5 163.3 %reduce-scatter.2.cloned.1.call-start = ((), (), s32[]{:S(2)}) async-start(), calls=%async_computation.3 | async-start | bytes 3981312 | tf_op jit(solution)/shard_map/reduce_scatter | solution.py:95
  157.5 3.9 %copy-start.2 = (bf16[432,3,256]{2,0,1:T(8,128)(2,1)S(1)}, bf16[432,3,256]{2,0,1:T(8,128)(2,1)}, u32[]{:S(2)}) copy-start(bf16[432,3,256]{2,0,1:T(8,128)(2,1)} %all-reduce.21.cloned.1.call-done) | copy-start | bytes 1990660
  161.4 3.4 %copy-start.19 = (bf16[1,6,72,256]{3,2,1,0:T(8,128)(2,1)S(1)}, bf16[1,6,72,256]{3,2,1,0:T(8,128)(2,1)}, u32[]{:S(2)}) copy-start(bf16[1,6,72,256]{3,2,1,0:T(8,128)(2,1)} %copy-done.18) | copy-start | bytes 663556
  161.4 4.4 %copy-start.15 = (bf16[1,6,72,256]{3,2,1,0:T(8,128)(2,1)S(1)}, bf16[1,6,72,256]{3,2,1,0:T(8,128)(2,1)}, u32[]{:S(2)}) copy-start(bf16[1,6,72,256]{3,2,1,0:T(8,128)(2,1)} %copy-done.14) | copy-start | bytes 663556
  161.4 6.2 %copy-start.13 = (bf16[1,6,72,256]{3,2,1,0:T(8,128)(2,1)S(1)}, bf16[1,6,72,256]{3,2,1,0:T(8,128)(2,1)}, u32[]{:S(2)}) copy-start(bf16[1,6,72,256]{3,2,1,0:T(8,128)(2,1)} %copy-done.12) | copy-start | bytes 663556
  161.4 7.2 %copy-start.37 = (bf16[1,6,72,256]{3,2,1,0:T(8,128)(2,1)S(1)}, bf16[1,6,72,256]{3,2,1,0:T(8,128)(2,1)}, u32[]{:S(2)}) copy-start(bf16[1,6,72,256]{3,2,1,0:T(8,128)(2,1)} %pad.82) | copy-start | bytes 663556
  162.0 8.5 %copy-start.17 = (bf16[1,6,72,256]{3,2,1,0:T(8,128)(2,1)S(1)}, bf16[1,6,72,256]{3,2,1,0:T(8,128)(2,1)}, u32[]{:S(2)}) copy-start(bf16[1,6,72,256]{3,2,1,0:T(8,128)(2,1)} %copy-done.16) | copy-start | bytes 663556
  162.0 9.4 %copy-start.11 = (bf16[1,6,72,256]{3,2,1,0:T(8,128)(2,1)S(1)}, bf16[1,6,72,256]{3,2,1,0:T(8,128)(2,1)}, u32[]{:S(2)}) copy-start(bf16[1,6,72,256]{3,2,1,0:T(8,128)(2,1)} %copy-done.10) | copy-start | bytes 663556
  164.8 8.4 %copy-start.35 = (bf16[1,6,72,256]{3,2,1,0:T(8,128)(2,1)S(1)}, bf16[1,6,72,256]{3,2,1,0:T(8,128)(2,1)}, u32[]{:S(2)}) copy-start(bf16[1,6,72,256]{3,2,1,0:T(8,128)(2,1)} %pad.85) | copy-start | bytes 663556
  165.8 8.4 %copy-start.27 = (bf16[1,6,72,256]{3,2,1,0:T(8,128)(2,1)S(1)}, bf16[1,6,72,256]{3,2,1,0:T(8,128)(2,1)}, u32[]{:S(2)}) copy-start(bf16[1,6,72,256]{3,2,1,0:T(8,128)(2,1)} %pad.86) | copy-start | bytes 663556
  167.7 8.4 %copy-start.25 = (bf16[1,6,72,256]{3,2,1,0:T(8,128)(2,1)S(1)}, bf16[1,6,72,256]{3,2,1,0:T(8,128)(2,1)}, u32[]{:S(2)}) copy-start(bf16[1,6,72,256]{3,2,1,0:T(8,128)(2,1)} %pad.87) | copy-start | bytes 663556
  168.6 8.4 %copy-start.41 = (bf16[1,6,72,256]{3,2,1,0:T(8,128)(2,1)S(1)}, bf16[1,6,72,256]{3,2,1,0:T(8,128)(2,1)}, u32[]{:S(2)}) copy-start(bf16[1,6,72,256]{3,2,1,0:T(8,128)(2,1)} %pad.88) | copy-start | bytes 663556
  170.5 8.4 %copy-start.31 = (bf16[1,6,72,256]{3,2,1,0:T(8,128)(2,1)S(1)}, bf16[1,6,72,256]{3,2,1,0:T(8,128)(2,1)}, u32[]{:S(2)}) copy-start(bf16[1,6,72,256]{3,2,1,0:T(8,128)(2,1)} %pad.89) | copy-start | bytes 663556
  171.4 8.4 %copy-start.9 = (bf16[1,6,72,256]{3,2,1,0:T(8,128)(2,1)S(1)}, bf16[1,6,72,256]{3,2,1,0:T(8,128)(2,1)}, u32[]{:S(2)}) copy-start(bf16[1,6,72,256]{3,2,1,0:T(8,128)(2,1)} %copy-done.8) | copy-start | bytes 663556
  172.3 8.4 %copy-start.4 = (bf16[1,6,72,256]{3,2,1,0:T(8,128)(2,1)S(1)}, bf16[1,6,72,256]{3,2,1,0:T(8,128)(2,1)}, u32[]{:S(2)}) copy-start(bf16[1,6,72,256]{3,2,1,0:T(8,128)(2,1)} %copy-done.3) | copy-start | bytes 663556
  173.3 8.4 %copy-start.33 = (bf16[1,6,72,256]{3,2,1,0:T(8,128)(2,1)S(1)}, bf16[1,6,72,256]{3,2,1,0:T(8,128)(2,1)}, u32[]{:S(2)}) copy-start(bf16[1,6,72,256]{3,2,1,0:T(8,128)(2,1)} %pad.91) | copy-start | bytes 663556
  174.2 8.4 %copy-start.23 = (bf16[1,6,72,256]{3,2,1,0:T(8,128)(2,1)S(1)}, bf16[1,6,72,256]{3,2,1,0:T(8,128)(2,1)}, u32[]{:S(2)}) copy-start(bf16[1,6,72,256]{3,2,1,0:T(8,128)(2,1)} %pad.92) | copy-start | bytes 663556
  176.1 8.4 %copy-start.21 = (bf16[1,6,72,256]{3,2,1,0:T(8,128)(2,1)S(1)}, bf16[1,6,72,256]{3,2,1,0:T(8,128)(2,1)}, u32[]{:S(2)}) copy-start(bf16[1,6,72,256]{3,2,1,0:T(8,128)(2,1)} %pad.93) | copy-start | bytes 663556
  177.0 8.4 %copy-start.39 = (bf16[1,6,72,256]{3,2,1,0:T(8,128)(2,1)S(1)}, bf16[1,6,72,256]{3,2,1,0:T(8,128)(2,1)}, u32[]{:S(2)}) copy-start(bf16[1,6,72,256]{3,2,1,0:T(8,128)(2,1)} %pad.94) | copy-start | bytes 663556
  178.0 8.5 %copy-start.6 = (bf16[1,6,72,256]{3,2,1,0:T(8,128)(2,1)S(1)}, bf16[1,6,72,256]{3,2,1,0:T(8,128)(2,1)}, u32[]{:S(2)}) copy-start(bf16[1,6,72,256]{3,2,1,0:T(8,128)(2,1)} %copy-done.5) | copy-start | bytes 663556
  178.9 8.4 %copy-start.29 = (bf16[1,6,72,256]{3,2,1,0:T(8,128)(2,1)S(1)}, bf16[1,6,72,256]{3,2,1,0:T(8,128)(2,1)}, u32[]{:S(2)}) copy-start(bf16[1,6,72,256]{3,2,1,0:T(8,128)(2,1)} %pad.95) | copy-start | bytes 663556
  188.3 134.4 %all-reduce.23.cloned.1.call-start = ((), (), s32[]{:S(2)}) async-start(), calls=%async_computation.4 | async-start | bytes 884736 | tf_op jit(solution)/shard_map/psum | solution.py:103
  (6 other events, 8.3 us)
Sparse Core Ops, SparseCore 0:
  9.4 57.5 all-gather.1
  77.6 77.6 all-reduce.20
  188.4 52.3 reduce-scatter.1
  243.8 78.8 all-reduce.22
where the time goes:
time: 335 us; the launch traced here: 331 us
  waiting for transfers between devices  241 us (72%)
  matrix products  35.4 us (11%)
  starting transfers between devices  20.2 us (6%)
  local copies, waits for them, and re-layouts  17.1 us (5%)
  between operations  14 us (4%)
    psum x1, waiting for transfers between devices, shards(): row_summed = lax.psum(sample_summed, 'row').astype(jnp.float32)  81.9 us
    psum x1, waiting for transfers between devices, shards(): lax.psum(partial_pre.astype(jnp.bfloat16), 'channel').astype(jnp.float32)  77.4 us
    reduce_scatter x1, waiting for transfers between devices, shards(): lax.psum_scatter(jnp.stack(grad_blocks, axis=1).reshape(weights.shape[0]...  52.4 us
    dot_general x27, matrix products, shards(): lax.dot_general(grad_pre[:, branch, :], pick_tap(branch, tap_index), (((0...  26.2 us
    all_gather x1, waiting for transfers between devices, shards(): portion = lax.all_gather(weights, 'sample', axis=0, tiled=True)  25.2 us
    ppermute x6, starting transfers between devices, passed_along(): return lax.ppermute(value, axis, pairs)  19.9 us
    dot_general x27, matrix products, branch_pre(): lax.dot_general(pick_tap(branch, tap_index), kernels[:, tap_index, :], ((...  6.72 us
  transfers between devices with their start and end apart: 10, of which 5 were waited for; matrix products, arithmetic and copies ran while one was open for 3% of the time, Pallas kernels for 0%

commit v1 on v0

v1 whole, which is shorter than its diff:
```python
import jax
import jax.numpy as jnp
from jax import lax
from jax.experimental import pallas as pl
from jax.experimental.pallas import tpu as pltpu
from jax.sharding import Mesh, PartitionSpec as P

BF16 = jnp.bfloat16
F32 = jnp.float32

ROWS = 8
GRID_J = 4
GRID_Q = 6
UNIT = 72
UNITS = GRID_J * GRID_Q
HALF = UNITS * UNIT
PARTS = 32
SHARE = 56
PADDED = PARTS * SHARE
LANES = 128
CHAN = 256
OUTS = 32
TAPS = 27
ROW_AXES = ("row",)
VMEM_LIMIT = 48 * 1024 * 1024


def block_taps(j, q):
    found = []
    for branch in range(3):
        rate = branch + 1
        for tap_row in range(3):
            out_j = j - rate * (tap_row - 1)
            if not 0 <= out_j < GRID_J:
                continue
            for tap_col in range(3):
                out_q = q - rate * (tap_col - 1)
                if not 0 <= out_q < GRID_Q:
                    continue
                found.append((9 * branch + 3 * tap_row + tap_col, branch, out_j * GRID_Q + out_q))
    return found


def compiler_params():
    return pltpu.CompilerParams(vmem_limit_bytes=VMEM_LIMIT)


def prepare_kernel(features_ref, out_ref, rows_ref, units_ref):
    rows_ref[...] = features_ref[...].astype(F32)
    for row in range(6):
        for q in range(GRID_Q):
            units_ref[q * UNIT + row * 12 : q * UNIT + row * 12 + 12, :] = rows_ref[
                row * 72 + q * 12 : row * 72 + q * 12 + 12, :
            ]
    for q in range(GRID_Q):
        unit = units_ref[q * UNIT : (q + 1) * UNIT, :].astype(BF16)
        for device in range(ROWS):
            out_ref[device, q] = unit


def prepare(features):
    return pl.pallas_call(
        prepare_kernel,
        out_shape=jax.ShapeDtypeStruct((ROWS, GRID_Q, UNIT, CHAN), BF16),
        scratch_shapes=[pltpu.VMEM((432, CHAN), F32), pltpu.VMEM((432, CHAN), F32)],
        compiler_params=compiler_params(),
        cost_estimate=pl.CostEstimate(flops=0, bytes_accessed=2 * 9 * 432 * CHAN, transcendentals=0),
        name="prepare_features",
    )(features)


def forward_kernel(parity_ref, features_ref, weights_ref, out_ref, acc_ref, flat_ref):
    del parity_ref
    acc_ref[...] = jnp.zeros(acc_ref.shape, F32)
    for j in range(GRID_J):
        for q in range(GRID_Q):
            taps = block_taps(j, q)
            kernels = jnp.concatenate(
                [weights_ref[tap * OUTS : (tap + 1) * OUTS, :] for tap, _, _ in taps], axis=0
            )
            product = lax.dot_general(
                kernels, features_ref[j, 0, q], (((1,), (1,)), ((), ())), preferred_element_type=F32
            )
            for place, (_, branch, block) in enumerate(taps):
                acc_ref[block, branch * OUTS : (branch + 1) * OUTS, :UNIT] += product[
                    place * OUTS : (place + 1) * OUTS, :
                ]
    for block in range(UNITS):
        flat_ref[block * UNIT : (block + 1) * UNIT, :] = jnp.transpose(acc_ref[block])[:UNIT, :]
    flat_ref[HALF:, :] = jnp.zeros((PADDED - HALF, LANES), F32)
    out_ref[...] = flat_ref[...].astype(BF16)


def forward(parity, features, weights):
    return pl.pallas_call(
        forward_kernel,
        grid_spec=pltpu.PrefetchScalarGridSpec(
            num_scalar_prefetch=1,
            grid=(1,),
            in_specs=[
                pl.BlockSpec((GRID_J, 1, GRID_Q, UNIT, CHAN), lambda i, p: (0, p[0], 0, 0, 0)),
                pl.BlockSpec((TAPS * OUTS, CHAN), lambda i, p: (0, 0)),
            ],
            out_specs=pl.BlockSpec((PADDED, LANES), lambda i, p: (0, 0)),
            scratch_shapes=[
                pltpu.VMEM((UNITS, LANES, LANES), F32),
                pltpu.VMEM((PADDED, LANES), F32),
            ],
        ),
        out_shape=jax.ShapeDtypeStruct((PADDED, LANES), BF16),
        compiler_params=compiler_params(),
        cost_estimate=pl.CostEstimate(
            flops=2 * HALF * CHAN * TAPS * OUTS, bytes_accessed=2000000, transcendentals=0
        ),
        name="forward_taps",
    )(parity, features, weights)


def sigmoid(values):
    return 1.0 / (1.0 + jnp.exp(-values))


def swish_grad(values, gate_value):
    return gate_value * (1.0 + values * (1.0 - gate_value))


def tail_kernel(parts_ref, proj_ref, classify_ref, classify_t_ref, onehot_ref, out_ref):
    pre = []
    for row in range(ROWS):
        total = parts_ref[row].astype(F32)
        for part in range(1, PARTS // ROWS):
            total = total + parts_ref[part * ROWS + row].astype(F32)
        pre.append(total)
    preact = jnp.concatenate(pre, axis=1)
    gate = sigmoid(preact)
    activated = (preact * gate).astype(BF16)
    mixed_pre = jnp.dot(activated, proj_ref[...], preferred_element_type=F32)
    mixed_gate = sigmoid(mixed_pre)
    hidden = (mixed_pre * mixed_gate).astype(BF16)
    logits = jnp.dot(hidden, classify_ref[...], preferred_element_type=F32)
    lane = lax.broadcasted_iota(jnp.int32, logits.shape, 1)
    exp_logits = jnp.where(lane < 3, jnp.exp(logits), 0.0)
    probabilities = exp_logits / jnp.sum(exp_logits, axis=1, keepdims=True)
    dlogits = (probabilities - onehot_ref[...]).astype(BF16)
    grad_hidden = jnp.dot(dlogits, classify_t_ref[...], preferred_element_type=F32)
    grad_mixed = (grad_hidden * swish_grad(mixed_pre, mixed_gate)).astype(BF16)
    grad_act = lax.dot_general(
        grad_mixed, proj_ref[...], (((1,), (1,)), ((), ())), preferred_element_type=F32
    )
    grad_pre = (grad_act * swish_grad(preact, gate)).astype(BF16)
    for row in range(ROWS):
        block = grad_pre[:, row * LANES : (row + 1) * LANES]
        for part in range(PARTS // ROWS):
            out_ref[part * ROWS + row] = block


def tail(parts, proj, classify, classify_t, onehot):
    return pl.pallas_call(
        tail_kernel,
        out_shape=jax.ShapeDtypeStruct((PARTS, SHARE, LANES), BF16),
        compiler_params=compiler_params(),
        cost_estimate=pl.CostEstimate(
            flops=4 * SHARE * 1024 * CHAN, bytes_accessed=1500000, transcendentals=SHARE * 2000
        ),
        name="tail",
    )(parts, proj, classify, classify_t, onehot)


def gradient_kernel(parity_ref, own_ref, other_ref, features_ref, out_ref, flat_ref, turned_ref, acc_ref):
    own = parity_ref[0]
    for half, grads in enumerate((own_ref, other_ref)):
        flat_ref[...] = grads[...].astype(F32)
        for block in range(UNITS):
            turned = jnp.transpose(flat_ref[block * UNIT : block * UNIT + LANES, :])
            turned_ref[block, :, half * LANES : (half + 1) * LANES] = turned[: 3 * OUTS, :].astype(BF16)
    acc_ref[...] = jnp.zeros(acc_ref.shape, F32)
    gap = jnp.zeros((LANES - UNIT, CHAN), BF16)
    for j in range(GRID_J):
        for q in range(GRID_Q):
            taps = block_taps(j, q)
            grads = jnp.concatenate(
                [turned_ref[block, branch * OUTS : (branch + 1) * OUTS, :] for _, branch, block in taps],
                axis=0,
            )
            pixels = jnp.concatenate(
                [features_ref[j, own, q], gap, features_ref[j, 1 - own, q], gap], axis=0
            )
            product = jnp.dot(grads, pixels, preferred_element_type=F32)
            for place, (tap, _, _) in enumerate(taps):
                for lanes in range(2):
                    acc_ref[lanes, tap * OUTS : (tap + 1) * OUTS, :] += product[
                        place * OUTS : (place + 1) * OUTS, lanes * LANES : (lanes + 1) * LANES
                    ]
    for slot in range(OUTS):
        for lanes in range(2):
            start = slot % 4 * CHAN + lanes * LANES
            out_ref[slot // 4, :, start : start + LANES] = acc_ref[
                lanes, pl.ds(slot, 32, stride=OUTS), :
            ].astype(BF16)


def gradient(parity, own, other, features):
    whole = pl.BlockSpec(memory_space=pltpu.VMEM)
    return pl.pallas_call(
        gradient_kernel,
        in_specs=[pl.BlockSpec(memory_space=pltpu.SMEM), whole, whole, whole],
        out_specs=whole,
        out_shape=jax.ShapeDtypeStruct((8, 32, 4 * CHAN), BF16),
        scratch_shapes=[
            pltpu.VMEM((PADDED, LANES), F32),
            pltpu.VMEM((UNITS, 3 * OUTS, 2 * LANES), BF16),
            pltpu.VMEM((2, 32 * OUTS, LANES), F32),
        ],
        compiler_params=compiler_params(),
        cost_estimate=pl.CostEstimate(
            flops=4 * HALF * CHAN * TAPS * OUTS, bytes_accessed=4000000, transcendentals=0
        ),
        name="gradient_taps",
    )(parity, own, other, features)


def unshuffle_kernel(parts_ref, out_ref, rows_ref):
    for slot in range(OUTS):
        for lanes in range(2):
            start = slot % 4 * CHAN + lanes * LANES
            rows_ref[lanes, pl.ds(slot, 32, stride=OUTS), :] = parts_ref[
                slot // 4, :, start : start + LANES
            ].astype(F32)
    for lanes in range(2):
        out_ref[:, lanes * LANES : (lanes + 1) * LANES] = rows_ref[lanes, : TAPS * OUTS, :].astype(BF16)


def unshuffle(parts):
    return pl.pallas_call(
        unshuffle_kernel,
        out_shape=jax.ShapeDtypeStruct((TAPS * OUTS, CHAN), BF16),
        scratch_shapes=[pltpu.VMEM((2, 32 * OUTS, LANES), F32)],
        compiler_params=compiler_params(),
        cost_estimate=pl.CostEstimate(flops=0, bytes_accessed=1000000, transcendentals=0),
        name="unshuffle",
    )(parts)


def shards(features, weights, proj, classify, labels):
    row = lax.axis_index("row")
    core = lax.axis_index("core")
    part = lax.axis_index("yhi") * ROWS + row
    swap = [(0, 1), (1, 0)]

    sent = prepare(features.reshape(432, CHAN))
    gathered = lax.all_to_all(sent, "row", 0, 0).reshape(GRID_J, 2, GRID_Q, UNIT, CHAN)

    by_tap = weights.transpose(1, 2, 0, 3).reshape(TAPS, 32, CHAN)
    mine = lax.dynamic_slice_in_dim(by_tap, 4 * row, 4, 1).reshape(TAPS, 4 * CHAN)
    mine = jnp.pad(mine, ((0, 32 - TAPS), (0, 0)))
    kernels = unshuffle(lax.all_to_all(jnp.broadcast_to(mine[None], (8, 32, 4 * CHAN)), "sample", 0, 0))

    marks = labels.reshape(6, GRID_Q, 12).transpose(1, 0, 2).reshape(1, 432)
    marks = lax.all_to_all(jnp.broadcast_to(marks, (ROWS, 432)), "row", 0, 0).reshape(GRID_J, 2, 432)
    marks = lax.dynamic_index_in_dim(marks, core, 1, keepdims=False).reshape(HALF)
    marks = jnp.pad(marks, (0, PADDED - HALF)).reshape(PARTS, SHARE)
    marks = lax.dynamic_index_in_dim(marks, part, 0, keepdims=False)
    onehot = (marks[:, None] == jnp.arange(LANES, dtype=jnp.int32)[None, :]).astype(F32)

    mixing = proj.reshape(3, 8, ROWS, 4, CHAN).transpose(2, 0, 1, 3, 4).reshape(ROWS, 3 * OUTS, CHAN)
    mixing = jnp.pad(mixing, ((0, 0), (0, LANES - 3 * OUTS), (0, 0))).reshape(ROWS * LANES, CHAN)
    heads = jnp.pad(classify, ((0, 0), (0, LANES - 3)))
    heads_t = jnp.pad(classify.T, ((0, LANES - 3), (0, 0)))

    parity = core.astype(jnp.int32).reshape(1)
    other = forward(1 - parity, gathered, kernels)
    received = lax.ppermute(other, "core", swap)
    own = forward(parity, gathered, kernels)
    pair = (own.astype(F32) + received.astype(F32)).astype(BF16).reshape(PARTS, SHARE, LANES)
    parts = lax.all_to_all(pair, ("yhi", "row"), 0, 0)
    grads = tail(parts, mixing, heads, heads_t, onehot)
    grads_own = lax.all_to_all(grads, ("yhi", "row"), 0, 0).reshape(PADDED, LANES)
    grads_other = lax.ppermute(grads_own, "core", swap)
    partial = gradient(parity, grads_own, grads_other, gathered)
    over_samples = lax.all_to_all(partial, "sample", 0, 0)
    summed = jnp.sum(over_samples.astype(F32), axis=0).astype(BF16)
    final = lax.all_to_all(jnp.broadcast_to(summed[None], (ROWS, 32, 4 * CHAN)), "row", 0, 0)
    return unshuffle(final).reshape(3, 9, 32, CHAN).transpose(2, 0, 1, 3)


def solution(mesh):
    split = Mesh(mesh.devices.reshape(8, 4, 2, 8), ("row", "yhi", "core", "sample"))
    in_specs = (
        P("sample", "row", None, ("yhi", "core")),
        P("sample", None, None, ("yhi", "core")),
        P(),
        P(),
        P("sample", "row", None),
    )
    out_specs = P("sample", None, None, ("yhi", "core"))
    return jax.shard_map(shards, mesh=split, in_specs=in_specs, out_specs=out_specs, check_vma=False)
```

time: 335 us -> 159 us (0.47); the launches traced: 331 us -> 159 us
  waiting for transfers between devices: 241 us -> 53.5 us
  blocking collectives: 0 us -> 51.4 us
  matrix products: 35.4 us -> 0 us
  starting transfers between devices: 20.2 us -> 34.7 us
  between operations: 14 us -> 0.24 us
  Pallas kernels: 0 us -> 12.1 us
  local copies, waits for them, and re-layouts: 17.1 us -> 5.4 us
    psum x2 -> x0, waiting for transfers between devices: 159 us -> none  [the longest x1 81.9 us: shards(): row_summed = lax.psum(sample_summed, 'row').astype(jnp.float32)]
    reduce_scatter x1 -> x0, waiting for transfers between devices: 52.4 us -> none  [shards(): lax.psum_scatter(jnp.stack(grad_blocks, axis=1).reshape(weights.shape[0]...]
    all_to_all x0 -> x4, waiting for transfers between devices: none -> 52.1 us  [the longest x1 21.7 us: shards(): lax.all_to_all(sent, 'row', 0, 0).reshape(GRID_J, 2, GRID_Q, UNIT, CHAN)]
    all_to_all x0 -> x3, blocking collectives: none -> 51.4 us  [the longest x1 20.4 us: shards(): over_samples = lax.all_to_all(partial, 'sample', 0, 0)]
    dot_general x57 -> x0, matrix products: 35.4 us -> none  [the longest x27 26.2 us: shards(): lax.dot_general(grad_pre[:, branch, :], pick_tap(branch, tap_index), (((0...]
    all_to_all x0 -> x4, starting transfers between devices: none -> 26.4 us  [the longest x1 10.9 us: shards(): lax.all_to_all(jnp.broadcast_to(mine[None], (8, 32, 4 * CHAN)), 'sample',...]
    all_gather x1 -> x0, waiting for transfers between devices: 25.2 us -> none  [shards(): portion = lax.all_gather(weights, 'sample', axis=0, tiled=True)]
    pallas_call x0 -> x7, Pallas kernels: none -> 12.1 us  [the longest x2 4.55 us: forward(): pl.pallas_call(forward_kernel, grid_spec=pltpu.PrefetchScalarGridSpec(num...]
  transfers between devices with their start and end apart: 10 -> 6, of which waited for: 5 -> 5; matrix products, arithmetic and copies ran while one was open for 3% -> 3% of each run, Pallas kernels for 0% -> 3%
where the time goes in v1:
time: 159 us
  waiting for transfers between devices  53.5 us (34%)
  blocking collectives  51.4 us (32%)
  starting transfers between devices  34.7 us (22%)
  Pallas kernels  12.1 us (8%)
  local copies, waits for them, and re-layouts  5.4 us (3%)
    all_to_all x1, waiting for transfers between devices, shards(): lax.all_to_all(sent, 'row', 0, 0).reshape(GRID_J, 2, GRID_Q, UNIT, CHAN)  21.7 us
    all_to_all x1, blocking collectives, shards(): over_samples = lax.all_to_all(partial, 'sample', 0, 0)  20.4 us
    all_to_all x1, blocking collectives, shards(): lax.all_to_all(grads, ('yhi', 'row'), 0, 0).reshape(PADDED, LANES)  19.5 us
    all_to_all x1, waiting for transfers between devices, shards(): lax.all_to_all(jnp.broadcast_to(mine[None], (8, 32, 4 * CHAN)), 'sample',...  16.6 us
    all_to_all x1, blocking collectives, shards(): lax.all_to_all(jnp.broadcast_to(summed[None], (ROWS, 32, 4 * CHAN)), 'row...  11.6 us
    all_to_all x1, waiting for transfers between devices, shards(): parts = lax.all_to_all(pair, ('yhi', 'row'), 0, 0)  11.6 us
    all_to_all x1, starting transfers between devices, shards(): lax.all_to_all(jnp.broadcast_to(mine[None], (8, 32, 4 * CHAN)), 'sample',...  10.9 us
    all_to_all x1, starting transfers between devices, shards(): parts = lax.all_to_all(pair, ('yhi', 'row'), 0, 0)  7.19 us
  transfers between devices with their start and end apart: 6, of which 5 were waited for; matrix products, arithmetic and copies ran while one was open for 3% of the time, Pallas kernels for 3%

profile of v1, /device:TPU:1, one launch (start us, length us, event | category | flops | bytes accessed | tf_op | source)
XLA Modules:
  0.0 158.5 jit_solution(5380341321965614519)
XLA Ops:
  0.0 0.0 copy-start
  0.0 0.0 copy-start.1
  0.0 1.0 copy-done
  1.1 0.9 broadcast_in_dim.8
  2.0 10.9 %all-to-all-start.1 = ((bf16[8,32,1024]{2,1,0:T(8,128)(2,1)}), bf16[8,32,1024]{2,1,0:T(8,128)(2,1)S(1)}, u32[]{:S(2)}, u32[]{:S(2)}) async-start(bf16[8,32,1024]{2,1,0:T(8,128)(2,1)} %broadcast_in_dim.8), calls=%async_computation.1 | async-start | bytes 1048576 | tf_op jit(solution)/shard_map/all_to_all | solution.py:256
  12.9 0.0 copy-done.1
  12.9 1.4 prepare_features.1
  14.3 16.6 %all-to-all-done.1.parts_ref = bf16[8,32,1024]{2,1,0:T(8,128)(2,1)S(1)} async-done(((bf16[8,32,1024]{2,1,0:T(8,128)(2,1)}), bf16[8,32,1024]{2,1,0:T(8,128)(2,1)S(1)}, u32[]{:S(2)}, u32[]{:S(2)}) %all-to-all-start.1) | async-done | bytes 524320 | tf_op jit(solution)/shard_map/all_to_all | solution.py:256
  30.8 5.0 %all-to-all-start = ((bf16[8,6,72,256]{3,2,1,0:T(8,128)(2,1)}), bf16[8,6,72,256]{3,2,1,0:T(8,128)(2,1)S(1)}, u32[]{:S(2)}, u32[]{:S(2)}) async-start(bf16[8,6,72,256]{3,2,1,0:T(8,128)(2,1)} %prepare_features.1), calls=%async_computation | async-start | bytes 3538944 | tf_op jit(solution)/shard_map/all_to_all | solution.py:251
  35.9 0.0 copy-start.4
  35.9 0.9 unshuffle.2.weights_ref
  36.8 21.7 %all-to-all-done = bf16[8,6,72,256]{3,2,1,0:T(8,128)(2,1)S(1)} async-done(((bf16[8,6,72,256]{3,2,1,0:T(8,128)(2,1)}), bf16[8,6,72,256]{3,2,1,0:T(8,128)(2,1)S(1)}, u32[]{:S(2)}, u32[]{:S(2)}) %all-to-all-start) | async-done | bytes 1769504 | tf_op jit(solution)/shard_map/all_to_all | solution.py:251
  58.5 2.7 %forward_taps.3 = bf16[1792,128]{1,0:T(8,128)(2,1)} custom-call(s32[1]{0:T(128)S(6)} %sub.3.parity_ref, bf16[4,2,6,72,256]{4,3,2,1,0:T(8,128)(2,1)S(1)} %bitcast.24, bf16[864,256]{1,0:T(8,128)(2,1)S(1)} %unshuffle.2.weights_ref), custom_call_target="tpu_custom_call" | custom-call | flops 764411904 | bytes 2000000 | tf_op jit(solution)/shard_map/forward_taps/pallas_call | solution.py:95
  61.2 2.7 %collective-permute-start = (bf16[1792,128]{1,0:T(8,128)(2,1)}, bf16[1792,128]{1,0:T(8,128)(2,1)S(1)}, u32[]{:S(2)}, u32[]{:S(2)}) collective-permute-start(bf16[1792,128]{1,0:T(8,128)(2,1)} %forward_taps.3), channel_id=1, source_target_pairs={{0,8},{8,0},{1,9},{9,1},{2,10},{10,2},{3,11},{11,3},{4,12},{12,4},... | collective-permute-start | bytes 1376264 | tf_op jit(solution)/shard_map/ppermute | solution.py:272
  63.9 0.0 copy-done.4
  63.9 0.1 reshape.69
  64.0 0.1 broadcast_in_dim.9
  64.1 0.6 broadcast_in_dim.10
  64.7 3.4 %all-to-all-start.3 = ((s32[8,1,432]{2,1,0:T(1,128)}), s32[8,1,432]{2,1,0:T(1,128)S(1)}, u32[]{:S(2)}, u32[]{:S(2)}) async-start(s32[8,1,432]{2,1,0:T(1,128)} %broadcast_in_dim.10), calls=%async_computation.3 | async-start | bytes 32768 | tf_op jit(solution)/shard_map/all_to_all | solution.py:259
  68.1 1.9 %forward_taps.2 = bf16[1792,128]{1,0:T(8,128)(2,1)S(1)} custom-call(s32[1]{0:T(128)} %bitcast.parity_ref, bf16[4,2,6,72,256]{4,3,2,1,0:T(8,128)(2,1)S(1)} %bitcast.25, bf16[864,256]{1,0:T(8,128)(2,1)S(1)} %unshuffle.2.weights_ref), custom_call_target="tpu_custom_call" | custom-call | flops 764411904 | bytes 2000000 | tf_op jit(solution)/shard_map/forward_taps/pallas_call | solution.py:95
  70.0 0.0 copy-start.2
  70.0 0.0 collective-permute-done
  70.0 0.9 add_convert_fusion
  70.9 2.2 %all-to-all-done.3 = s32[8,1,432]{2,1,0:T(1,128)S(1)} async-done(((s32[8,1,432]{2,1,0:T(1,128)}), s32[8,1,432]{2,1,0:T(1,128)S(1)}, u32[]{:S(2)}, u32[]{:S(2)}) %all-to-all-start.3) | async-done | bytes 13856 | tf_op jit(solution)/shard_map/all_to_all | solution.py:259
  73.2 7.2 %all-to-all-start.2 = ((bf16[32,56,128]{2,1,0:T(8,128)(2,1)}), bf16[32,56,128]{2,1,0:T(8,128)(2,1)S(1)}, u32[]{:S(2)}, u32[]{:S(2)}) async-start(bf16[32,56,128]{2,1,0:T(8,128)(2,1)} %bitcast.5), calls=%async_computation.2 | async-start | bytes 917504 | tf_op jit(solution)/shard_map/all_to_all | solution.py:275
  80.4 0.0 copy-start.3
  80.4 0.0 copy-done.2
  80.4 0.1 reshape.66
  80.5 0.2 copy.8
  80.7 0.8 reshape.67
  81.5 1.0 pad.21
  82.6 0.0 copy-done.3
  82.6 0.1 copy.9
  82.9 0.1 reshape.71
  83.0 0.1 reshape.72
  83.1 0.1 fusion.onehot_ref
  83.2 11.6 %all-to-all-done.2.parts_ref = bf16[32,56,128]{2,1,0:T(8,128)(2,1)S(1)} async-done(((bf16[32,56,128]{2,1,0:T(8,128)(2,1)}), bf16[32,56,128]{2,1,0:T(8,128)(2,1)S(1)}, u32[]{:S(2)}, u32[]{:S(2)}) %all-to-all-start.2) | async-done | bytes 458784 | tf_op jit(solution)/shard_map/all_to_all | solution.py:275
  94.7 0.9 tail.1
  95.6 19.5 %all_to_all.36 = bf16[32,56,128]{2,1,0:T(8,128)(2,1)S(1)} all-to-all(bf16[32,56,128]{2,1,0:T(8,128)(2,1)S(1)} %tail.1), channel_id=1, replica_groups=mesh['row'=8,'yhi'=4,'core'=2,'sample'=8] {'yhi','row'}, dimensions={0} | all-to-all | bytes 917504 | tf_op jit(solution)/shard_map/all_to_all | solution.py:277
  115.1 5.6 %collective-permute-start.1 = (bf16[1792,128]{1,0:T(8,128)(2,1)S(1)}, bf16[1792,128]{1,0:T(8,128)(2,1)S(1)}, u32[]{:S(2)}, u32[]{:S(2)}) collective-permute-start(bf16[1792,128]{1,0:T(8,128)(2,1)S(1)} %bitcast.27), channel_id=1, source_target_pairs={{0,8},{8,0},{1,9},{9,1},{2,10},{10,2},{3,11},{11,3},{4,12},{12,4},... | collective-permute-start | bytes 1376264 | tf_op jit(solution)/shard_map/ppermute | solution.py:278
  120.7 1.4 collective-permute-done.1.other_ref
  122.1 2.6 %gradient_taps.1 = bf16[8,32,1024]{2,1,0:T(8,128)(2,1)S(1)} custom-call(s32[1]{0:T(128)} %bitcast.parity_ref, bf16[1792,128]{1,0:T(8,128)(2,1)S(1)} %bitcast.28, bf16[1792,128]{1,0:T(8,128)(2,1)S(1)} %collective-permute-done.1.other_ref, bf16[4,2,6,72,256]{4,3,2,1,0:T(8,128)(2,1)S(1)} %bitcast.26), custom_call_target="tpu_custom_call" | custom-call | flops 1528823808 | bytes 4000000 | tf_op jit(solution)/shard_map/gradient_taps/pallas_call | solution.py:204
  124.7 20.4 %all_to_all.37 = bf16[8,32,1024]{2,1,0:T(8,128)(2,1)S(1)} all-to-all(bf16[8,32,1024]{2,1,0:T(8,128)(2,1)S(1)} %gradient_taps.1), channel_id=1, replica_groups=mesh['row'=8,'yhi'=4,'core'=2,'sample'=8] {'sample'}, dimensions={0} | all-to-all | bytes 1048576 | tf_op jit(solution)/shard_map/all_to_all | solution.py:280
  145.1 0.1 reduce_sum.12
  145.2 0.1 broadcast_in_dim.11
  145.2 11.6 %all_to_all.38.parts_ref = bf16[8,32,1024]{2,1,0:T(8,128)(2,1)S(1)} all-to-all(bf16[8,32,1024]{2,1,0:T(8,128)(2,1)S(1)} %broadcast_in_dim.11), channel_id=1, replica_groups=mesh['row'=8,'yhi'=4,'core'=2,'sample'=8] {'row'}, dimensions={0} | all-to-all | bytes 1048576 | tf_op jit(solution)/shard_map/all_to_all | solution.py:282
  156.8 1.7 %unshuffle.3 = bf16[864,256]{1,0:T(8,128)(2,1)} custom-call(bf16[8,32,1024]{2,1,0:T(8,128)(2,1)S(1)} %all_to_all.38.parts_ref), custom_call_target="tpu_custom_call" | custom-call | bytes 1000000 | tf_op jit(solution)/shard_map/unshuffle/pallas_call | solution.py:234
  (13 shorter events, 0.2 us)
Async XLA Ops:
  0.0 1.0 copy-start
  0.0 12.9 %copy-start.1 = (bf16[1,6,72,256]{3,2,1,0:T(8,128)(2,1)S(1)}, bf16[1,6,72,256]{3,2,1,0:T(8,128)(2,1)}, u32[]{:S(2)}) copy-start(bf16[1,6,72,256]{3,2,1,0:T(8,128)(2,1)} %param.5) | copy-start | bytes 663556
  2.0 28.8 %all-to-all-start.1 = ((bf16[8,32,1024]{2,1,0:T(8,128)(2,1)}), bf16[8,32,1024]{2,1,0:T(8,128)(2,1)S(1)}, u32[]{:S(2)}, u32[]{:S(2)}) async-start(bf16[8,32,1024]{2,1,0:T(8,128)(2,1)} %broadcast_in_dim.8), calls=%async_computation.1 | async-start | bytes 1048576 | tf_op jit(solution)/shard_map/all_to_all | solution.py:256
  30.8 27.7 %all-to-all-start = ((bf16[8,6,72,256]{3,2,1,0:T(8,128)(2,1)}), bf16[8,6,72,256]{3,2,1,0:T(8,128)(2,1)S(1)}, u32[]{:S(2)}, u32[]{:S(2)}) async-start(bf16[8,6,72,256]{3,2,1,0:T(8,128)(2,1)} %prepare_features.1), calls=%async_computation | async-start | bytes 3538944 | tf_op jit(solution)/shard_map/all_to_all | solution.py:251
  35.9 28.1 %copy-start.4 = (s32[1,6,72]{2,0,1:T(1,128)S(1)}, s32[1,6,72]{2,0,1:T(1,128)}, u32[]{:S(2)}) copy-start(s32[1,6,72]{2,0,1:T(1,128)} %param.9) | copy-start | bytes 5188
  61.2 8.9 %collective-permute-start = (bf16[1792,128]{1,0:T(8,128)(2,1)}, bf16[1792,128]{1,0:T(8,128)(2,1)S(1)}, u32[]{:S(2)}, u32[]{:S(2)}) collective-permute-start(bf16[1792,128]{1,0:T(8,128)(2,1)} %forward_taps.3), channel_id=1, source_target_pairs={{0,8},{8,0},{1,9},{9,1},{2,10},{10,2},{3,11},{11,3},{4,12},{12,4},... | collective-permute-start | bytes 1376264 | tf_op jit(solution)/shard_map/ppermute | solution.py:272
  64.7 8.4 %all-to-all-start.3 = ((s32[8,1,432]{2,1,0:T(1,128)}), s32[8,1,432]{2,1,0:T(1,128)S(1)}, u32[]{:S(2)}, u32[]{:S(2)}) async-start(s32[8,1,432]{2,1,0:T(1,128)} %broadcast_in_dim.10), calls=%async_computation.3 | async-start | bytes 32768 | tf_op jit(solution)/shard_map/all_to_all | solution.py:259
  70.0 10.4 %copy-start.2 = (bf16[768,256]{1,0:T(8,128)(2,1)S(1)}, bf16[768,256]{1,0:T(8,128)(2,1)}, u32[]{:S(2)}) copy-start(bf16[768,256]{1,0:T(8,128)(2,1)} %param.7) | copy-start | bytes 1179652
  73.2 21.6 %all-to-all-start.2 = ((bf16[32,56,128]{2,1,0:T(8,128)(2,1)}), bf16[32,56,128]{2,1,0:T(8,128)(2,1)S(1)}, u32[]{:S(2)}, u32[]{:S(2)}) async-start(bf16[32,56,128]{2,1,0:T(8,128)(2,1)} %bitcast.5), calls=%async_computation.2 | async-start | bytes 917504 | tf_op jit(solution)/shard_map/all_to_all | solution.py:275
  80.4 2.2 %copy-start.3 = (bf16[256,3]{0,1:T(4,128)(2,1)S(1)}, bf16[256,3]{0,1:T(4,128)(2,1)}, u32[]{:S(2)}) copy-start(bf16[256,3]{0,1:T(4,128)(2,1)} %param.8) | copy-start | bytes 4612
  115.1 7.0 %collective-permute-start.1 = (bf16[1792,128]{1,0:T(8,128)(2,1)S(1)}, bf16[1792,128]{1,0:T(8,128)(2,1)S(1)}, u32[]{:S(2)}, u32[]{:S(2)}) collective-permute-start(bf16[1792,128]{1,0:T(8,128)(2,1)S(1)} %bitcast.27), channel_id=1, source_target_pairs={{0,8},{8,0},{1,9},{9,1},{2,10},{10,2},{3,11},{11,3},{4,12},{12,4},... | collective-permute-start | bytes 1376264 | tf_op jit(solution)/shard_map/ppermute | solution.py:278

commit v2 on v1

v2 whole, which is shorter than its diff:
```python
import jax
import jax.numpy as jnp
from jax import lax
from jax.experimental import pallas as pl
from jax.experimental.pallas import tpu as pltpu
from jax.sharding import Mesh, PartitionSpec as P

BF16 = jnp.bfloat16
F32 = jnp.float32

ROWS = 8
GRID_J = 4
GRID_Q = 6
UNIT = 72
UNITS = GRID_J * GRID_Q
HALF = UNITS * UNIT
SHARD = 432
SENT = 440
PARTS = 32
USED = 27
SHARE = 48
BLOCK = 216
LANES = 128
CHAN = 256
OUTS = 32
TAPS = 27
ROW_AXES = ("row",)
VMEM_LIMIT = 48 * 1024 * 1024


def block_taps(j, q):
    found = []
    for branch in range(3):
        rate = branch + 1
        for tap_row in range(3):
            out_j = j - rate * (tap_row - 1)
            if not 0 <= out_j < GRID_J:
                continue
            for tap_col in range(3):
                out_q = q - rate * (tap_col - 1)
                if not 0 <= out_q < GRID_Q:
                    continue
                found.append((9 * branch + 3 * tap_row + tap_col, branch, out_j * GRID_Q + out_q))
    return found


def compiler_params():
    return pltpu.CompilerParams(vmem_limit_bytes=VMEM_LIMIT)


def prepare_kernel(features_ref, marks_ref, out_ref, rows_ref, units_ref):
    rows_ref[...] = features_ref[...].astype(F32)
    for row in range(6):
        for q in range(GRID_Q):
            units_ref[q * UNIT + row * 12 : q * UNIT + row * 12 + 12, :] = rows_ref[
                row * 72 + q * 12 : row * 72 + q * 12 + 12, :
            ]
    units_ref[SHARD:, :] = marks_ref[...]
    block = units_ref[...].astype(BF16)
    for device in range(ROWS):
        out_ref[device] = block


def prepare(features, marks):
    return pl.pallas_call(
        prepare_kernel,
        out_shape=jax.ShapeDtypeStruct((ROWS, SENT, CHAN), BF16),
        scratch_shapes=[pltpu.VMEM((SHARD, CHAN), F32), pltpu.VMEM((SENT, CHAN), F32)],
        compiler_params=compiler_params(),
        cost_estimate=pl.CostEstimate(flops=0, bytes_accessed=2 * 9 * SHARD * CHAN, transcendentals=0),
        name="prepare_features",
    )(features, marks)


def unit_rows(q):
    return slice(q * UNIT, (q + 1) * UNIT)


def forward_kernel(parity_ref, features_ref, weights_ref, out_ref, acc_ref, flat_ref):
    del parity_ref
    acc_ref[...] = jnp.zeros(acc_ref.shape, F32)
    for j in range(GRID_J):
        for q in range(GRID_Q):
            taps = block_taps(j, q)
            kernels = jnp.concatenate(
                [weights_ref[tap * OUTS : (tap + 1) * OUTS, :] for tap, _, _ in taps], axis=0
            )
            product = lax.dot_general(
                kernels,
                features_ref[j, 0, unit_rows(q), :],
                (((1,), (1,)), ((), ())),
                preferred_element_type=F32,
            )
            for place, (_, branch, block) in enumerate(taps):
                lane = block % 4 * OUTS
                acc_ref[block // 4, branch, lane : lane + OUTS, :UNIT] += product[
                    place * OUTS : (place + 1) * OUTS, :
                ]
    for group in range(UNITS // 4):
        for branch in range(3):
            flat_ref[branch, group * UNIT : (group + 1) * UNIT, :] = jnp.transpose(
                acc_ref[group, branch]
            )[:UNIT, :]
    for part in range(USED):
        for branch in range(3):
            out_ref[part, branch * 16 : (branch + 1) * 16, :] = flat_ref[
                branch, part * 16 : (part + 1) * 16, :
            ].astype(BF16)
    out_ref[USED:] = jnp.zeros((PARTS - USED, SHARE, LANES), BF16)


def forward(parity, features, weights):
    return pl.pallas_call(
        forward_kernel,
        grid_spec=pltpu.PrefetchScalarGridSpec(
            num_scalar_prefetch=1,
            grid=(1,),
            in_specs=[
                pl.BlockSpec((GRID_J, 1, SENT, CHAN), lambda i, p: (0, p[0], 0, 0)),
                pl.BlockSpec((TAPS * OUTS, CHAN), lambda i, p: (0, 0)),
            ],
            out_specs=pl.BlockSpec((PARTS, SHARE, LANES), lambda i, p: (0, 0, 0)),
            scratch_shapes=[
                pltpu.VMEM((UNITS // 4, 3, LANES, LANES), F32),
                pltpu.VMEM((3, HALF // 4, LANES), F32),
            ],
        ),
        out_shape=jax.ShapeDtypeStruct((PARTS, SHARE, LANES), BF16),
        compiler_params=compiler_params(),
        cost_estimate=pl.CostEstimate(
            flops=2 * HALF * CHAN * TAPS * OUTS, bytes_accessed=2000000, transcendentals=0
        ),
        name="forward_taps",
    )(parity, features, weights)


def sigmoid(values):
    return 1.0 / (1.0 + jnp.exp(-values))


def swish_grad(values, gate_value):
    return gate_value * (1.0 + values * (1.0 - gate_value))


def tail_kernel(parts_ref, proj_ref, classify_ref, classify_t_ref, onehot_ref, out_ref, act_ref, packed_ref):
    pieces = [(row, branch, place) for row in range(ROWS) for branch in range(3) for place in range(4)]

    def packed_at(branch, place):
        return slice(branch * 16, (branch + 1) * 16), slice(place * OUTS, (place + 1) * OUTS)

    def flat_at(row, branch, place):
        start = (row * 3 + branch) * OUTS
        return slice(place * 16, (place + 1) * 16), slice(start, start + OUTS)

    preact, gate = [], []
    for row in range(ROWS):
        total = parts_ref[row].astype(F32)
        for part in range(1, PARTS // ROWS):
            total = total + parts_ref[part * ROWS + row].astype(F32)
        preact.append(total)
        gate.append(sigmoid(total))
        packed_ref[row] = total * gate[row]
    for row, branch, place in pieces:
        at, lanes = packed_at(branch, place)
        act_ref[flat_at(row, branch, place)] = packed_ref[row, at, lanes]
    mixed_pre = jnp.dot(act_ref[...].astype(BF16), proj_ref[...], preferred_element_type=F32)
    mixed_gate = sigmoid(mixed_pre)
    hidden = (mixed_pre * mixed_gate).astype(BF16)
    logits = jnp.dot(hidden, classify_ref[...], preferred_element_type=F32)
    lane = lax.broadcasted_iota(jnp.int32, logits.shape, 1)
    exp_logits = jnp.where(lane < 3, jnp.exp(logits), 0.0)
    probabilities = exp_logits / jnp.sum(exp_logits, axis=1, keepdims=True)
    dlogits = (probabilities - onehot_ref[...]).astype(BF16)
    grad_hidden = jnp.dot(dlogits, classify_t_ref[...], preferred_element_type=F32)
    grad_mixed = (grad_hidden * swish_grad(mixed_pre, mixed_gate)).astype(BF16)
    act_ref[...] = lax.dot_general(
        grad_mixed, proj_ref[...], (((1,), (1,)), ((), ())), preferred_element_type=F32
    )
    for row, branch, place in pieces:
        at, lanes = packed_at(branch, place)
        packed_ref[row, at, lanes] = act_ref[flat_at(row, branch, place)]
    for row in range(ROWS):
        block = (packed_ref[row] * swish_grad(preact[row], gate[row])).astype(BF16)
        for part in range(PARTS // ROWS):
            out_ref[part * ROWS + row] = block


def tail(parts, proj, classify, classify_t, onehot):
    return pl.pallas_call(
        tail_kernel,
        out_shape=jax.ShapeDtypeStruct((PARTS, SHARE, LANES), BF16),
        scratch_shapes=[
            pltpu.VMEM((64, ROWS * 3 * OUTS), F32),
            pltpu.VMEM((ROWS, SHARE, LANES), F32),
        ],
        compiler_params=compiler_params(),
        cost_estimate=pl.CostEstimate(
            flops=4 * 64 * 768 * CHAN, bytes_accessed=1500000, transcendentals=64 * 2000
        ),
        name="tail",
    )(parts, proj, classify, classify_t, onehot)


def gradient_kernel(
    parity_ref, own_ref, other_ref, features_ref, out_ref, flat_ref, turned_ref, acc_ref, rows_ref
):
    own = parity_ref[0]
    flat_ref[:, HALF // 4 :, :] = jnp.zeros((3, LANES - UNIT, LANES), F32)
    for half, grads in enumerate((own_ref, other_ref)):
        for part in range(USED):
            for branch in range(3):
                flat_ref[branch, part * 16 : (part + 1) * 16, :] = grads[
                    part, branch * 16 : (branch + 1) * 16, :
                ].astype(F32)
        for group in range(UNITS // 4):
            for branch in range(3):
                turned = jnp.transpose(flat_ref[branch, group * UNIT : group * UNIT + LANES, :]).astype(BF16)
                for place in range(4):
                    turned_ref[
                        group * 4 + place,
                        branch * OUTS : (branch + 1) * OUTS,
                        half * LANES : (half + 1) * LANES,
                    ] = turned[place * OUTS : (place + 1) * OUTS, :]
    acc_ref[...] = jnp.zeros(acc_ref.shape, F32)
    gap = jnp.zeros((LANES - UNIT, CHAN), BF16)
    for j in range(GRID_J):
        for q in range(GRID_Q):
            taps = block_taps(j, q)
            grads = jnp.concatenate(
                [turned_ref[block, branch * OUTS : (branch + 1) * OUTS, :] for _, branch, block in taps],
                axis=0,
            )
            pixels = jnp.concatenate(
                [features_ref[j, own, unit_rows(q), :], gap, features_ref[j, 1 - own, unit_rows(q), :], gap],
                axis=0,
            )
            product = jnp.dot(grads, pixels, preferred_element_type=F32)
            for place, (tap, _, _) in enumerate(taps):
                for lanes in range(2):
                    acc_ref[lanes, tap * OUTS : (tap + 1) * OUTS, :] += product[
                        place * OUTS : (place + 1) * OUTS, lanes * LANES : (lanes + 1) * LANES
                    ]
    for slot in range(OUTS):
        for lanes in range(2):
            rows_ref[pl.ds(slot // 4 * BLOCK + slot % 4 * 2 + lanes, TAPS, stride=8), :] = acc_ref[
                lanes, pl.ds(slot, TAPS, stride=OUTS), :
            ]
    for sample in range(8):
        out_ref[sample] = rows_ref[sample * BLOCK : (sample + 1) * BLOCK, :].astype(BF16)


def gradient(parity, own, other, features):
    whole = pl.BlockSpec(memory_space=pltpu.VMEM)
    return pl.pallas_call(
        gradient_kernel,
        in_specs=[pl.BlockSpec(memory_space=pltpu.SMEM), whole, whole, whole],
        out_specs=whole,
        out_shape=jax.ShapeDtypeStruct((8, BLOCK, LANES), BF16),
        scratch_shapes=[
            pltpu.VMEM((3, HALF // 4 + LANES - UNIT, LANES), F32),
            pltpu.VMEM((UNITS, 3 * OUTS, 2 * LANES), BF16),
            pltpu.VMEM((2, TAPS * OUTS, LANES), F32),
            pltpu.VMEM((8 * BLOCK, LANES), F32),
        ],
        compiler_params=compiler_params(),
        cost_estimate=pl.CostEstimate(
            flops=4 * HALF * CHAN * TAPS * OUTS, bytes_accessed=4000000, transcendentals=0
        ),
        name="gradient_taps",
    )(parity, own, other, features)


def unshuffle_kernel(parts_ref, out_ref, packed_ref, rows_ref):
    for block in range(8):
        packed_ref[block * BLOCK : (block + 1) * BLOCK, :] = parts_ref[block].astype(F32)
    for slot in range(OUTS):
        for lanes in range(2):
            rows_ref[lanes, pl.ds(slot, TAPS, stride=OUTS), :] = packed_ref[
                pl.ds(slot // 4 * BLOCK + slot % 4 * 2 + lanes, TAPS, stride=8), :
            ]
    for lanes in range(2):
        out_ref[:, lanes * LANES : (lanes + 1) * LANES] = rows_ref[lanes].astype(BF16)


def unshuffle(parts):
    return pl.pallas_call(
        unshuffle_kernel,
        out_shape=jax.ShapeDtypeStruct((TAPS * OUTS, CHAN), BF16),
        scratch_shapes=[
            pltpu.VMEM((8 * BLOCK, LANES), F32),
            pltpu.VMEM((2, TAPS * OUTS, LANES), F32),
        ],
        compiler_params=compiler_params(),
        cost_estimate=pl.CostEstimate(flops=0, bytes_accessed=1000000, transcendentals=0),
        name="unshuffle",
    )(parts)


def shards(features, weights, proj, classify, labels):
    row = lax.axis_index("row")
    core = lax.axis_index("core")
    part = lax.axis_index("yhi") * ROWS + row
    swap = [(0, 1), (1, 0)]

    marks = labels.reshape(6, GRID_Q, 12).transpose(1, 0, 2).reshape(SHARD).astype(F32)
    marks = jnp.pad(marks, (0, (SENT - SHARD) * CHAN - SHARD)).reshape(SENT - SHARD, CHAN)
    sent = prepare(features.reshape(SHARD, CHAN), marks)
    by_tap = weights.transpose(1, 2, 0, 3).reshape(TAPS, 32, CHAN)
    mine = lax.dynamic_slice_in_dim(by_tap, 4 * row, 4, 1).reshape(BLOCK, LANES)
    sent, mine = lax.optimization_barrier((sent, mine))
    gathered = lax.all_to_all(sent, "row", 0, 0).reshape(GRID_J, 2, SENT, CHAN)
    kernels = unshuffle(lax.all_gather(mine, "sample"))

    mixing = proj.reshape(3, 8, ROWS, 4, CHAN).transpose(2, 0, 1, 3, 4).reshape(ROWS * 3 * OUTS, CHAN)
    heads = jnp.pad(classify, ((0, 0), (0, LANES - 3)))
    heads_t = jnp.pad(classify.T, ((0, LANES - 3), (0, 0)))
    kernels, mixing, heads, heads_t = lax.optimization_barrier((kernels, mixing, heads, heads_t))

    parity = core.astype(jnp.int32).reshape(1)
    other = forward(1 - parity, gathered, kernels)
    received = lax.ppermute(other, "core", swap)
    own = forward(parity, gathered, kernels)
    pair = (own.astype(F32) + received.astype(F32)).astype(BF16)

    marks = lax.dynamic_index_in_dim(gathered[:, :, SHARD : SHARD + 2, :], core, 1, keepdims=False)
    marks = marks.reshape(GRID_J, 2 * CHAN)[:, :SHARD].reshape(UNITS // 4, 4, UNIT)
    marks = marks.transpose(1, 0, 2).reshape(4, HALF // 4)
    marks = lax.dynamic_slice_in_dim(jnp.pad(marks, ((0, 0), (0, (PARTS - USED) * 16))), part * 16, 16, 1)
    onehot = (marks.reshape(64, 1) == jnp.arange(LANES, dtype=BF16)[None, :]).astype(F32)
    pair, onehot = lax.optimization_barrier((pair, onehot))

    parts = lax.all_to_all(pair, ("yhi", "row"), 0, 0)
    grads = tail(parts, mixing, heads, heads_t, onehot)
    grads_own = lax.all_to_all(grads, ("yhi", "row"), 0, 0)
    grads_other = lax.ppermute(grads_own, "core", swap)
    partial = gradient(parity, grads_own, grads_other, gathered)
    over_samples = lax.all_to_all(partial, "sample", 0, 0)
    summed = jnp.sum(over_samples.astype(F32), axis=0).astype(BF16)
    final = lax.all_to_all(jnp.broadcast_to(summed[None], (ROWS, BLOCK, LANES)), "row", 0, 0)
    return unshuffle(final).reshape(3, 9, 32, CHAN).transpose(2, 0, 1, 3)


def solution(mesh):
    split = Mesh(mesh.devices.reshape(8, 4, 2, 8), ("row", "yhi", "core", "sample"))
    in_specs = (
        P("sample", "row", None, ("yhi", "core")),
        P("sample", None, None, ("yhi", "core")),
        P(),
        P(),
        P("sample", "row", None),
    )
    out_specs = P("sample", None, None, ("yhi", "core"))
    return jax.shard_map(shards, mesh=split, in_specs=in_specs, out_specs=out_specs, check_vma=False)
```

time: 159 us -> 134 us (0.84)
  waiting for transfers between devices: 53.5 us -> 1.33 us
  blocking collectives: 51.4 us -> 96.4 us
  starting transfers between devices: 34.7 us -> 18.8 us
  local copies, waits for them, and re-layouts: 5.4 us -> 2.24 us
    all_to_all x4 -> x1, waiting for transfers between devices: 52.1 us -> 0.01 us  [shards(): gathered = lax.all_to_all(sent, 'row', 0, 0).reshape(GRID_J, 2, SENT, CHAN)]
    all_gather x0 -> x1, blocking collectives: none -> 27 us  [shards(): kernels = unshuffle(lax.all_gather(mine, 'sample'))]
    all_to_all x4 -> x1, starting transfers between devices: 26.4 us -> 5.99 us  [shards(): gathered = lax.all_to_all(sent, 'row', 0, 0).reshape(GRID_J, 2, SENT, CHAN)]
    all_to_all x2 -> x3, blocking collectives: 31.1 us -> 50.7 us  [the longest x1 23.6 us: shards(): parts = lax.all_to_all(pair, ('yhi', 'row'), 0, 0)]
    ppermute x1, starting transfers between devices: 2.73 us -> 7.38 us  [shards(): received = lax.ppermute(other, 'core', swap)]
    all_to_all x1, blocking collectives: 20.4 us -> 18.7 us  [shards(): over_samples = lax.all_to_all(partial, 'sample', 0, 0)]
  transfers between devices with their start and end apart: 6 -> 3, of which waited for: 5 -> 1; matrix products, arithmetic and copies ran while one was open for 3% -> 1% of each run, Pallas kernels for 3% -> 2%
where the time goes in v2:
time: 134 us; the launch traced here: 133 us
  blocking collectives  96.4 us (72%)
  starting transfers between devices  18.8 us (14%)
  Pallas kernels  12.3 us (9%)
  local copies, waits for them, and re-layouts  2.24 us (2%)
  other arithmetic  1.99 us (1%)
    all_gather x1, blocking collectives, shards(): kernels = unshuffle(lax.all_gather(mine, 'sample'))  27 us
    all_to_all x1, blocking collectives, shards(): parts = lax.all_to_all(pair, ('yhi', 'row'), 0, 0)  23.6 us
    all_to_all x1, blocking collectives, shards(): over_samples = lax.all_to_all(partial, 'sample', 0, 0)  18.7 us
    all_to_all x1, blocking collectives, shards(): grads_own = lax.all_to_all(grads, ('yhi', 'row'), 0, 0)  17 us
    all_to_all x1, blocking collectives, shards(): lax.all_to_all(jnp.broadcast_to(summed[None], (ROWS, BLOCK, LANES)), 'row...  10.1 us
    ppermute x1, starting transfers between devices, shards(): received = lax.ppermute(other, 'core', swap)  7.38 us
    all_to_all x1, starting transfers between devices, shards(): gathered = lax.all_to_all(sent, 'row', 0, 0).reshape(GRID_J, 2, SENT, CHAN)  5.99 us
    ppermute x1, starting transfers between devices, shards(): grads_other = lax.ppermute(grads_own, 'core', swap)  5.38 us
  transfers between devices with their start and end apart: 3, of which 1 were waited for; matrix products, arithmetic and copies ran while one was open for 1% of the time, Pallas kernels for 2%

profile of v2, /device:TPU:1, one launch (start us, length us, event | category | flops | bytes accessed | tf_op | source)
XLA Modules:
  0.0 133.2 jit_solution(6840200278946308939)
XLA Ops:
  0.0 0.0 copy-start
  0.0 0.8 convert_reduce_fusion
  0.8 0.1 convert_element_type.35
  0.8 0.1 convert_element_type.37
  1.0 0.1 copy-done
  1.1 0.0 copy-start.1
  1.1 0.9 copy-done.1
  2.0 1.4 %prepare_features.1 = bf16[8,440,256]{2,1,0:T(8,128)(2,1)} custom-call(bf16[432,256]{1,0:T(8,128)(2,1)S(1)} %bitcast.29, f32[8,256]{1,0:T(8,128)S(1)} %reshape.46.marks_ref), custom_call_target="tpu_custom_call" | custom-call | bytes 1990656 | tf_op jit(solution)/shard_map/prepare_features/pallas_call | solution.py:65
  3.5 0.0 copy-start.2
  3.5 6.0 %all-to-all-start = ((bf16[8,440,256]{2,1,0:T(8,128)(2,1)}), bf16[8,440,256]{2,1,0:T(8,128)(2,1)S(1)}, u32[]{:S(2)}, u32[]{:S(2)}) async-start(bf16[8,440,256]{2,1,0:T(8,128)(2,1)} %prepare_features.1), calls=%async_computation | async-start | bytes 3604480 | tf_op jit(solution)/shard_map/all_to_all | solution.py:311
  9.5 0.0 copy-start.3
  9.5 27.0 %all-gather = bf16[1728,128]{1,0:T(8,128)(2,1)S(1)} all-gather(bf16[216,128]{1,0:T(8,128)(2,1)S(1)} %reshape.48), channel_id=2, replica_groups=mesh['row'=8,'yhi'=4,'core'=2,'sample'=8] {'sample'}, dimensions={0}, use_global_device_ids=true | all-gather | bytes 497664 | tf_op jit(solution)/shard_map/all_gather | solution.py:312
  36.4 1.1 unshuffle.2.weights_ref
  37.5 0.0 copy-done.2
  37.5 0.1 reshape.50
  37.6 0.2 copy.15
  37.8 0.1 reshape.51.proj_ref
  37.9 0.0 copy-done.3
  37.9 0.1 copy.10
  38.1 0.0 all-to-all-done
  38.1 2.6 %forward_taps.3 = bf16[32,48,128]{2,1,0:T(8,128)(2,1)} custom-call(s32[1]{0:T(128)S(6)} %sub.3.parity_ref, bf16[4,2,440,256]{3,2,1,0:T(8,128)(2,1)S(1)} %bitcast.25, bf16[864,256]{1,0:T(8,128)(2,1)S(1)} %unshuffle.2.weights_ref), custom_call_target="tpu_custom_call" | custom-call | flops 764411904 | bytes 2000000 | tf_op jit(solution)/shard_map/forward_taps/pallas_call | solution.py:113
  40.8 7.4 %collective-permute-start = (bf16[32,48,128]{2,1,0:T(8,128)(2,1)}, bf16[32,48,128]{2,1,0:T(8,128)(2,1)}, u32[]{:S(2)}, u32[]{:S(2)}) collective-permute-start(bf16[32,48,128]{2,1,0:T(8,128)(2,1)} %forward_taps.3), channel_id=1, source_target_pairs={{0,8},{8,0},{1,9},{9,1},{2,10},{10,2},{3,11},{11,3},{4,12},{12,4},... | collective-permute-start | bytes 1179656 | tf_op jit(solution)/shard_map/ppermute | solution.py:321
  48.2 0.1 reshape.53
  48.3 0.1 reshape.54
  48.4 0.1 pad_dynamic-slice_fusion
  48.5 0.1 eq.15
  48.5 1.9 %forward_taps.2 = bf16[32,48,128]{2,1,0:T(8,128)(2,1)S(1)} custom-call(s32[1]{0:T(128)} %bitcast.parity_ref, bf16[4,2,440,256]{3,2,1,0:T(8,128)(2,1)S(1)} %bitcast.26, bf16[864,256]{1,0:T(8,128)(2,1)S(1)} %unshuffle.2.weights_ref), custom_call_target="tpu_custom_call" | custom-call | flops 764411904 | bytes 2000000 | tf_op jit(solution)/shard_map/forward_taps/pallas_call | solution.py:113
  50.4 0.1 compare_convert_fusion.onehot_ref
  50.5 0.0 collective-permute-done
  50.5 1.1 add_convert_fusion
  51.6 23.6 %all_to_all.25.parts_ref = bf16[32,48,128]{2,1,0:T(8,128)(2,1)S(1)} all-to-all(bf16[32,48,128]{2,1,0:T(8,128)(2,1)S(1)} %add_convert_fusion), channel_id=1, replica_groups=mesh['row'=8,'yhi'=4,'core'=2,'sample'=8] {'yhi','row'}, dimensions={0} | all-to-all | bytes 786432 | tf_op jit(solution)/shard_map/all_to_all | solution.py:332
  75.2 1.1 tail.1
  76.3 17.0 %all_to_all.26.own_ref = bf16[32,48,128]{2,1,0:T(8,128)(2,1)S(1)} all-to-all(bf16[32,48,128]{2,1,0:T(8,128)(2,1)S(1)} %tail.1), channel_id=1, replica_groups=mesh['row'=8,'yhi'=4,'core'=2,'sample'=8] {'yhi','row'}, dimensions={0} | all-to-all | bytes 786432 | tf_op jit(solution)/shard_map/all_to_all | solution.py:334
  93.3 5.4 %collective-permute-start.1 = (bf16[32,48,128]{2,1,0:T(8,128)(2,1)S(1)}, bf16[32,48,128]{2,1,0:T(8,128)(2,1)S(1)}, u32[]{:S(2)}, u32[]{:S(2)}) collective-permute-start(bf16[32,48,128]{2,1,0:T(8,128)(2,1)S(1)} %all_to_all.26.own_ref), channel_id=1, source_target_pairs={{0,8},{8,0},{1,9},{9,1},{2,10},{10,2},{3,11},{11,3},{4,12},{12,4},... | collective-permute-start | bytes 1179656 | tf_op jit(solution)/shard_map/ppermute | solution.py:335
  98.7 1.3 collective-permute-done.1.other_ref
  100.0 2.4 %gradient_taps.1 = bf16[8,216,128]{2,1,0:T(8,128)(2,1)S(1)} custom-call(s32[1]{0:T(128)} %bitcast.parity_ref, bf16[32,48,128]{2,1,0:T(8,128)(2,1)S(1)} %all_to_all.26.own_ref, bf16[32,48,128]{2,1,0:T(8,128)(2,1)S(1)} %collective-permute-done.1.other_ref, bf16[4,2,440,256]{3,2,1,0:T(8,128)(2,1)S(1)} %bitcast.27), custom_call_target="tpu_custom_call" | custom-call | flops 1528823808 | bytes 4000000 | tf_op jit(solution)/shard_map/gradient_taps/pallas_call | solution.py:254
  102.5 18.7 %all_to_all.27 = bf16[8,216,128]{2,1,0:T(8,128)(2,1)S(1)} all-to-all(bf16[8,216,128]{2,1,0:T(8,128)(2,1)S(1)} %gradient_taps.1), channel_id=1, replica_groups=mesh['row'=8,'yhi'=4,'core'=2,'sample'=8] {'sample'}, dimensions={0} | all-to-all | bytes 884736 | tf_op jit(solution)/shard_map/all_to_all | solution.py:337
  121.2 0.1 reduce_sum.12
  121.3 0.1 broadcast_in_dim.2
  121.3 10.1 %all_to_all.28.parts_ref = bf16[8,216,128]{2,1,0:T(8,128)(2,1)S(1)} all-to-all(bf16[8,216,128]{2,1,0:T(8,128)(2,1)S(1)} %broadcast_in_dim.2), channel_id=1, replica_groups=mesh['row'=8,'yhi'=4,'core'=2,'sample'=8] {'row'}, dimensions={0} | all-to-all | bytes 884736 | tf_op jit(solution)/shard_map/all_to_all | solution.py:339
  131.4 1.8 %unshuffle.3 = bf16[864,256]{1,0:T(8,128)(2,1)} custom-call(bf16[8,216,128]{2,1,0:T(8,128)(2,1)S(1)} %all_to_all.28.parts_ref), custom_call_target="tpu_custom_call" | custom-call | bytes 1000000 | tf_op jit(solution)/shard_map/unshuffle/pallas_call | solution.py:286
  (11 shorter events, 0.1 us)
Async XLA Ops:
  0.0 1.0 copy-start
  1.1 0.9 copy-start.1
  3.5 34.0 %copy-start.2 = (bf16[768,256]{1,0:T(8,128)(2,1)S(1)}, bf16[768,256]{1,0:T(8,128)(2,1)}, u32[]{:S(2)}) copy-start(bf16[768,256]{1,0:T(8,128)(2,1)} %param.7) | copy-start | bytes 1179652
  3.5 34.7 %all-to-all-start = ((bf16[8,440,256]{2,1,0:T(8,128)(2,1)}), bf16[8,440,256]{2,1,0:T(8,128)(2,1)S(1)}, u32[]{:S(2)}, u32[]{:S(2)}) async-start(bf16[8,440,256]{2,1,0:T(8,128)(2,1)} %prepare_features.1), calls=%async_computation | async-start | bytes 3604480 | tf_op jit(solution)/shard_map/all_to_all | solution.py:311
  9.5 28.5 %copy-start.3 = (bf16[256,3]{0,1:T(4,128)(2,1)S(1)}, bf16[256,3]{0,1:T(4,128)(2,1)}, u32[]{:S(2)}) copy-start(bf16[256,3]{0,1:T(4,128)(2,1)} %param.8) | copy-start | bytes 4612
  40.8 9.7 %collective-permute-start = (bf16[32,48,128]{2,1,0:T(8,128)(2,1)}, bf16[32,48,128]{2,1,0:T(8,128)(2,1)}, u32[]{:S(2)}, u32[]{:S(2)}) collective-permute-start(bf16[32,48,128]{2,1,0:T(8,128)(2,1)} %forward_taps.3), channel_id=1, source_target_pairs={{0,8},{8,0},{1,9},{9,1},{2,10},{10,2},{3,11},{11,3},{4,12},{12,4},... | collective-permute-start | bytes 1179656 | tf_op jit(solution)/shard_map/ppermute | solution.py:321
  93.3 6.7 %collective-permute-start.1 = (bf16[32,48,128]{2,1,0:T(8,128)(2,1)S(1)}, bf16[32,48,128]{2,1,0:T(8,128)(2,1)S(1)}, u32[]{:S(2)}, u32[]{:S(2)}) collective-permute-start(bf16[32,48,128]{2,1,0:T(8,128)(2,1)S(1)} %all_to_all.26.own_ref), channel_id=1, source_target_pairs={{0,8},{8,0},{1,9},{9,1},{2,10},{10,2},{3,11},{11,3},{4,12},{12,4},... | collective-permute-start | bytes 1179656 | tf_op jit(solution)/shard_map/ppermute | solution.py:335

commit v3 on v2

--- a/solution.py
+++ b/solution.py
@@ -25,7 +25,7 @@
 OUTS = 32
 TAPS = 27
 ROW_AXES = ("row",)
-VMEM_LIMIT = 48 * 1024 * 1024
+VMEM_LIMIT = 16 * 1024 * 1024
 
 
 def block_taps(j, q):
@@ -44,40 +44,102 @@
     return found
 
 
-def compiler_params():
-    return pltpu.CompilerParams(vmem_limit_bytes=VMEM_LIMIT)
-
-
-def prepare_kernel(features_ref, marks_ref, out_ref, rows_ref, units_ref):
-    rows_ref[...] = features_ref[...].astype(F32)
+def compiler_params(limit=VMEM_LIMIT):
+    return pltpu.CompilerParams(vmem_limit_bytes=limit)
+
+
+def prepare_kernel(
+    row_ref,
+    features_ref,
+    labels_ref,
+    weights_ref,
+    out_ref,
+    mine_ref,
+    local_ref,
+    marks_ref,
+    taps_ref,
+    rows_ref,
+    units_ref,
+    wide_ref,
+    packed_ref,
+    block_ref,
+    sems,
+):
+    copies = [
+        pltpu.make_async_copy(source, target, sems.at[place])
+        for place, (source, target) in enumerate(
+            ((features_ref, local_ref), (labels_ref, marks_ref), (weights_ref, taps_ref))
+        )
+    ]
+    for copy in copies:
+        copy.start()
+    units_ref[SHARD:, :] = jnp.zeros((SENT - SHARD, CHAN), F32)
+    copies[1].wait()
+    for row in range(6):
+        for q in range(GRID_Q):
+            units_ref[SHARD + q : SHARD + q + 1, row * 12 : row * 12 + 12] = marks_ref[
+                row, :, q * 12 : q * 12 + 12
+            ].astype(F32)
+    copies[0].wait()
+    rows_ref[...] = local_ref[...].astype(F32)
     for row in range(6):
         for q in range(GRID_Q):
             units_ref[q * UNIT + row * 12 : q * UNIT + row * 12 + 12, :] = rows_ref[
                 row * 72 + q * 12 : row * 72 + q * 12 + 12, :
             ]
-    units_ref[SHARD:, :] = marks_ref[...]
-    block = units_ref[...].astype(BF16)
-    for device in range(ROWS):
-        out_ref[device] = block
-
-
-def prepare(features, marks):
+    block_ref[...] = units_ref[...].astype(BF16)
+    sends = [
+        pltpu.make_async_copy(block_ref, out_ref.at[device], sems.at[3 + device]) for device in range(ROWS)
+    ]
+    for send in sends:
+        send.start()
+    copies[2].wait()
+    for lanes in range(2):
+        wide_ref[lanes] = taps_ref[:, lanes * LANES : (lanes + 1) * LANES].astype(F32)
+    first = row_ref[0] * 4
+    for slot in range(4):
+        for lanes in range(2):
+            packed_ref[pl.ds(slot * 2 + lanes, TAPS, stride=8), :] = wide_ref[
+                lanes, pl.ds(first + slot, TAPS, stride=OUTS), :
+            ]
+    mine_ref[...] = packed_ref[...].astype(BF16)
+    for send in sends:
+        send.wait()
+
+
+def prepare(row, features, labels, weights):
+    hbm = pl.BlockSpec(memory_space=pl.ANY)
+    vmem = pl.BlockSpec(memory_space=pltpu.VMEM)
     return pl.pallas_call(
         prepare_kernel,
-        out_shape=jax.ShapeDtypeStruct((ROWS, SENT, CHAN), BF16),
-        scratch_shapes=[pltpu.VMEM((SHARD, CHAN), F32), pltpu.VMEM((SENT, CHAN), F32)],
-        compiler_params=compiler_params(),
+        in_specs=[pl.BlockSpec(memory_space=pltpu.SMEM), hbm, hbm, hbm],
+        out_specs=[hbm, vmem],
+        out_shape=[
+            jax.ShapeDtypeStruct((ROWS, SENT, CHAN), BF16),
+            jax.ShapeDtypeStruct((BLOCK, LANES), BF16),
+        ],
+        scratch_shapes=[
+            pltpu.VMEM((SHARD, CHAN), BF16),
+            pltpu.VMEM((6, 1, 72), jnp.int32),
+            pltpu.VMEM((TAPS * OUTS, CHAN), BF16),
+            pltpu.VMEM((SHARD, CHAN), F32),
+            pltpu.VMEM((SENT, CHAN), F32),
+            pltpu.VMEM((2, TAPS * OUTS, LANES), F32),
+            pltpu.VMEM((BLOCK, LANES), F32),
+            pltpu.VMEM((SENT, CHAN), BF16),
+            pltpu.SemaphoreType.DMA((3 + ROWS,)),
+        ],
+        compiler_params=compiler_params(60 * 1024 * 1024),
         cost_estimate=pl.CostEstimate(flops=0, bytes_accessed=2 * 9 * SHARD * CHAN, transcendentals=0),
-        name="prepare_features",
-    )(features, marks)
+        name="prepare_blocks",
+    )(row, features, labels, weights)
 
 
 def unit_rows(q):
     return slice(q * UNIT, (q + 1) * UNIT)
 
 
-def forward_kernel(parity_ref, features_ref, weights_ref, out_ref, acc_ref, flat_ref):
-    del parity_ref
+def forward_kernel(core_ref, features_ref, weights_ref, own_ref, other_ref, acc_ref, flat_ref):
     acc_ref[...] = jnp.zeros(acc_ref.shape, F32)
     for j in range(GRID_J):
         for q in range(GRID_Q):
@@ -85,53 +147,51 @@
             kernels = jnp.concatenate(
                 [weights_ref[tap * OUTS : (tap + 1) * OUTS, :] for tap, _, _ in taps], axis=0
             )
+            pixels = jnp.concatenate(
+                [features_ref[j, 0, unit_rows(q), :], features_ref[j, 1, unit_rows(q), :]], axis=0
+            )
             product = lax.dot_general(
-                kernels,
-                features_ref[j, 0, unit_rows(q), :],
-                (((1,), (1,)), ((), ())),
-                preferred_element_type=F32,
+                kernels, pixels, (((1,), (1,)), ((), ())), preferred_element_type=F32
             )
             for place, (_, branch, block) in enumerate(taps):
                 lane = block % 4 * OUTS
-                acc_ref[block // 4, branch, lane : lane + OUTS, :UNIT] += product[
+                acc_ref[block // 4, branch, lane : lane + OUTS, : 2 * UNIT] += product[
                     place * OUTS : (place + 1) * OUTS, :
                 ]
     for group in range(UNITS // 4):
         for branch in range(3):
-            flat_ref[branch, group * UNIT : (group + 1) * UNIT, :] = jnp.transpose(
-                acc_ref[group, branch]
-            )[:UNIT, :]
-    for part in range(USED):
-        for branch in range(3):
-            out_ref[part, branch * 16 : (branch + 1) * 16, :] = flat_ref[
-                branch, part * 16 : (part + 1) * 16, :
-            ].astype(BF16)
-    out_ref[USED:] = jnp.zeros((PARTS - USED, SHARE, LANES), BF16)
-
-
-def forward(parity, features, weights):
+            turned = jnp.transpose(acc_ref[group, branch])
+            for half in range(2):
+                flat_ref[half, branch, group * UNIT : (group + 1) * UNIT, :] = turned[
+                    half * UNIT : (half + 1) * UNIT, :
+                ]
+    own = core_ref[0]
+    for half, out_ref in ((own, own_ref), (1 - own, other_ref)):
+        for part in range(USED):
+            for branch in range(3):
+                out_ref[part, branch * 16 : (branch + 1) * 16, :] = flat_ref[
+                    half, branch, part * 16 : (part + 1) * 16, :
+                ].astype(BF16)
+        out_ref[USED:] = jnp.zeros((PARTS - USED, SHARE, LANES), BF16)
+
+
+def forward(core, features, weights):
+    whole = pl.BlockSpec(memory_space=pltpu.VMEM)
     return pl.pallas_call(
         forward_kernel,
-        grid_spec=pltpu.PrefetchScalarGridSpec(
-            num_scalar_prefetch=1,
-            grid=(1,),
-            in_specs=[
-                pl.BlockSpec((GRID_J, 1, SENT, CHAN), lambda i, p: (0, p[0], 0, 0)),
-                pl.BlockSpec((TAPS * OUTS, CHAN), lambda i, p: (0, 0)),
-            ],
-            out_specs=pl.BlockSpec((PARTS, SHARE, LANES), lambda i, p: (0, 0, 0)),
-            scratch_shapes=[
-                pltpu.VMEM((UNITS // 4, 3, LANES, LANES), F32),
-                pltpu.VMEM((3, HALF // 4, LANES), F32),
-            ],
-        ),
-        out_shape=jax.ShapeDtypeStruct((PARTS, SHARE, LANES), BF16),
+        in_specs=[pl.BlockSpec(memory_space=pltpu.SMEM), whole, whole],
+        out_specs=[whole, whole],
+        out_shape=[jax.ShapeDtypeStruct((PARTS, SHARE, LANES), BF16)] * 2,
+        scratch_shapes=[
+            pltpu.VMEM((UNITS // 4, 3, LANES, 2 * LANES), F32),
+            pltpu.VMEM((2, 3, HALF // 4, LANES), F32),
+        ],
         compiler_params=compiler_params(),
         cost_estimate=pl.CostEstimate(
-            flops=2 * HALF * CHAN * TAPS * OUTS, bytes_accessed=2000000, transcendentals=0
+            flops=4 * HALF * CHAN * TAPS * OUTS, bytes_accessed=4000000, transcendentals=0
         ),
         name="forward_taps",
-    )(parity, features, weights)
+    )(core, features, weights)
 
 
 def sigmoid(values):
@@ -302,32 +362,30 @@
     part = lax.axis_index("yhi") * ROWS + row
     swap = [(0, 1), (1, 0)]
 
-    marks = labels.reshape(6, GRID_Q, 12).transpose(1, 0, 2).reshape(SHARD).astype(F32)
-    marks = jnp.pad(marks, (0, (SENT - SHARD) * CHAN - SHARD)).reshape(SENT - SHARD, CHAN)
-    sent = prepare(features.reshape(SHARD, CHAN), marks)
-    by_tap = weights.transpose(1, 2, 0, 3).reshape(TAPS, 32, CHAN)
-    mine = lax.dynamic_slice_in_dim(by_tap, 4 * row, 4, 1).reshape(BLOCK, LANES)
-    sent, mine = lax.optimization_barrier((sent, mine))
+    sent, mine = prepare(
+        row.astype(jnp.int32).reshape(1),
+        features.reshape(SHARD, CHAN),
+        labels.transpose(1, 0, 2),
+        weights.transpose(1, 2, 0, 3).reshape(TAPS * OUTS, CHAN),
+    )
     gathered = lax.all_to_all(sent, "row", 0, 0).reshape(GRID_J, 2, SENT, CHAN)
     kernels = unshuffle(lax.all_gather(mine, "sample"))
 
     mixing = proj.reshape(3, 8, ROWS, 4, CHAN).transpose(2, 0, 1, 3, 4).reshape(ROWS * 3 * OUTS, CHAN)
     heads = jnp.pad(classify, ((0, 0), (0, LANES - 3)))
     heads_t = jnp.pad(classify.T, ((0, LANES - 3), (0, 0)))
-    kernels, mixing, heads, heads_t = lax.optimization_barrier((kernels, mixing, heads, heads_t))
-
-    parity = core.astype(jnp.int32).reshape(1)
-    other = forward(1 - parity, gathered, kernels)
-    received = lax.ppermute(other, "core", swap)
-    own = forward(parity, gathered, kernels)
-    pair = (own.astype(F32) + received.astype(F32)).astype(BF16)
-
-    marks = lax.dynamic_index_in_dim(gathered[:, :, SHARD : SHARD + 2, :], core, 1, keepdims=False)
-    marks = marks.reshape(GRID_J, 2 * CHAN)[:, :SHARD].reshape(UNITS // 4, 4, UNIT)
-    marks = marks.transpose(1, 0, 2).reshape(4, HALF // 4)
+    marks = lax.dynamic_index_in_dim(gathered[:, :, SHARD : SHARD + GRID_Q, :UNIT], core, 1, keepdims=False)
+    marks = marks.reshape(UNITS // 4, 4, UNIT).transpose(1, 0, 2).reshape(4, HALF // 4)
     marks = lax.dynamic_slice_in_dim(jnp.pad(marks, ((0, 0), (0, (PARTS - USED) * 16))), part * 16, 16, 1)
     onehot = (marks.reshape(64, 1) == jnp.arange(LANES, dtype=BF16)[None, :]).astype(F32)
-    pair, onehot = lax.optimization_barrier((pair, onehot))
+    kernels, mixing, heads, heads_t, onehot = lax.optimization_barrier(
+        (kernels, mixing, heads, heads_t, onehot)
+    )
+
+    parity = core.astype(jnp.int32).reshape(1)
+    own, other = forward(parity, gathered, kernels)
+    received = lax.ppermute(other, "core", swap)
+    pair = (own.astype(F32) + received.astype(F32)).astype(BF16)
 
     parts = lax.all_to_all(pair, ("yhi", "row"), 0, 0)
     grads = tail(parts, mixing, heads, heads_t, onehot)

time: 134 us -> 131 us (0.978)
  other arithmetic: 1.99 us -> 0.25 us
    pallas_call x3 -> x2, Pallas kernels: 5.92 us -> 5.02 us  [the longest x1 2.95 us: prepare(): pl.pallas_call(prepare_kernel, in_specs=[pl.BlockSpec(memory_space=pltpu....]
  transfers between devices with their start and end apart: 3 -> 3, of which waited for: 1 -> 2; matrix products, arithmetic and copies ran while one was open for 1% -> 0% of each run, Pallas kernels for 2% -> 1%
where the time goes in v3:
time: 131 us
  blocking collectives  96.5 us (74%)
  starting transfers between devices  18.7 us (14%)
  Pallas kernels  11.4 us (9%)
  waiting for transfers between devices  2.66 us (2%)
    all_gather x1, blocking collectives, shards(): kernels = unshuffle(lax.all_gather(mine, 'sample'))  27 us
    all_to_all x1, blocking collectives, shards(): parts = lax.all_to_all(pair, ('yhi', 'row'), 0, 0)  23 us
    all_to_all x1, blocking collectives, shards(): over_samples = lax.all_to_all(partial, 'sample', 0, 0)  18.7 us
    all_to_all x1, blocking collectives, shards(): grads_own = lax.all_to_all(grads, ('yhi', 'row'), 0, 0)  17.6 us
    all_to_all x1, blocking collectives, shards(): lax.all_to_all(jnp.broadcast_to(summed[None], (ROWS, BLOCK, LANES)), 'row...  10.1 us
    ppermute x1, starting transfers between devices, shards(): received = lax.ppermute(other, 'core', swap)  7.38 us
    all_to_all x1, starting transfers between devices, shards(): gathered = lax.all_to_all(sent, 'row', 0, 0).reshape(GRID_J, 2, SENT, CHAN)  6.01 us
    ppermute x1, starting transfers between devices, shards(): grads_other = lax.ppermute(grads_own, 'core', swap)  5.3 us
  transfers between devices with their start and end apart: 3, of which 2 were waited for; matrix products, arithmetic and copies ran while one was open for 0% of the time, Pallas kernels for 1%

profile of v3, /device:TPU:1, one launch (start us, length us, event | category | flops | bytes accessed | tf_op | source)
XLA Modules:
  0.0 130.5 jit_solution(16172419919360061104)
XLA Ops:
  0.0 3.0 %prepare_blocks.1 = (bf16[8,440,256]{2,1,0:T(8,128)(2,1)}, bf16[216,128]{1,0:T(8,128)(2,1)}) custom-call(s32[1]{0:T(128)} %bitcast.1.row_ref, bf16[432,256]{1,0:T(8,128)(2,1)} %bitcast.23, s32[6,1,72]{2,1,0:T(1,128)} %bitcast.26, bf16[864,256]{1,0:T(8,128)(2,1)} %bitcast.22), custom_call_target="tpu_custom_call" | custom-call | bytes 1990656 | tf_op jit(solution)/shard_map/prepare_blocks/pallas_call | solution.py:113
  3.0 0.0 copy-start.1
  3.0 0.0 copy-start
  3.0 6.0 %all-to-all-start = ((bf16[8,440,256]{2,1,0:T(8,128)(2,1)}), bf16[8,440,256]{2,1,0:T(8,128)(2,1)S(1)}, u32[]{:S(2)}, u32[]{:S(2)}) async-start(bf16[8,440,256]{2,1,0:T(8,128)(2,1)} %get-tuple-element.14), calls=%async_computation | async-start | bytes 3604480 | tf_op jit(solution)/shard_map/all_to_all | solution.py:371
  9.0 0.0 copy-done.1
  9.0 0.0 copy-start.2
  9.0 27.0 %all-gather = bf16[1728,128]{1,0:T(8,128)(2,1)S(1)} all-gather(bf16[216,128]{1,0:T(8,128)(2,1)S(1)} %copy-done.1), channel_id=2, replica_groups=mesh['row'=8,'yhi'=4,'core'=2,'sample'=8] {'sample'}, dimensions={0}, use_global_device_ids=true | all-gather | bytes 497664 | tf_op jit(solution)/shard_map/all_gather | solution.py:372
  36.0 1.1 unshuffle.2.weights_ref
  37.1 0.0 copy-done
  37.1 0.1 reshape.39
  37.2 0.2 copy.12
  37.4 0.1 reshape.40.proj_ref
  37.5 0.0 copy-done.2
  37.5 0.1 copy.9
  37.7 0.0 all-to-all-done
  37.7 0.1 reshape.42
  37.8 0.1 pad_dynamic-slice_fusion
  37.9 0.1 eq.15
  38.0 0.1 compare_convert_fusion.onehot_ref
  38.1 2.1 %forward_taps.1 = (bf16[32,48,128]{2,1,0:T(8,128)(2,1)S(1)}, bf16[32,48,128]{2,1,0:T(8,128)(2,1)S(1)}) custom-call(s32[1]{0:T(128)} %bitcast.core_ref.parity_ref, bf16[4,2,440,256]{3,2,1,0:T(8,128)(2,1)S(1)} %bitcast.18, bf16[864,256]{1,0:T(8,128)(2,1)S(1)} %unshuffle.2.weights_ref), custom_call_target="tpu_custom_call" | custom-call | flops 1528823808 | bytes 4000000 | tf_op jit(solution)/shard_map/forward_taps/pallas_call | solution.py:180
  40.1 7.4 %collective-permute-start = (bf16[32,48,128]{2,1,0:T(8,128)(2,1)S(1)}, bf16[32,48,128]{2,1,0:T(8,128)(2,1)S(1)}, u32[]{:S(2)}, u32[]{:S(2)}) collective-permute-start(bf16[32,48,128]{2,1,0:T(8,128)(2,1)S(1)} %get-tuple-element.18), channel_id=1, source_target_pairs={{0,8},{8,0},{1,9},{9,1},{2,10},{10,2},{3,11},{11,3},{4,12},{12,4},... | collective-permute-start | bytes 1179656 | tf_op jit(solution)/shard_map/ppermute | solution.py:387
  47.5 1.3 %collective-permute-done = bf16[32,48,128]{2,1,0:T(8,128)(2,1)S(1)} collective-permute-done((bf16[32,48,128]{2,1,0:T(8,128)(2,1)S(1)}, bf16[32,48,128]{2,1,0:T(8,128)(2,1)S(1)}, u32[]{:S(2)}, u32[]{:S(2)}) %collective-permute-start) | collective-permute-done | bytes 393248 | tf_op jit(solution)/shard_map/ppermute | solution.py:387
  48.9 0.1 add_convert_fusion
  49.0 23.0 %all_to_all.25.parts_ref = bf16[32,48,128]{2,1,0:T(8,128)(2,1)S(1)} all-to-all(bf16[32,48,128]{2,1,0:T(8,128)(2,1)S(1)} %add_convert_fusion), channel_id=1, replica_groups=mesh['row'=8,'yhi'=4,'core'=2,'sample'=8] {'yhi','row'}, dimensions={0} | all-to-all | bytes 786432 | tf_op jit(solution)/shard_map/all_to_all | solution.py:390
  72.0 1.1 tail.1
  73.1 17.6 %all_to_all.26.own_ref = bf16[32,48,128]{2,1,0:T(8,128)(2,1)S(1)} all-to-all(bf16[32,48,128]{2,1,0:T(8,128)(2,1)S(1)} %tail.1), channel_id=1, replica_groups=mesh['row'=8,'yhi'=4,'core'=2,'sample'=8] {'yhi','row'}, dimensions={0} | all-to-all | bytes 786432 | tf_op jit(solution)/shard_map/all_to_all | solution.py:392
  90.7 5.3 %collective-permute-start.1 = (bf16[32,48,128]{2,1,0:T(8,128)(2,1)S(1)}, bf16[32,48,128]{2,1,0:T(8,128)(2,1)S(1)}, u32[]{:S(2)}, u32[]{:S(2)}) collective-permute-start(bf16[32,48,128]{2,1,0:T(8,128)(2,1)S(1)} %all_to_all.26.own_ref), channel_id=1, source_target_pairs={{0,8},{8,0},{1,9},{9,1},{2,10},{10,2},{3,11},{11,3},{4,12},{12,4},... | collective-permute-start | bytes 1179656 | tf_op jit(solution)/shard_map/ppermute | solution.py:393
  96.0 1.3 %collective-permute-done.1.other_ref = bf16[32,48,128]{2,1,0:T(8,128)(2,1)S(1)} collective-permute-done((bf16[32,48,128]{2,1,0:T(8,128)(2,1)S(1)}, bf16[32,48,128]{2,1,0:T(8,128)(2,1)S(1)}, u32[]{:S(2)}, u32[]{:S(2)}) %collective-permute-start.1) | collective-permute-done | bytes 393248 | tf_op jit(solution)/shard_map/ppermute | solution.py:393
  97.3 2.4 %gradient_taps.1 = bf16[8,216,128]{2,1,0:T(8,128)(2,1)S(1)} custom-call(s32[1]{0:T(128)} %bitcast.core_ref.parity_ref, bf16[32,48,128]{2,1,0:T(8,128)(2,1)S(1)} %all_to_all.26.own_ref, bf16[32,48,128]{2,1,0:T(8,128)(2,1)S(1)} %collective-permute-done.1.other_ref, bf16[4,2,440,256]{3,2,1,0:T(8,128)(2,1)S(1)} %bitcast.19), custom_call_target="tpu_custom_call" | custom-call | flops 1528823808 | bytes 4000000 | tf_op jit(solution)/shard_map/gradient_taps/pallas_call | solution.py:314
  99.8 18.7 %all_to_all.27 = bf16[8,216,128]{2,1,0:T(8,128)(2,1)S(1)} all-to-all(bf16[8,216,128]{2,1,0:T(8,128)(2,1)S(1)} %gradient_taps.1), channel_id=1, replica_groups=mesh['row'=8,'yhi'=4,'core'=2,'sample'=8] {'sample'}, dimensions={0} | all-to-all | bytes 884736 | tf_op jit(solution)/shard_map/all_to_all | solution.py:395
  118.5 0.1 reduce_sum.12
  118.6 0.1 broadcast_in_dim.2
  118.6 10.1 %all_to_all.28.parts_ref = bf16[8,216,128]{2,1,0:T(8,128)(2,1)S(1)} all-to-all(bf16[8,216,128]{2,1,0:T(8,128)(2,1)S(1)} %broadcast_in_dim.2), channel_id=1, replica_groups=mesh['row'=8,'yhi'=4,'core'=2,'sample'=8] {'row'}, dimensions={0} | all-to-all | bytes 884736 | tf_op jit(solution)/shard_map/all_to_all | solution.py:397
  128.7 1.8 %unshuffle.3 = bf16[864,256]{1,0:T(8,128)(2,1)} custom-call(bf16[8,216,128]{2,1,0:T(8,128)(2,1)S(1)} %all_to_all.28.parts_ref), custom_call_target="tpu_custom_call" | custom-call | bytes 1000000 | tf_op jit(solution)/shard_map/unshuffle/pallas_call | solution.py:346
  (6 shorter events, 0.1 us)
Async XLA Ops:
  3.0 6.0 %copy-start.1 = (bf16[216,128]{1,0:T(8,128)(2,1)S(1)}, bf16[216,128]{1,0:T(8,128)(2,1)}, u32[]{:S(2)}) copy-start(bf16[216,128]{1,0:T(8,128)(2,1)} %get-tuple-element.15) | copy-start | bytes 165892
  3.0 34.1 %copy-start = (bf16[768,256]{1,0:T(8,128)(2,1)S(1)}, bf16[768,256]{1,0:T(8,128)(2,1)}, u32[]{:S(2)}) copy-start(bf16[768,256]{1,0:T(8,128)(2,1)} %param.7) | copy-start | bytes 1179652
  3.0 34.7 %all-to-all-start = ((bf16[8,440,256]{2,1,0:T(8,128)(2,1)}), bf16[8,440,256]{2,1,0:T(8,128)(2,1)S(1)}, u32[]{:S(2)}, u32[]{:S(2)}) async-start(bf16[8,440,256]{2,1,0:T(8,128)(2,1)} %get-tuple-element.14), calls=%async_computation | async-start | bytes 3604480 | tf_op jit(solution)/shard_map/all_to_all | solution.py:371
  9.0 28.5 %copy-start.2 = (bf16[256,3]{0,1:T(4,128)(2,1)S(1)}, bf16[256,3]{0,1:T(4,128)(2,1)}, u32[]{:S(2)}) copy-start(bf16[256,3]{0,1:T(4,128)(2,1)} %param.8) | copy-start | bytes 4612
  40.1 8.7 %collective-permute-start = (bf16[32,48,128]{2,1,0:T(8,128)(2,1)S(1)}, bf16[32,48,128]{2,1,0:T(8,128)(2,1)S(1)}, u32[]{:S(2)}, u32[]{:S(2)}) collective-permute-start(bf16[32,48,128]{2,1,0:T(8,128)(2,1)S(1)} %get-tuple-element.18), channel_id=1, source_target_pairs={{0,8},{8,0},{1,9},{9,1},{2,10},{10,2},{3,11},{11,3},{4,12},{12,4},... | collective-permute-start | bytes 1179656 | tf_op jit(solution)/shard_map/ppermute | solution.py:387
  90.7 6.6 %collective-permute-start.1 = (bf16[32,48,128]{2,1,0:T(8,128)(2,1)S(1)}, bf16[32,48,128]{2,1,0:T(8,128)(2,1)S(1)}, u32[]{:S(2)}, u32[]{:S(2)}) collective-permute-start(bf16[32,48,128]{2,1,0:T(8,128)(2,1)S(1)} %all_to_all.26.own_ref), channel_id=1, source_target_pairs={{0,8},{8,0},{1,9},{9,1},{2,10},{10,2},{3,11},{11,3},{4,12},{12,4},... | collective-permute-start | bytes 1179656 | tf_op jit(solution)/shard_map/ppermute | solution.py:393

commit v4 on v3

--- a/solution.py
+++ b/solution.py
@@ -65,10 +65,11 @@
     block_ref,
     sems,
 ):
+    near = weights_ref.at[:, pl.ds(row_ref[0] // 4 * 16, 16), :]
     copies = [
         pltpu.make_async_copy(source, target, sems.at[place])
         for place, (source, target) in enumerate(
-            ((features_ref, local_ref), (labels_ref, marks_ref), (weights_ref, taps_ref))
+            ((features_ref, local_ref), (labels_ref, marks_ref), (near, taps_ref))
         )
     ]
     for copy in copies:
@@ -94,13 +95,16 @@
     for send in sends:
         send.start()
     copies[2].wait()
-    for lanes in range(2):
-        wide_ref[lanes] = taps_ref[:, lanes * LANES : (lanes + 1) * LANES].astype(F32)
-    first = row_ref[0] * 4
+    for tap in range(TAPS):
+        for lanes in range(2):
+            wide_ref[lanes, tap * 16 : (tap + 1) * 16, :] = taps_ref[
+                tap, :, lanes * LANES : (lanes + 1) * LANES
+            ].astype(F32)
+    first = row_ref[0] % 4 * 4
     for slot in range(4):
         for lanes in range(2):
             packed_ref[pl.ds(slot * 2 + lanes, TAPS, stride=8), :] = wide_ref[
-                lanes, pl.ds(first + slot, TAPS, stride=OUTS), :
+                lanes, pl.ds(first + slot, TAPS, stride=16), :
             ]
     mine_ref[...] = packed_ref[...].astype(BF16)
     for send in sends:
@@ -121,10 +125,10 @@
         scratch_shapes=[
             pltpu.VMEM((SHARD, CHAN), BF16),
             pltpu.VMEM((6, 1, 72), jnp.int32),
-            pltpu.VMEM((TAPS * OUTS, CHAN), BF16),
+            pltpu.VMEM((TAPS, 16, CHAN), BF16),
             pltpu.VMEM((SHARD, CHAN), F32),
             pltpu.VMEM((SENT, CHAN), F32),
-            pltpu.VMEM((2, TAPS * OUTS, LANES), F32),
+            pltpu.VMEM((2, TAPS * 16, LANES), F32),
             pltpu.VMEM((BLOCK, LANES), F32),
             pltpu.VMEM((SENT, CHAN), BF16),
             pltpu.SemaphoreType.DMA((3 + ROWS,)),
@@ -139,8 +143,25 @@
     return slice(q * UNIT, (q + 1) * UNIT)
 
 
-def forward_kernel(core_ref, features_ref, weights_ref, own_ref, other_ref, acc_ref, flat_ref):
+def spread_rows(packed_ref, rows_ref, out_ref):
+    for slot in range(OUTS):
+        for lanes in range(2):
+            rows_ref[lanes, pl.ds(slot, TAPS, stride=OUTS), :] = packed_ref[
+                pl.ds(slot // 4 * BLOCK + slot % 4 * 2 + lanes, TAPS, stride=8), :
+            ]
+    for lanes in range(2):
+        out_ref[:, lanes * LANES : (lanes + 1) * LANES] = rows_ref[lanes].astype(BF16)
+
+
+def forward_kernel(
+    core_ref, zlo_ref, features_ref, parts_ref, own_ref, other_ref, acc_ref, flat_ref, packed_ref, rows_ref, weights_ref
+):
     acc_ref[...] = jnp.zeros(acc_ref.shape, F32)
+    for sample in range(8):
+        packed_ref[sample * BLOCK : (sample + 1) * BLOCK, :] = parts_ref[
+            sample // 2, sample % 2 ^ zlo_ref[0]
+        ].astype(F32)
+    spread_rows(packed_ref, rows_ref, weights_ref)
     for j in range(GRID_J):
         for q in range(GRID_Q):
             taps = block_taps(j, q)
@@ -175,23 +196,26 @@
         out_ref[USED:] = jnp.zeros((PARTS - USED, SHARE, LANES), BF16)
 
 
-def forward(core, features, weights):
+def forward(core, zlo, features, parts):
     whole = pl.BlockSpec(memory_space=pltpu.VMEM)
     return pl.pallas_call(
         forward_kernel,
-        in_specs=[pl.BlockSpec(memory_space=pltpu.SMEM), whole, whole],
+        in_specs=[pl.BlockSpec(memory_space=pltpu.SMEM)] * 2 + [whole, whole],
         out_specs=[whole, whole],
         out_shape=[jax.ShapeDtypeStruct((PARTS, SHARE, LANES), BF16)] * 2,
         scratch_shapes=[
             pltpu.VMEM((UNITS // 4, 3, LANES, 2 * LANES), F32),
             pltpu.VMEM((2, 3, HALF // 4, LANES), F32),
+            pltpu.VMEM((8 * BLOCK, LANES), F32),
+            pltpu.VMEM((2, TAPS * OUTS, LANES), F32),
+            pltpu.VMEM((TAPS * OUTS, CHAN), BF16),
         ],
         compiler_params=compiler_params(),
         cost_estimate=pl.CostEstimate(
             flops=4 * HALF * CHAN * TAPS * OUTS, bytes_accessed=4000000, transcendentals=0
         ),
         name="forward_taps",
-    )(core, features, weights)
+    )(core, zlo, features, parts)
 
 
 def sigmoid(values):
@@ -330,29 +354,41 @@
     )(parity, own, other, features)
 
 
-def unshuffle_kernel(parts_ref, out_ref, packed_ref, rows_ref):
+def finish_kernel(parts_ref, out_ref, packed_ref, rows_ref, done_ref, sems):
     for block in range(8):
         packed_ref[block * BLOCK : (block + 1) * BLOCK, :] = parts_ref[block].astype(F32)
-    for slot in range(OUTS):
+    sends = []
+    for place, first in enumerate(range(0, TAPS, 9)):
+        at = slice(first * OUTS, (first + 9) * OUTS)
+        for slot in range(OUTS):
+            for lanes in range(2):
+                source = slot // 4 * BLOCK + slot % 4 * 2 + lanes + first * 8
+                rows_ref[lanes, pl.ds(first * OUTS + slot, 9, stride=OUTS), :] = packed_ref[
+                    pl.ds(source, 9, stride=8), :
+                ]
         for lanes in range(2):
-            rows_ref[lanes, pl.ds(slot, TAPS, stride=OUTS), :] = packed_ref[
-                pl.ds(slot // 4 * BLOCK + slot % 4 * 2 + lanes, TAPS, stride=8), :
-            ]
-    for lanes in range(2):
-        out_ref[:, lanes * LANES : (lanes + 1) * LANES] = rows_ref[lanes].astype(BF16)
-
-
-def unshuffle(parts):
+            done_ref[at, lanes * LANES : (lanes + 1) * LANES] = rows_ref[lanes, at, :].astype(BF16)
+        sends.append(pltpu.make_async_copy(done_ref.at[at], out_ref.at[at], sems.at[place]))
+        sends[-1].start()
+    for send in sends:
+        send.wait()
+
+
+def finish(parts):
     return pl.pallas_call(
-        unshuffle_kernel,
+        finish_kernel,
+        in_specs=[pl.BlockSpec(memory_space=pltpu.VMEM)],
+        out_specs=pl.BlockSpec(memory_space=pl.ANY),
         out_shape=jax.ShapeDtypeStruct((TAPS * OUTS, CHAN), BF16),
         scratch_shapes=[
             pltpu.VMEM((8 * BLOCK, LANES), F32),
             pltpu.VMEM((2, TAPS * OUTS, LANES), F32),
+            pltpu.VMEM((TAPS * OUTS, CHAN), BF16),
+            pltpu.SemaphoreType.DMA((3,)),
         ],
         compiler_params=compiler_params(),
         cost_estimate=pl.CostEstimate(flops=0, bytes_accessed=1000000, transcendentals=0),
-        name="unshuffle",
+        name="finish",
     )(parts)
 
 
@@ -366,10 +402,11 @@
         row.astype(jnp.int32).reshape(1),
         features.reshape(SHARD, CHAN),
         labels.transpose(1, 0, 2),
-        weights.transpose(1, 2, 0, 3).reshape(TAPS * OUTS, CHAN),
+        weights.transpose(1, 2, 0, 3).reshape(TAPS, OUTS, CHAN),
     )
     gathered = lax.all_to_all(sent, "row", 0, 0).reshape(GRID_J, 2, SENT, CHAN)
-    kernels = unshuffle(lax.all_gather(mine, "sample"))
+    pairs = jnp.stack([mine, lax.ppermute(mine, "zlo", swap)])
+    kernels = lax.all_gather(pairs, "zhi")
 
     mixing = proj.reshape(3, 8, ROWS, 4, CHAN).transpose(2, 0, 1, 3, 4).reshape(ROWS * 3 * OUTS, CHAN)
     heads = jnp.pad(classify, ((0, 0), (0, LANES - 3)))
@@ -383,7 +420,8 @@
     )
 
     parity = core.astype(jnp.int32).reshape(1)
-    own, other = forward(parity, gathered, kernels)
+    zlo = lax.axis_index("zlo").astype(jnp.int32).reshape(1)
+    own, other = forward(parity, zlo, gathered, kernels)
     received = lax.ppermute(other, "core", swap)
     pair = (own.astype(F32) + received.astype(F32)).astype(BF16)
 
@@ -392,20 +430,21 @@
     grads_own = lax.all_to_all(grads, ("yhi", "row"), 0, 0)
     grads_other = lax.ppermute(grads_own, "core", swap)
     partial = gradient(parity, grads_own, grads_other, gathered)
-    over_samples = lax.all_to_all(partial, "sample", 0, 0)
+    over_samples = lax.all_to_all(partial, ("zhi", "zlo"), 0, 0)
     summed = jnp.sum(over_samples.astype(F32), axis=0).astype(BF16)
     final = lax.all_to_all(jnp.broadcast_to(summed[None], (ROWS, BLOCK, LANES)), "row", 0, 0)
-    return unshuffle(final).reshape(3, 9, 32, CHAN).transpose(2, 0, 1, 3)
+    return finish(final).reshape(3, 9, 32, CHAN).transpose(2, 0, 1, 3)
 
 
 def solution(mesh):
-    split = Mesh(mesh.devices.reshape(8, 4, 2, 8), ("row", "yhi", "core", "sample"))
+    split = Mesh(mesh.devices.reshape(8, 4, 2, 4, 2), ("row", "yhi", "core", "zhi", "zlo"))
+    sample, channel = ("zhi", "zlo"), ("yhi", "core")
     in_specs = (
-        P("sample", "row", None, ("yhi", "core")),
-        P("sample", None, None, ("yhi", "core")),
+        P(sample, "row", None, channel),
+        P(sample, None, None, channel),
         P(),
         P(),
-        P("sample", "row", None),
+        P(sample, "row", None),
     )
-    out_specs = P("sample", None, None, ("yhi", "core"))
+    out_specs = P(sample, None, None, channel)
     return jax.shard_map(shards, mesh=split, in_specs=in_specs, out_specs=out_specs, check_vma=False)

time: 131 us -> 127 us (0.969)
  blocking collectives: 96.5 us -> 89 us
  starting transfers between devices: 18.7 us -> 21.2 us
    all_gather x1, blocking collectives: 27 us -> 18.7 us  [shards(): kernels = lax.all_gather(pairs, 'zhi')]
    ppermute x0 -> x1, starting transfers between devices: none -> 4 us  [shards(): pairs = jnp.stack([mine, lax.ppermute(mine, 'zlo', swap)])]
    ppermute x1, starting transfers between devices: 7.38 us -> 5.93 us  [shards(): received = lax.ppermute(other, 'core', swap)]
    pallas_call x2 -> x1, Pallas kernels: 2.89 us -> 1.67 us  [finish(): pl.pallas_call(finish_kernel, in_specs=[pl.BlockSpec(memory_space=pltpu.V...]
  transfers between devices with their start and end apart: 3 -> 4, of which waited for: 2 -> 3; matrix products, arithmetic and copies ran while one was open for 0% -> 0% of each run, Pallas kernels for 1% -> 0%
where the time goes in v4:
time: 127 us; the launch traced here: 126 us
  blocking collectives  89 us (70%)
  starting transfers between devices  21.2 us (17%)
  Pallas kernels  11.1 us (9%)
  waiting for transfers between devices  3.57 us (3%)
    all_to_all x1, blocking collectives, shards(): parts = lax.all_to_all(pair, ('yhi', 'row'), 0, 0)  23.2 us
    all_to_all x1, blocking collectives, shards(): over_samples = lax.all_to_all(partial, ('zhi', 'zlo'), 0, 0)  19.3 us
    all_gather x1, blocking collectives, shards(): kernels = lax.all_gather(pairs, 'zhi')  18.7 us
    all_to_all x1, blocking collectives, shards(): grads_own = lax.all_to_all(grads, ('yhi', 'row'), 0, 0)  17.6 us
    all_to_all x1, blocking collectives, shards(): lax.all_to_all(jnp.broadcast_to(summed[None], (ROWS, BLOCK, LANES)), 'row...  10.1 us
    all_to_all x1, starting transfers between devices, shards(): gathered = lax.all_to_all(sent, 'row', 0, 0).reshape(GRID_J, 2, SENT, CHAN)  6.01 us
    ppermute x1, starting transfers between devices, shards(): received = lax.ppermute(other, 'core', swap)  5.93 us
    ppermute x1, starting transfers between devices, shards(): grads_other = lax.ppermute(grads_own, 'core', swap)  5.3 us
  transfers between devices with their start and end apart: 4, of which 3 were waited for; matrix products, arithmetic and copies ran while one was open for 0% of the time, Pallas kernels for 0%

profile of v4, /device:TPU:1, one launch (start us, length us, event | category | flops | bytes accessed | tf_op | source)
XLA Modules:
  0.0 126.3 jit_solution(17751780191900721398)
XLA Ops:
  0.0 2.9 %prepare_blocks.1 = (bf16[8,440,256]{2,1,0:T(8,128)(2,1)}, bf16[216,128]{1,0:T(8,128)(2,1)}) custom-call(s32[1]{0:T(128)} %bitcast.2.row_ref, bf16[432,256]{1,0:T(8,128)(2,1)} %bitcast.26, s32[6,1,72]{2,1,0:T(1,128)} %bitcast.31, bf16[27,32,256]{2,1,0:T(8,128)(2,1)} %bitcast.25), custom_call_target="tpu_custom_call" | custom-call | bytes 1990656 | tf_op jit(solution)/shard_map/prepare_blocks/pallas_call | solution.py:117
  3.0 0.0 copy-start.1
  3.0 0.0 copy-start
  3.0 6.0 %all-to-all-start = ((bf16[8,440,256]{2,1,0:T(8,128)(2,1)}), bf16[8,440,256]{2,1,0:T(8,128)(2,1)S(1)}, u32[]{:S(2)}, u32[]{:S(2)}) async-start(bf16[8,440,256]{2,1,0:T(8,128)(2,1)} %get-tuple-element.14), calls=%async_computation | async-start | bytes 3604480 | tf_op jit(solution)/shard_map/all_to_all | solution.py:407
  9.0 0.0 copy-start.2
  9.0 0.0 copy-done.1
  9.0 4.0 %collective-permute-start = (bf16[216,128]{1,0:T(8,128)(2,1)S(1)}, bf16[216,128]{1,0:T(8,128)(2,1)S(1)}, u32[]{:S(2)}, u32[]{:S(2)}) collective-permute-start(bf16[216,128]{1,0:T(8,128)(2,1)S(1)} %copy-done.1), channel_id=1, source_target_pairs={{0,1},{1,0},{2,3},{3,2},{4,5},{5,4},{6,7},{7,6},{8,9},{9,8},{10,11... | collective-permute-start | bytes 165896 | tf_op jit(solution)/shard_map/ppermute | solution.py:408
  13.0 0.0 copy-done
  13.0 0.1 reshape.43
  13.1 0.2 copy.15
  13.3 0.1 reshape.44.proj_ref
  13.4 0.0 copy-done.2
  13.4 0.1 copy.12
  13.6 0.9 collective-permute-done
  14.6 18.7 %all-gather = bf16[8,216,128]{2,1,0:T(8,128)(2,1)S(1)} all-gather(bf16[2,216,128]{2,1,0:T(8,128)(2,1)S(1)} %pad_maximum_fusion), channel_id=2, replica_groups=mesh['row'=8,'yhi'=4,'core'=2,'zhi'=4,'zlo'=2] {'zhi'}, dimensions={0}, use_global_device_ids=true | all-gather | bytes 552960 | tf_op jit(solution)/shard_map/all_gather | solution.py:409
  33.3 0.0 all-to-all-done
  33.4 0.1 reshape.46
  33.4 0.1 pad_dynamic-slice_fusion
  33.5 0.1 eq.15
  33.6 0.1 compare_convert_fusion.onehot_ref
  33.7 3.0 %forward_taps.1 = (bf16[32,48,128]{2,1,0:T(8,128)(2,1)S(1)}, bf16[32,48,128]{2,1,0:T(8,128)(2,1)S(1)}) custom-call(s32[1]{0:T(128)} %bitcast.core_ref.parity_ref, s32[1]{0:T(128)} %bitcast.1.zlo_ref, bf16[4,2,440,256]{3,2,1,0:T(8,128)(2,1)S(1)} %bitcast.21, bf16[4,2,216,128]{3,2,1,0:T(8,128)(2,1)S(1)} %bitcast.23), custom_call_target="tpu_custom_call" | custom-call | flops 1528823808 | bytes 4000000 | tf_op jit(solution)/shard_map/forward_taps/pallas_call | solution.py:201
  36.7 5.9 %collective-permute-start.1 = (bf16[32,48,128]{2,1,0:T(8,128)(2,1)S(1)}, bf16[32,48,128]{2,1,0:T(8,128)(2,1)S(1)}, u32[]{:S(2)}, u32[]{:S(2)}) collective-permute-start(bf16[32,48,128]{2,1,0:T(8,128)(2,1)S(1)} %get-tuple-element.18), channel_id=1, source_target_pairs={{0,8},{8,0},{1,9},{9,1},{2,10},{10,2},{3,11},{11,3},{4,12},{12,4},... | collective-permute-start | bytes 1179656 | tf_op jit(solution)/shard_map/ppermute | solution.py:425
  42.7 1.3 %collective-permute-done.1 = bf16[32,48,128]{2,1,0:T(8,128)(2,1)S(1)} collective-permute-done((bf16[32,48,128]{2,1,0:T(8,128)(2,1)S(1)}, bf16[32,48,128]{2,1,0:T(8,128)(2,1)S(1)}, u32[]{:S(2)}, u32[]{:S(2)}) %collective-permute-start.1) | collective-permute-done | bytes 393248 | tf_op jit(solution)/shard_map/ppermute | solution.py:425
  44.0 0.1 add_convert_fusion
  44.1 23.2 %all_to_all.25.parts_ref = bf16[32,48,128]{2,1,0:T(8,128)(2,1)S(1)} all-to-all(bf16[32,48,128]{2,1,0:T(8,128)(2,1)S(1)} %add_convert_fusion), channel_id=1, replica_groups=mesh['row'=8,'yhi'=4,'core'=2,'zhi'=4,'zlo'=2] {'yhi','row'}, dimensions={0} | all-to-all | bytes 786432 | tf_op jit(solution)/shard_map/all_to_all | solution.py:428
  67.3 1.1 tail.1
  68.4 17.6 %all_to_all.26.own_ref = bf16[32,48,128]{2,1,0:T(8,128)(2,1)S(1)} all-to-all(bf16[32,48,128]{2,1,0:T(8,128)(2,1)S(1)} %tail.1), channel_id=1, replica_groups=mesh['row'=8,'yhi'=4,'core'=2,'zhi'=4,'zlo'=2] {'yhi','row'}, dimensions={0} | all-to-all | bytes 786432 | tf_op jit(solution)/shard_map/all_to_all | solution.py:430
  86.0 5.3 %collective-permute-start.2 = (bf16[32,48,128]{2,1,0:T(8,128)(2,1)S(1)}, bf16[32,48,128]{2,1,0:T(8,128)(2,1)S(1)}, u32[]{:S(2)}, u32[]{:S(2)}) collective-permute-start(bf16[32,48,128]{2,1,0:T(8,128)(2,1)S(1)} %all_to_all.26.own_ref), channel_id=1, source_target_pairs={{0,8},{8,0},{1,9},{9,1},{2,10},{10,2},{3,11},{11,3},{4,12},{12,4},... | collective-permute-start | bytes 1179656 | tf_op jit(solution)/shard_map/ppermute | solution.py:431
  91.3 1.3 %collective-permute-done.2.other_ref = bf16[32,48,128]{2,1,0:T(8,128)(2,1)S(1)} collective-permute-done((bf16[32,48,128]{2,1,0:T(8,128)(2,1)S(1)}, bf16[32,48,128]{2,1,0:T(8,128)(2,1)S(1)}, u32[]{:S(2)}, u32[]{:S(2)}) %collective-permute-start.2) | collective-permute-done | bytes 393248 | tf_op jit(solution)/shard_map/ppermute | solution.py:431
  92.6 2.4 %gradient_taps.1 = bf16[8,216,128]{2,1,0:T(8,128)(2,1)S(1)} custom-call(s32[1]{0:T(128)} %bitcast.core_ref.parity_ref, bf16[32,48,128]{2,1,0:T(8,128)(2,1)S(1)} %all_to_all.26.own_ref, bf16[32,48,128]{2,1,0:T(8,128)(2,1)S(1)} %collective-permute-done.2.other_ref, bf16[4,2,440,256]{3,2,1,0:T(8,128)(2,1)S(1)} %bitcast.22), custom_call_target="tpu_custom_call" | custom-call | flops 1528823808 | bytes 4000000 | tf_op jit(solution)/shard_map/gradient_taps/pallas_call | solution.py:338
  95.1 19.3 %all_to_all.27 = bf16[8,216,128]{2,1,0:T(8,128)(2,1)S(1)} all-to-all(bf16[8,216,128]{2,1,0:T(8,128)(2,1)S(1)} %gradient_taps.1), channel_id=1, replica_groups=mesh['row'=8,'yhi'=4,'core'=2,'zhi'=4,'zlo'=2] {'zhi','zlo'}, dimensions={0} | all-to-all | bytes 884736 | tf_op jit(solution)/shard_map/all_to_all | solution.py:433
  114.4 0.1 reduce_sum.12
  114.4 0.1 broadcast_in_dim.2
  114.5 10.1 %all_to_all.28.parts_ref = bf16[8,216,128]{2,1,0:T(8,128)(2,1)S(1)} all-to-all(bf16[8,216,128]{2,1,0:T(8,128)(2,1)S(1)} %broadcast_in_dim.2), channel_id=1, replica_groups=mesh['row'=8,'yhi'=4,'core'=2,'zhi'=4,'zlo'=2] {'row'}, dimensions={0} | all-to-all | bytes 884736 | tf_op jit(solution)/shard_map/all_to_all | solution.py:435
  124.6 1.7 %finish.1 = bf16[864,256]{1,0:T(8,128)(2,1)} custom-call(bf16[8,216,128]{2,1,0:T(8,128)(2,1)S(1)} %all_to_all.28.parts_ref), custom_call_target="tpu_custom_call" | custom-call | bytes 1000000 | tf_op jit(solution)/shard_map/finish/pallas_call | solution.py:378
  (7 shorter events, 0.1 us)
Async XLA Ops:
  3.0 6.0 %copy-start.1 = (bf16[216,128]{1,0:T(8,128)(2,1)S(1)}, bf16[216,128]{1,0:T(8,128)(2,1)}, u32[]{:S(2)}) copy-start(bf16[216,128]{1,0:T(8,128)(2,1)} %get-tuple-element.15) | copy-start | bytes 165892
  3.0 10.1 %copy-start = (bf16[768,256]{1,0:T(8,128)(2,1)S(1)}, bf16[768,256]{1,0:T(8,128)(2,1)}, u32[]{:S(2)}) copy-start(bf16[768,256]{1,0:T(8,128)(2,1)} %param.7) | copy-start | bytes 1179652
  3.0 30.3 %all-to-all-start = ((bf16[8,440,256]{2,1,0:T(8,128)(2,1)}), bf16[8,440,256]{2,1,0:T(8,128)(2,1)S(1)}, u32[]{:S(2)}, u32[]{:S(2)}) async-start(bf16[8,440,256]{2,1,0:T(8,128)(2,1)} %get-tuple-element.14), calls=%async_computation | async-start | bytes 3604480 | tf_op jit(solution)/shard_map/all_to_all | solution.py:407
  9.0 4.5 %copy-start.2 = (bf16[256,3]{0,1:T(4,128)(2,1)S(1)}, bf16[256,3]{0,1:T(4,128)(2,1)}, u32[]{:S(2)}) copy-start(bf16[256,3]{0,1:T(4,128)(2,1)} %param.8) | copy-start | bytes 4612
  9.0 5.5 %collective-permute-start = (bf16[216,128]{1,0:T(8,128)(2,1)S(1)}, bf16[216,128]{1,0:T(8,128)(2,1)S(1)}, u32[]{:S(2)}, u32[]{:S(2)}) collective-permute-start(bf16[216,128]{1,0:T(8,128)(2,1)S(1)} %copy-done.1), channel_id=1, source_target_pairs={{0,1},{1,0},{2,3},{3,2},{4,5},{5,4},{6,7},{7,6},{8,9},{9,8},{10,11... | collective-permute-start | bytes 165896 | tf_op jit(solution)/shard_map/ppermute | solution.py:408
  36.7 7.3 %collective-permute-start.1 = (bf16[32,48,128]{2,1,0:T(8,128)(2,1)S(1)}, bf16[32,48,128]{2,1,0:T(8,128)(2,1)S(1)}, u32[]{:S(2)}, u32[]{:S(2)}) collective-permute-start(bf16[32,48,128]{2,1,0:T(8,128)(2,1)S(1)} %get-tuple-element.18), channel_id=1, source_target_pairs={{0,8},{8,0},{1,9},{9,1},{2,10},{10,2},{3,11},{11,3},{4,12},{12,4},... | collective-permute-start | bytes 1179656 | tf_op jit(solution)/shard_map/ppermute | solution.py:425
  86.0 6.6 %collective-permute-start.2 = (bf16[32,48,128]{2,1,0:T(8,128)(2,1)S(1)}, bf16[32,48,128]{2,1,0:T(8,128)(2,1)S(1)}, u32[]{:S(2)}, u32[]{:S(2)}) collective-permute-start(bf16[32,48,128]{2,1,0:T(8,128)(2,1)S(1)} %all_to_all.26.own_ref), channel_id=1, source_target_pairs={{0,8},{8,0},{1,9},{9,1},{2,10},{10,2},{3,11},{11,3},{4,12},{12,4},... | collective-permute-start | bytes 1179656 | tf_op jit(solution)/shard_map/ppermute | solution.py:431

commit v5 on v3

--- a/solution.py
+++ b/solution.py
@@ -19,7 +19,6 @@
 PARTS = 32
 USED = 27
 SHARE = 48
-BLOCK = 216
 LANES = 128
 CHAN = 256
 OUTS = 32
@@ -65,10 +64,11 @@
     block_ref,
     sems,
 ):
+    near = weights_ref.at[:, pl.ds(row_ref[0] // 4 * 16, 16), :]
     copies = [
         pltpu.make_async_copy(source, target, sems.at[place])
         for place, (source, target) in enumerate(
-            ((features_ref, local_ref), (labels_ref, marks_ref), (weights_ref, taps_ref))
+            ((features_ref, local_ref), (labels_ref, marks_ref), (near, taps_ref))
         )
     ]
     for copy in copies:
@@ -94,15 +94,19 @@
     for send in sends:
         send.start()
     copies[2].wait()
-    for lanes in range(2):
-        wide_ref[lanes] = taps_ref[:, lanes * LANES : (lanes + 1) * LANES].astype(F32)
-    first = row_ref[0] * 4
+    for tap in range(TAPS):
+        for lanes in range(2):
+            wide_ref[lanes, tap * 16 : (tap + 1) * 16, :] = taps_ref[
+                tap, :, lanes * LANES : (lanes + 1) * LANES
+            ].astype(F32)
+    first = row_ref[0] % 4 * 4
     for slot in range(4):
         for lanes in range(2):
-            packed_ref[pl.ds(slot * 2 + lanes, TAPS, stride=8), :] = wide_ref[
-                lanes, pl.ds(first + slot, TAPS, stride=OUTS), :
+            packed_ref[lanes, pl.ds(slot, TAPS, stride=4), :] = wide_ref[
+                lanes, pl.ds(first + slot, TAPS, stride=16), :
             ]
-    mine_ref[...] = packed_ref[...].astype(BF16)
+    for lanes in range(2):
+        mine_ref[:, lanes * LANES : (lanes + 1) * LANES] = packed_ref[lanes].astype(BF16)
     for send in sends:
         send.wait()
 
@@ -116,16 +120,16 @@
         out_specs=[hbm, vmem],
         out_shape=[
             jax.ShapeDtypeStruct((ROWS, SENT, CHAN), BF16),
-            jax.ShapeDtypeStruct((BLOCK, LANES), BF16),
+            jax.ShapeDtypeStruct((4 * TAPS, CHAN), BF16),
         ],
         scratch_shapes=[
             pltpu.VMEM((SHARD, CHAN), BF16),
             pltpu.VMEM((6, 1, 72), jnp.int32),
-            pltpu.VMEM((TAPS * OUTS, CHAN), BF16),
+            pltpu.VMEM((TAPS, 16, CHAN), BF16),
             pltpu.VMEM((SHARD, CHAN), F32),
             pltpu.VMEM((SENT, CHAN), F32),
-            pltpu.VMEM((2, TAPS * OUTS, LANES), F32),
-            pltpu.VMEM((BLOCK, LANES), F32),
+            pltpu.VMEM((2, TAPS * 16, LANES), F32),
+            pltpu.VMEM((2, 4 * TAPS, LANES), F32),
             pltpu.VMEM((SENT, CHAN), BF16),
             pltpu.SemaphoreType.DMA((3 + ROWS,)),
         ],
@@ -262,7 +266,7 @@
 
 
 def gradient_kernel(
-    parity_ref, own_ref, other_ref, features_ref, out_ref, flat_ref, turned_ref, acc_ref, rows_ref
+    parity_ref, own_ref, other_ref, features_ref, out_ref, flat_ref, turned_ref, acc_ref
 ):
     own = parity_ref[0]
     flat_ref[:, HALF // 4 :, :] = jnp.zeros((3, LANES - UNIT, LANES), F32)
@@ -296,17 +300,8 @@
             )
             product = jnp.dot(grads, pixels, preferred_element_type=F32)
             for place, (tap, _, _) in enumerate(taps):
-                for lanes in range(2):
-                    acc_ref[lanes, tap * OUTS : (tap + 1) * OUTS, :] += product[
-                        place * OUTS : (place + 1) * OUTS, lanes * LANES : (lanes + 1) * LANES
-                    ]
-    for slot in range(OUTS):
-        for lanes in range(2):
-            rows_ref[pl.ds(slot // 4 * BLOCK + slot % 4 * 2 + lanes, TAPS, stride=8), :] = acc_ref[
-                lanes, pl.ds(slot, TAPS, stride=OUTS), :
-            ]
-    for sample in range(8):
-        out_ref[sample] = rows_ref[sample * BLOCK : (sample + 1) * BLOCK, :].astype(BF16)
+                acc_ref[tap * OUTS : (tap + 1) * OUTS, :] += product[place * OUTS : (place + 1) * OUTS, :]
+    out_ref[...] = acc_ref[...].astype(BF16)
 
 
 def gradient(parity, own, other, features):
@@ -315,12 +310,11 @@
         gradient_kernel,
         in_specs=[pl.BlockSpec(memory_space=pltpu.SMEM), whole, whole, whole],
         out_specs=whole,
-        out_shape=jax.ShapeDtypeStruct((8, BLOCK, LANES), BF16),
+        out_shape=jax.ShapeDtypeStruct((TAPS * OUTS, CHAN), BF16),
         scratch_shapes=[
             pltpu.VMEM((3, HALF // 4 + LANES - UNIT, LANES), F32),
             pltpu.VMEM((UNITS, 3 * OUTS, 2 * LANES), BF16),
-            pltpu.VMEM((2, TAPS * OUTS, LANES), F32),
-            pltpu.VMEM((8 * BLOCK, LANES), F32),
+            pltpu.VMEM((TAPS * OUTS, CHAN), F32),
         ],
         compiler_params=compiler_params(),
         cost_estimate=pl.CostEstimate(
@@ -330,32 +324,6 @@
     )(parity, own, other, features)
 
 
-def unshuffle_kernel(parts_ref, out_ref, packed_ref, rows_ref):
-    for block in range(8):
-        packed_ref[block * BLOCK : (block + 1) * BLOCK, :] = parts_ref[block].astype(F32)
-    for slot in range(OUTS):
-        for lanes in range(2):
-            rows_ref[lanes, pl.ds(slot, TAPS, stride=OUTS), :] = packed_ref[
-                pl.ds(slot // 4 * BLOCK + slot % 4 * 2 + lanes, TAPS, stride=8), :
-            ]
-    for lanes in range(2):
-        out_ref[:, lanes * LANES : (lanes + 1) * LANES] = rows_ref[lanes].astype(BF16)
-
-
-def unshuffle(parts):
-    return pl.pallas_call(
-        unshuffle_kernel,
-        out_shape=jax.ShapeDtypeStruct((TAPS * OUTS, CHAN), BF16),
-        scratch_shapes=[
-            pltpu.VMEM((8 * BLOCK, LANES), F32),
-            pltpu.VMEM((2, TAPS * OUTS, LANES), F32),
-        ],
-        compiler_params=compiler_params(),
-        cost_estimate=pl.CostEstimate(flops=0, bytes_accessed=1000000, transcendentals=0),
-        name="unshuffle",
-    )(parts)
-
-
 def shards(features, weights, proj, classify, labels):
     row = lax.axis_index("row")
     core = lax.axis_index("core")
@@ -366,10 +334,15 @@
         row.astype(jnp.int32).reshape(1),
         features.reshape(SHARD, CHAN),
         labels.transpose(1, 0, 2),
-        weights.transpose(1, 2, 0, 3).reshape(TAPS * OUTS, CHAN),
+        weights.transpose(1, 2, 0, 3).reshape(TAPS, OUTS, CHAN),
     )
     gathered = lax.all_to_all(sent, "row", 0, 0).reshape(GRID_J, 2, SENT, CHAN)
-    kernels = unshuffle(lax.all_gather(mine, "sample"))
+    mine = mine.reshape(TAPS, 4, CHAN)
+    theirs = lax.ppermute(mine, "zlo", swap)
+    even = lax.axis_index("zlo") == 0
+    pairs = jnp.stack([jnp.where(even, mine, theirs), jnp.where(even, theirs, mine)])
+    kernels = lax.all_gather(pairs, "zhi").reshape(8, TAPS, 4, CHAN)
+    kernels = kernels.transpose(1, 0, 2, 3).reshape(TAPS * OUTS, CHAN)
 
     mixing = proj.reshape(3, 8, ROWS, 4, CHAN).transpose(2, 0, 1, 3, 4).reshape(ROWS * 3 * OUTS, CHAN)
     heads = jnp.pad(classify, ((0, 0), (0, LANES - 3)))
@@ -392,20 +365,22 @@
     grads_own = lax.all_to_all(grads, ("yhi", "row"), 0, 0)
     grads_other = lax.ppermute(grads_own, "core", swap)
     partial = gradient(parity, grads_own, grads_other, gathered)
-    over_samples = lax.all_to_all(partial, "sample", 0, 0)
+    partial = partial.reshape(TAPS, 8, 4, CHAN).transpose(1, 0, 2, 3)
+    over_samples = lax.all_to_all(partial, ("zhi", "zlo"), 0, 0)
     summed = jnp.sum(over_samples.astype(F32), axis=0).astype(BF16)
-    final = lax.all_to_all(jnp.broadcast_to(summed[None], (ROWS, BLOCK, LANES)), "row", 0, 0)
-    return unshuffle(final).reshape(3, 9, 32, CHAN).transpose(2, 0, 1, 3)
+    final = lax.all_to_all(jnp.broadcast_to(summed[None], (ROWS, TAPS, 4, CHAN)), "row", 0, 0)
+    return final.transpose(0, 2, 1, 3).reshape(OUTS, 3, 9, CHAN)
 
 
 def solution(mesh):
-    split = Mesh(mesh.devices.reshape(8, 4, 2, 8), ("row", "yhi", "core", "sample"))
+    split = Mesh(mesh.devices.reshape(8, 4, 2, 4, 2), ("row", "yhi", "core", "zhi", "zlo"))
+    sample, channel = ("zhi", "zlo"), ("yhi", "core")
     in_specs = (
-        P("sample", "row", None, ("yhi", "core")),
-        P("sample", None, None, ("yhi", "core")),
+        P(sample, "row", None, channel),
+        P(sample, None, None, channel),
         P(),
         P(),
-        P("sample", "row", None),
+        P(sample, "row", None),
     )
-    out_specs = P("sample", None, None, ("yhi", "core"))
+    out_specs = P(sample, None, None, channel)
     return jax.shard_map(shards, mesh=split, in_specs=in_specs, out_specs=out_specs, check_vma=False)

time: 131 us -> 126 us (0.962)
  blocking collectives: 96.5 us -> 88.9 us
  Pallas kernels: 11.4 us -> 7.83 us
  starting transfers between devices: 18.7 us -> 21.2 us
  local copies, waits for them, and re-layouts: 0.93 us -> 2.47 us
    all_gather x1, blocking collectives: 27 us -> 18.7 us  [shards(): kernels = lax.all_gather(pairs, 'zhi').reshape(8, TAPS, 4, CHAN)]
    ppermute x0 -> x1, starting transfers between devices: none -> 4 us  [shards(): theirs = lax.ppermute(mine, 'zlo', swap)]
    pallas_call x2 -> x0, Pallas kernels: 2.89 us -> none  [unshuffle(): pl.pallas_call(unshuffle_kernel, out_shape=jax.ShapeDtypeStruct((TAPS * O...]
    ppermute x1, starting transfers between devices: 7.38 us -> 5.93 us  [shards(): received = lax.ppermute(other, 'core', swap)]
  transfers between devices with their start and end apart: 3 -> 4, of which waited for: 2 -> 3; matrix products, arithmetic and copies ran while one was open for 0% -> 1% of each run, Pallas kernels for 1% -> 0%
where the time goes in v5:
time: 126 us; the launch traced here: 125 us
  blocking collectives  88.9 us (71%)
  starting transfers between devices  21.2 us (17%)
  Pallas kernels  7.83 us (6%)
  waiting for transfers between devices  3.56 us (3%)
  local copies, waits for them, and re-layouts  2.47 us (2%)
    all_to_all x1, blocking collectives, shards(): parts = lax.all_to_all(pair, ('yhi', 'row'), 0, 0)  23.1 us
    all_to_all x1, blocking collectives, shards(): over_samples = lax.all_to_all(partial, ('zhi', 'zlo'), 0, 0)  19.3 us
    all_gather x1, blocking collectives, shards(): kernels = lax.all_gather(pairs, 'zhi').reshape(8, TAPS, 4, CHAN)  18.7 us
    all_to_all x1, blocking collectives, shards(): grads_own = lax.all_to_all(grads, ('yhi', 'row'), 0, 0)  17.6 us
    all_to_all x1, blocking collectives, shards(): lax.all_to_all(jnp.broadcast_to(summed[None], (ROWS, TAPS, 4, CHAN)), 'ro...  10.1 us
    all_to_all x1, starting transfers between devices, shards(): gathered = lax.all_to_all(sent, 'row', 0, 0).reshape(GRID_J, 2, SENT, CHAN)  6.01 us
    ppermute x1, starting transfers between devices, shards(): received = lax.ppermute(other, 'core', swap)  5.93 us
    ppermute x1, starting transfers between devices, shards(): grads_other = lax.ppermute(grads_own, 'core', swap)  5.3 us
  transfers between devices with their start and end apart: 4, of which 3 were waited for; matrix products, arithmetic and copies ran while one was open for 1% of the time, Pallas kernels for 0%

profile of v5, /device:TPU:1, one launch (start us, length us, event | category | flops | bytes accessed | tf_op | source)
XLA Modules:
  0.0 124.7 jit_solution(3625371707821988904)
XLA Ops:
  0.0 2.9 %prepare_blocks.1 = (bf16[8,440,256]{2,1,0:T(8,128)(2,1)}, bf16[108,256]{1,0:T(8,128)(2,1)}) custom-call(s32[1]{0:T(128)} %bitcast.1.row_ref, bf16[432,256]{1,0:T(8,128)(2,1)} %bitcast.34, s32[6,1,72]{2,1,0:T(1,128)} %bitcast.37, bf16[27,32,256]{2,1,0:T(8,128)(2,1)} %bitcast.33), custom_call_target="tpu_custom_call" | custom-call | bytes 1990656 | tf_op jit(solution)/shard_map/prepare_blocks/pallas_call | solution.py:117
  3.0 0.0 copy-start.1
  3.0 0.0 copy-start
  3.0 6.0 %all-to-all-start = ((bf16[8,440,256]{2,1,0:T(8,128)(2,1)}), bf16[8,440,256]{2,1,0:T(8,128)(2,1)S(1)}, u32[]{:S(2)}, u32[]{:S(2)}) async-start(bf16[8,440,256]{2,1,0:T(8,128)(2,1)} %get-tuple-element.14), calls=%async_computation | async-start | bytes 3604480 | tf_op jit(solution)/shard_map/all_to_all | solution.py:339
  9.0 0.0 copy-start.2
  9.0 0.0 copy-done.1
  9.0 4.0 %collective-permute-start = (bf16[27,4,256]{2,1,0:T(4,128)(2,1)S(1)}, bf16[27,4,256]{2,1,0:T(4,128)(2,1)S(1)}, u32[]{:S(2)}, u32[]{:S(2)}) collective-permute-start(bf16[27,4,256]{2,1,0:T(4,128)(2,1)S(1)} %reshape.51), channel_id=1, source_target_pairs={{0,1},{1,0},{2,3},{3,2},{4,5},{5,4},{6,7},{7,6},{8,9},{9,8},{10,11... | collective-permute-start | bytes 165896 | tf_op jit(solution)/shard_map/ppermute | solution.py:341
  13.0 0.0 copy-done
  13.0 0.1 reshape.54
  13.1 0.2 copy.27
  13.3 0.1 reshape.55.proj_ref
  13.4 0.0 copy-done.2
  13.5 0.1 copy.20
  13.7 0.9 collective-permute-done
  14.6 0.1 pad_maximum_fusion
  14.7 18.7 %all-gather = bf16[8,27,4,256]{3,2,0,1:T(4,128)(2,1)S(1)} all-gather(bf16[2,27,4,256]{3,2,0,1:T(4,128)(2,1)S(1)} %pad_maximum_fusion), channel_id=2, replica_groups=mesh['row'=8,'yhi'=4,'core'=2,'zhi'=4,'zlo'=2] {'zhi'}, dimensions={0}, use_global_device_ids=true | all-gather | bytes 552960 | tf_op jit(solution)/shard_map/all_gather | solution.py:344
  33.4 0.1 reshape.53.weights_ref
  33.6 0.0 all-to-all-done
  33.6 0.1 reshape.57
  33.7 0.1 pad_dynamic-slice_fusion
  33.8 0.1 eq.19
  33.9 0.1 compare_convert_fusion.onehot_ref
  34.0 2.1 %forward_taps.1 = (bf16[32,48,128]{2,1,0:T(8,128)(2,1)S(1)}, bf16[32,48,128]{2,1,0:T(8,128)(2,1)S(1)}) custom-call(s32[1]{0:T(128)} %bitcast.core_ref.parity_ref, bf16[4,2,440,256]{3,2,1,0:T(8,128)(2,1)S(1)} %bitcast.27, bf16[864,256]{1,0:T(8,128)(2,1)S(1)} %reshape.53.weights_ref), custom_call_target="tpu_custom_call" | custom-call | flops 1528823808 | bytes 4000000 | tf_op jit(solution)/shard_map/forward_taps/pallas_call | solution.py:184
  36.0 5.9 %collective-permute-start.1 = (bf16[32,48,128]{2,1,0:T(8,128)(2,1)S(1)}, bf16[32,48,128]{2,1,0:T(8,128)(2,1)S(1)}, u32[]{:S(2)}, u32[]{:S(2)}) collective-permute-start(bf16[32,48,128]{2,1,0:T(8,128)(2,1)S(1)} %get-tuple-element.18), channel_id=1, source_target_pairs={{0,8},{8,0},{1,9},{9,1},{2,10},{10,2},{3,11},{11,3},{4,12},{12,4},... | collective-permute-start | bytes 1179656 | tf_op jit(solution)/shard_map/ppermute | solution.py:360
  42.0 1.3 %collective-permute-done.1 = bf16[32,48,128]{2,1,0:T(8,128)(2,1)S(1)} collective-permute-done((bf16[32,48,128]{2,1,0:T(8,128)(2,1)S(1)}, bf16[32,48,128]{2,1,0:T(8,128)(2,1)S(1)}, u32[]{:S(2)}, u32[]{:S(2)}) %collective-permute-start.1) | collective-permute-done | bytes 393248 | tf_op jit(solution)/shard_map/ppermute | solution.py:360
  43.3 0.1 add_convert_fusion
  43.4 23.1 %all_to_all.25.parts_ref = bf16[32,48,128]{2,1,0:T(8,128)(2,1)S(1)} all-to-all(bf16[32,48,128]{2,1,0:T(8,128)(2,1)S(1)} %add_convert_fusion), channel_id=1, replica_groups=mesh['row'=8,'yhi'=4,'core'=2,'zhi'=4,'zlo'=2] {'yhi','row'}, dimensions={0} | all-to-all | bytes 786432 | tf_op jit(solution)/shard_map/all_to_all | solution.py:363
  66.5 1.1 tail.1
  67.6 17.6 %all_to_all.26.own_ref = bf16[32,48,128]{2,1,0:T(8,128)(2,1)S(1)} all-to-all(bf16[32,48,128]{2,1,0:T(8,128)(2,1)S(1)} %tail.1), channel_id=1, replica_groups=mesh['row'=8,'yhi'=4,'core'=2,'zhi'=4,'zlo'=2] {'yhi','row'}, dimensions={0} | all-to-all | bytes 786432 | tf_op jit(solution)/shard_map/all_to_all | solution.py:365
  85.2 5.3 %collective-permute-start.2 = (bf16[32,48,128]{2,1,0:T(8,128)(2,1)S(1)}, bf16[32,48,128]{2,1,0:T(8,128)(2,1)S(1)}, u32[]{:S(2)}, u32[]{:S(2)}) collective-permute-start(bf16[32,48,128]{2,1,0:T(8,128)(2,1)S(1)} %all_to_all.26.own_ref), channel_id=1, source_target_pairs={{0,8},{8,0},{1,9},{9,1},{2,10},{10,2},{3,11},{11,3},{4,12},{12,4},... | collective-permute-start | bytes 1179656 | tf_op jit(solution)/shard_map/ppermute | solution.py:366
  90.5 1.3 %collective-permute-done.2.other_ref = bf16[32,48,128]{2,1,0:T(8,128)(2,1)S(1)} collective-permute-done((bf16[32,48,128]{2,1,0:T(8,128)(2,1)S(1)}, bf16[32,48,128]{2,1,0:T(8,128)(2,1)S(1)}, u32[]{:S(2)}, u32[]{:S(2)}) %collective-permute-start.2) | collective-permute-done | bytes 393248 | tf_op jit(solution)/shard_map/ppermute | solution.py:366
  91.8 1.8 %gradient_taps.1 = bf16[864,256]{1,0:T(8,128)(2,1)S(1)} custom-call(s32[1]{0:T(128)} %bitcast.core_ref.parity_ref, bf16[32,48,128]{2,1,0:T(8,128)(2,1)S(1)} %all_to_all.26.own_ref, bf16[32,48,128]{2,1,0:T(8,128)(2,1)S(1)} %collective-permute-done.2.other_ref, bf16[4,2,440,256]{3,2,1,0:T(8,128)(2,1)S(1)} %bitcast.28), custom_call_target="tpu_custom_call" | custom-call | flops 1528823808 | bytes 4000000 | tf_op jit(solution)/shard_map/gradient_taps/pallas_call | solution.py:309
  93.6 0.1 reshape.58
  93.7 0.2 copy.26
  93.9 19.3 %all_to_all.27 = bf16[8,27,4,256]{3,2,1,0:T(4,128)(2,1)S(1)} all-to-all(bf16[8,27,4,256]{3,2,1,0:T(4,128)(2,1)S(1)} %bitcast.29), channel_id=1, replica_groups=mesh['row'=8,'yhi'=4,'core'=2,'zhi'=4,'zlo'=2] {'zhi','zlo'}, dimensions={0} | all-to-all | bytes 884736 | tf_op jit(solution)/shard_map/all_to_all | solution.py:369
  113.2 0.2 reduce_sum.12
  113.4 0.1 broadcast_in_dim.2
  113.5 10.1 %all_to_all.28 = bf16[8,27,4,256]{3,2,1,0:T(4,128)(2,1)S(1)} all-to-all(bf16[8,27,4,256]{3,2,1,0:T(4,128)(2,1)S(1)} %broadcast_in_dim.2), channel_id=1, replica_groups=mesh['row'=8,'yhi'=4,'core'=2,'zhi'=4,'zlo'=2] {'row'}, dimensions={0} | all-to-all | bytes 884736 | tf_op jit(solution)/shard_map/all_to_all | solution.py:371
  123.6 0.2 copy.23
  123.8 0.9 reshape.59
  (8 shorter events, 0.1 us)
Async XLA Ops:
  3.0 6.0 %copy-start.1 = (bf16[108,256]{1,0:T(8,128)(2,1)S(1)}, bf16[108,256]{1,0:T(8,128)(2,1)}, u32[]{:S(2)}) copy-start(bf16[108,256]{1,0:T(8,128)(2,1)} %get-tuple-element.15) | copy-start | bytes 165892
  3.0 10.1 %copy-start = (bf16[768,256]{1,0:T(8,128)(2,1)S(1)}, bf16[768,256]{1,0:T(8,128)(2,1)}, u32[]{:S(2)}) copy-start(bf16[768,256]{1,0:T(8,128)(2,1)} %param.7) | copy-start | bytes 1179652
  3.0 30.6 %all-to-all-start = ((bf16[8,440,256]{2,1,0:T(8,128)(2,1)}), bf16[8,440,256]{2,1,0:T(8,128)(2,1)S(1)}, u32[]{:S(2)}, u32[]{:S(2)}) async-start(bf16[8,440,256]{2,1,0:T(8,128)(2,1)} %get-tuple-element.14), calls=%async_computation | async-start | bytes 3604480 | tf_op jit(solution)/shard_map/all_to_all | solution.py:339
  9.0 4.5 %copy-start.2 = (bf16[256,3]{0,1:T(4,128)(2,1)S(1)}, bf16[256,3]{0,1:T(4,128)(2,1)}, u32[]{:S(2)}) copy-start(bf16[256,3]{0,1:T(4,128)(2,1)} %param.8) | copy-start | bytes 4612
  9.0 5.5 %collective-permute-start = (bf16[27,4,256]{2,1,0:T(4,128)(2,1)S(1)}, bf16[27,4,256]{2,1,0:T(4,128)(2,1)S(1)}, u32[]{:S(2)}, u32[]{:S(2)}) collective-permute-start(bf16[27,4,256]{2,1,0:T(4,128)(2,1)S(1)} %reshape.51), channel_id=1, source_target_pairs={{0,1},{1,0},{2,3},{3,2},{4,5},{5,4},{6,7},{7,6},{8,9},{9,8},{10,11... | collective-permute-start | bytes 165896 | tf_op jit(solution)/shard_map/ppermute | solution.py:341
  36.0 7.3 %collective-permute-start.1 = (bf16[32,48,128]{2,1,0:T(8,128)(2,1)S(1)}, bf16[32,48,128]{2,1,0:T(8,128)(2,1)S(1)}, u32[]{:S(2)}, u32[]{:S(2)}) collective-permute-start(bf16[32,48,128]{2,1,0:T(8,128)(2,1)S(1)} %get-tuple-element.18), channel_id=1, source_target_pairs={{0,8},{8,0},{1,9},{9,1},{2,10},{10,2},{3,11},{11,3},{4,12},{12,4},... | collective-permute-start | bytes 1179656 | tf_op jit(solution)/shard_map/ppermute | solution.py:360
  85.2 6.6 %collective-permute-start.2 = (bf16[32,48,128]{2,1,0:T(8,128)(2,1)S(1)}, bf16[32,48,128]{2,1,0:T(8,128)(2,1)S(1)}, u32[]{:S(2)}, u32[]{:S(2)}) collective-permute-start(bf16[32,48,128]{2,1,0:T(8,128)(2,1)S(1)} %all_to_all.26.own_ref), channel_id=1, source_target_pairs={{0,8},{8,0},{1,9},{9,1},{2,10},{10,2},{3,11},{11,3},{4,12},{12,4},... | collective-permute-start | bytes 1179656 | tf_op jit(solution)/shard_map/ppermute | solution.py:366

commit v6 on v5

--- a/solution.py
+++ b/solution.py
@@ -15,7 +15,7 @@
 UNITS = GRID_J * GRID_Q
 HALF = UNITS * UNIT
 SHARD = 432
-SENT = 440
+SENT = 448
 PARTS = 32
 USED = 27
 SHARE = 48
@@ -139,12 +139,13 @@
     )(row, features, labels, weights)
 
 
-def unit_rows(q):
-    return slice(q * UNIT, (q + 1) * UNIT)
+def unit(features_ref, j, parity, q):
+    pair = features_ref[j, parity, q // 2 * 2 * UNIT : (q // 2 + 1) * 2 * UNIT, :]
+    return pair[q % 2 * UNIT : (q % 2 + 1) * UNIT, :]
 
 
 def forward_kernel(core_ref, features_ref, weights_ref, own_ref, other_ref, acc_ref, flat_ref):
-    acc_ref[...] = jnp.zeros(acc_ref.shape, F32)
+    written = set()
     for j in range(GRID_J):
         for q in range(GRID_Q):
             taps = block_taps(j, q)
@@ -152,16 +153,16 @@
                 [weights_ref[tap * OUTS : (tap + 1) * OUTS, :] for tap, _, _ in taps], axis=0
             )
             pixels = jnp.concatenate(
-                [features_ref[j, 0, unit_rows(q), :], features_ref[j, 1, unit_rows(q), :]], axis=0
+                [unit(features_ref, j, 0, q), unit(features_ref, j, 1, q)], axis=0
             )
             product = lax.dot_general(
                 kernels, pixels, (((1,), (1,)), ((), ())), preferred_element_type=F32
             )
             for place, (_, branch, block) in enumerate(taps):
-                lane = block % 4 * OUTS
-                acc_ref[block // 4, branch, lane : lane + OUTS, : 2 * UNIT] += product[
-                    place * OUTS : (place + 1) * OUTS, :
-                ]
+                at = (block // 4, branch, slice(block % 4 * OUTS, (block % 4 + 1) * OUTS), slice(2 * UNIT))
+                term = product[place * OUTS : (place + 1) * OUTS, :]
+                acc_ref[at] = acc_ref[at] + term if (branch, block) in written else term
+                written.add((branch, block))
     for group in range(UNITS // 4):
         for branch in range(3):
             turned = jnp.transpose(acc_ref[group, branch])
@@ -285,7 +286,7 @@
                         branch * OUTS : (branch + 1) * OUTS,
                         half * LANES : (half + 1) * LANES,
                     ] = turned[place * OUTS : (place + 1) * OUTS, :]
-    acc_ref[...] = jnp.zeros(acc_ref.shape, F32)
+    written = set()
     gap = jnp.zeros((LANES - UNIT, CHAN), BF16)
     for j in range(GRID_J):
         for q in range(GRID_Q):
@@ -295,12 +296,14 @@
                 axis=0,
             )
             pixels = jnp.concatenate(
-                [features_ref[j, own, unit_rows(q), :], gap, features_ref[j, 1 - own, unit_rows(q), :], gap],
-                axis=0,
+                [unit(features_ref, j, own, q), gap, unit(features_ref, j, 1 - own, q), gap], axis=0
             )
             product = jnp.dot(grads, pixels, preferred_element_type=F32)
             for place, (tap, _, _) in enumerate(taps):
-                acc_ref[tap * OUTS : (tap + 1) * OUTS, :] += product[place * OUTS : (place + 1) * OUTS, :]
+                at = slice(tap * OUTS, (tap + 1) * OUTS)
+                term = product[place * OUTS : (place + 1) * OUTS, :]
+                acc_ref[at, :] = acc_ref[at, :] + term if tap in written else term
+                written.add(tap)
     out_ref[...] = acc_ref[...].astype(BF16)
 
 

time: 126 us -> 126 us (level)
  no operation moved by 1% of the time
where the time goes in v6:
time: 126 us; the launch traced here: 125 us
  blocking collectives  88.8 us (70%)
  starting transfers between devices  21.2 us (17%)
  Pallas kernels  7.81 us (6%)
  waiting for transfers between devices  3.56 us (3%)
  local copies, waits for them, and re-layouts  2.47 us (2%)
    all_to_all x1, blocking collectives, shards(): parts = lax.all_to_all(pair, ('yhi', 'row'), 0, 0)  23.1 us
    all_to_all x1, blocking collectives, shards(): over_samples = lax.all_to_all(partial, ('zhi', 'zlo'), 0, 0)  19.3 us
    all_gather x1, blocking collectives, shards(): kernels = lax.all_gather(pairs, 'zhi').reshape(8, TAPS, 4, CHAN)  18.7 us
    all_to_all x1, blocking collectives, shards(): grads_own = lax.all_to_all(grads, ('yhi', 'row'), 0, 0)  17.6 us
    all_to_all x1, blocking collectives, shards(): lax.all_to_all(jnp.broadcast_to(summed[None], (ROWS, TAPS, 4, CHAN)), 'ro...  10.1 us
    all_to_all x1, starting transfers between devices, shards(): gathered = lax.all_to_all(sent, 'row', 0, 0).reshape(GRID_J, 2, SENT, CHAN)  6.01 us
    ppermute x1, starting transfers between devices, shards(): received = lax.ppermute(other, 'core', swap)  5.93 us
    ppermute x1, starting transfers between devices, shards(): grads_other = lax.ppermute(grads_own, 'core', swap)  5.3 us
  transfers between devices with their start and end apart: 4, of which 3 were waited for; matrix products, arithmetic and copies ran while one was open for 1% of the time, Pallas kernels for 0%

profile of v6, /device:TPU:1, one launch (start us, length us, event | category | flops | bytes accessed | tf_op | source)
XLA Modules:
  0.0 124.6 jit_solution(1391660937418955718)
XLA Ops:
  0.0 2.9 %prepare_blocks.1 = (bf16[8,448,256]{2,1,0:T(8,128)(2,1)}, bf16[108,256]{1,0:T(8,128)(2,1)}) custom-call(s32[1]{0:T(128)} %bitcast.1.row_ref, bf16[432,256]{1,0:T(8,128)(2,1)} %bitcast.34, s32[6,1,72]{2,1,0:T(1,128)} %bitcast.37, bf16[27,32,256]{2,1,0:T(8,128)(2,1)} %bitcast.33), custom_call_target="tpu_custom_call" | custom-call | bytes 1990656 | tf_op jit(solution)/shard_map/prepare_blocks/pallas_call | solution.py:117
  3.0 0.0 copy-start.1
  3.0 0.0 copy-start
  3.0 6.0 %all-to-all-start = ((bf16[8,448,256]{2,1,0:T(8,128)(2,1)}), bf16[8,448,256]{2,1,0:T(8,128)(2,1)S(1)}, u32[]{:S(2)}, u32[]{:S(2)}) async-start(bf16[8,448,256]{2,1,0:T(8,128)(2,1)} %get-tuple-element.14), calls=%async_computation | async-start | bytes 3670016 | tf_op jit(solution)/shard_map/all_to_all | solution.py:342
  9.0 0.0 copy-start.2
  9.0 0.0 copy-done.1
  9.0 4.0 %collective-permute-start = (bf16[27,4,256]{2,1,0:T(4,128)(2,1)S(1)}, bf16[27,4,256]{2,1,0:T(4,128)(2,1)S(1)}, u32[]{:S(2)}, u32[]{:S(2)}) collective-permute-start(bf16[27,4,256]{2,1,0:T(4,128)(2,1)S(1)} %reshape.51), channel_id=1, source_target_pairs={{0,1},{1,0},{2,3},{3,2},{4,5},{5,4},{6,7},{7,6},{8,9},{9,8},{10,11... | collective-permute-start | bytes 165896 | tf_op jit(solution)/shard_map/ppermute | solution.py:344
  13.0 0.0 copy-done
  13.0 0.1 reshape.54
  13.1 0.2 copy.27
  13.3 0.1 reshape.55.proj_ref
  13.4 0.0 copy-done.2
  13.5 0.1 copy.20
  13.7 0.9 collective-permute-done
  14.6 0.1 pad_maximum_fusion
  14.7 18.7 %all-gather = bf16[8,27,4,256]{3,2,0,1:T(4,128)(2,1)S(1)} all-gather(bf16[2,27,4,256]{3,2,0,1:T(4,128)(2,1)S(1)} %pad_maximum_fusion), channel_id=2, replica_groups=mesh['row'=8,'yhi'=4,'core'=2,'zhi'=4,'zlo'=2] {'zhi'}, dimensions={0}, use_global_device_ids=true | all-gather | bytes 552960 | tf_op jit(solution)/shard_map/all_gather | solution.py:347
  33.4 0.1 reshape.53.weights_ref
  33.6 0.0 all-to-all-done
  33.6 0.1 reshape.57
  33.7 0.1 pad_dynamic-slice_fusion
  33.8 0.1 eq.19
  33.9 0.1 compare_convert_fusion.onehot_ref
  34.0 2.0 %forward_taps.1 = (bf16[32,48,128]{2,1,0:T(8,128)(2,1)S(1)}, bf16[32,48,128]{2,1,0:T(8,128)(2,1)S(1)}) custom-call(s32[1]{0:T(128)} %bitcast.core_ref.parity_ref, bf16[4,2,448,256]{3,2,1,0:T(8,128)(2,1)S(1)} %bitcast.27, bf16[864,256]{1,0:T(8,128)(2,1)S(1)} %reshape.53.weights_ref), custom_call_target="tpu_custom_call" | custom-call | flops 1528823808 | bytes 4000000 | tf_op jit(solution)/shard_map/forward_taps/pallas_call | solution.py:185
  36.0 5.9 %collective-permute-start.1 = (bf16[32,48,128]{2,1,0:T(8,128)(2,1)S(1)}, bf16[32,48,128]{2,1,0:T(8,128)(2,1)S(1)}, u32[]{:S(2)}, u32[]{:S(2)}) collective-permute-start(bf16[32,48,128]{2,1,0:T(8,128)(2,1)S(1)} %get-tuple-element.18), channel_id=1, source_target_pairs={{0,8},{8,0},{1,9},{9,1},{2,10},{10,2},{3,11},{11,3},{4,12},{12,4},... | collective-permute-start | bytes 1179656 | tf_op jit(solution)/shard_map/ppermute | solution.py:363
  42.0 1.3 %collective-permute-done.1 = bf16[32,48,128]{2,1,0:T(8,128)(2,1)S(1)} collective-permute-done((bf16[32,48,128]{2,1,0:T(8,128)(2,1)S(1)}, bf16[32,48,128]{2,1,0:T(8,128)(2,1)S(1)}, u32[]{:S(2)}, u32[]{:S(2)}) %collective-permute-start.1) | collective-permute-done | bytes 393248 | tf_op jit(solution)/shard_map/ppermute | solution.py:363
  43.3 0.1 add_convert_fusion
  43.4 23.1 %all_to_all.25.parts_ref = bf16[32,48,128]{2,1,0:T(8,128)(2,1)S(1)} all-to-all(bf16[32,48,128]{2,1,0:T(8,128)(2,1)S(1)} %add_convert_fusion), channel_id=1, replica_groups=mesh['row'=8,'yhi'=4,'core'=2,'zhi'=4,'zlo'=2] {'yhi','row'}, dimensions={0} | all-to-all | bytes 786432 | tf_op jit(solution)/shard_map/all_to_all | solution.py:366
  66.5 1.1 tail.1
  67.5 17.6 %all_to_all.26.own_ref = bf16[32,48,128]{2,1,0:T(8,128)(2,1)S(1)} all-to-all(bf16[32,48,128]{2,1,0:T(8,128)(2,1)S(1)} %tail.1), channel_id=1, replica_groups=mesh['row'=8,'yhi'=4,'core'=2,'zhi'=4,'zlo'=2] {'yhi','row'}, dimensions={0} | all-to-all | bytes 786432 | tf_op jit(solution)/shard_map/all_to_all | solution.py:368
  85.2 5.3 %collective-permute-start.2 = (bf16[32,48,128]{2,1,0:T(8,128)(2,1)S(1)}, bf16[32,48,128]{2,1,0:T(8,128)(2,1)S(1)}, u32[]{:S(2)}, u32[]{:S(2)}) collective-permute-start(bf16[32,48,128]{2,1,0:T(8,128)(2,1)S(1)} %all_to_all.26.own_ref), channel_id=1, source_target_pairs={{0,8},{8,0},{1,9},{9,1},{2,10},{10,2},{3,11},{11,3},{4,12},{12,4},... | collective-permute-start | bytes 1179656 | tf_op jit(solution)/shard_map/ppermute | solution.py:369
  90.5 1.3 %collective-permute-done.2.other_ref = bf16[32,48,128]{2,1,0:T(8,128)(2,1)S(1)} collective-permute-done((bf16[32,48,128]{2,1,0:T(8,128)(2,1)S(1)}, bf16[32,48,128]{2,1,0:T(8,128)(2,1)S(1)}, u32[]{:S(2)}, u32[]{:S(2)}) %collective-permute-start.2) | collective-permute-done | bytes 393248 | tf_op jit(solution)/shard_map/ppermute | solution.py:369
  91.8 1.8 %gradient_taps.1 = bf16[864,256]{1,0:T(8,128)(2,1)S(1)} custom-call(s32[1]{0:T(128)} %bitcast.core_ref.parity_ref, bf16[32,48,128]{2,1,0:T(8,128)(2,1)S(1)} %all_to_all.26.own_ref, bf16[32,48,128]{2,1,0:T(8,128)(2,1)S(1)} %collective-permute-done.2.other_ref, bf16[4,2,448,256]{3,2,1,0:T(8,128)(2,1)S(1)} %bitcast.28), custom_call_target="tpu_custom_call" | custom-call | flops 1528823808 | bytes 4000000 | tf_op jit(solution)/shard_map/gradient_taps/pallas_call | solution.py:312
  93.6 0.1 reshape.58
  93.7 0.2 copy.26
  93.8 19.3 %all_to_all.27 = bf16[8,27,4,256]{3,2,1,0:T(4,128)(2,1)S(1)} all-to-all(bf16[8,27,4,256]{3,2,1,0:T(4,128)(2,1)S(1)} %bitcast.29), channel_id=1, replica_groups=mesh['row'=8,'yhi'=4,'core'=2,'zhi'=4,'zlo'=2] {'zhi','zlo'}, dimensions={0} | all-to-all | bytes 884736 | tf_op jit(solution)/shard_map/all_to_all | solution.py:372
  113.1 0.2 reduce_sum.12
  113.3 0.1 broadcast_in_dim.2
  113.5 10.1 %all_to_all.28 = bf16[8,27,4,256]{3,2,1,0:T(4,128)(2,1)S(1)} all-to-all(bf16[8,27,4,256]{3,2,1,0:T(4,128)(2,1)S(1)} %broadcast_in_dim.2), channel_id=1, replica_groups=mesh['row'=8,'yhi'=4,'core'=2,'zhi'=4,'zlo'=2] {'row'}, dimensions={0} | all-to-all | bytes 884736 | tf_op jit(solution)/shard_map/all_to_all | solution.py:374
  123.5 0.2 copy.23
  123.8 0.9 reshape.59
  (8 shorter events, 0.1 us)
Async XLA Ops:
  3.0 6.0 %copy-start.1 = (bf16[108,256]{1,0:T(8,128)(2,1)S(1)}, bf16[108,256]{1,0:T(8,128)(2,1)}, u32[]{:S(2)}) copy-start(bf16[108,256]{1,0:T(8,128)(2,1)} %get-tuple-element.15) | copy-start | bytes 165892
  3.0 10.1 %copy-start = (bf16[768,256]{1,0:T(8,128)(2,1)S(1)}, bf16[768,256]{1,0:T(8,128)(2,1)}, u32[]{:S(2)}) copy-start(bf16[768,256]{1,0:T(8,128)(2,1)} %param.7) | copy-start | bytes 1179652
  3.0 30.6 %all-to-all-start = ((bf16[8,448,256]{2,1,0:T(8,128)(2,1)}), bf16[8,448,256]{2,1,0:T(8,128)(2,1)S(1)}, u32[]{:S(2)}, u32[]{:S(2)}) async-start(bf16[8,448,256]{2,1,0:T(8,128)(2,1)} %get-tuple-element.14), calls=%async_computation | async-start | bytes 3670016 | tf_op jit(solution)/shard_map/all_to_all | solution.py:342
  9.0 4.5 %copy-start.2 = (bf16[256,3]{0,1:T(4,128)(2,1)S(1)}, bf16[256,3]{0,1:T(4,128)(2,1)}, u32[]{:S(2)}) copy-start(bf16[256,3]{0,1:T(4,128)(2,1)} %param.8) | copy-start | bytes 4612
  9.0 5.5 %collective-permute-start = (bf16[27,4,256]{2,1,0:T(4,128)(2,1)S(1)}, bf16[27,4,256]{2,1,0:T(4,128)(2,1)S(1)}, u32[]{:S(2)}, u32[]{:S(2)}) collective-permute-start(bf16[27,4,256]{2,1,0:T(4,128)(2,1)S(1)} %reshape.51), channel_id=1, source_target_pairs={{0,1},{1,0},{2,3},{3,2},{4,5},{5,4},{6,7},{7,6},{8,9},{9,8},{10,11... | collective-permute-start | bytes 165896 | tf_op jit(solution)/shard_map/ppermute | solution.py:344
  36.0 7.3 %collective-permute-start.1 = (bf16[32,48,128]{2,1,0:T(8,128)(2,1)S(1)}, bf16[32,48,128]{2,1,0:T(8,128)(2,1)S(1)}, u32[]{:S(2)}, u32[]{:S(2)}) collective-permute-start(bf16[32,48,128]{2,1,0:T(8,128)(2,1)S(1)} %get-tuple-element.18), channel_id=1, source_target_pairs={{0,8},{8,0},{1,9},{9,1},{2,10},{10,2},{3,11},{11,3},{4,12},{12,4},... | collective-permute-start | bytes 1179656 | tf_op jit(solution)/shard_map/ppermute | solution.py:363
  85.2 6.6 %collective-permute-start.2 = (bf16[32,48,128]{2,1,0:T(8,128)(2,1)S(1)}, bf16[32,48,128]{2,1,0:T(8,128)(2,1)S(1)}, u32[]{:S(2)}, u32[]{:S(2)}) collective-permute-start(bf16[32,48,128]{2,1,0:T(8,128)(2,1)S(1)} %all_to_all.26.own_ref), channel_id=1, source_target_pairs={{0,8},{8,0},{1,9},{9,1},{2,10},{10,2},{3,11},{11,3},{4,12},{12,4},... | collective-permute-start | bytes 1179656 | tf_op jit(solution)/shard_map/ppermute | solution.py:369

commit v7 on v6

--- a/solution.py
+++ b/solution.py
@@ -23,6 +23,7 @@
 CHAN = 256
 OUTS = 32
 TAPS = 27
+KEPT = 112
 ROW_AXES = ("row",)
 VMEM_LIMIT = 16 * 1024 * 1024
 
@@ -59,9 +60,8 @@
     taps_ref,
     rows_ref,
     units_ref,
-    wide_ref,
-    packed_ref,
     block_ref,
+    kept_ref,
     sems,
 ):
     near = weights_ref.at[:, pl.ds(row_ref[0] // 4 * 16, 16), :]
@@ -71,7 +71,7 @@
             ((features_ref, local_ref), (labels_ref, marks_ref), (near, taps_ref))
         )
     ]
-    for copy in copies:
+    for copy in (copies[2], copies[0], copies[1]):
         copy.start()
     units_ref[SHARD:, :] = jnp.zeros((SENT - SHARD, CHAN), F32)
     copies[1].wait()
@@ -94,33 +94,27 @@
     for send in sends:
         send.start()
     copies[2].wait()
-    for tap in range(TAPS):
-        for lanes in range(2):
-            wide_ref[lanes, tap * 16 : (tap + 1) * 16, :] = taps_ref[
-                tap, :, lanes * LANES : (lanes + 1) * LANES
-            ].astype(F32)
-    first = row_ref[0] % 4 * 4
-    for slot in range(4):
-        for lanes in range(2):
-            packed_ref[lanes, pl.ds(slot, TAPS, stride=4), :] = wide_ref[
-                lanes, pl.ds(first + slot, TAPS, stride=16), :
-            ]
-    for lanes in range(2):
-        mine_ref[:, lanes * LANES : (lanes + 1) * LANES] = packed_ref[lanes].astype(BF16)
+    picked = lax.broadcasted_iota(jnp.int32, (KEPT, 16 * TAPS), 0)
+    column = lax.broadcasted_iota(jnp.int32, (KEPT, 16 * TAPS), 1)
+    wanted = picked // 4 * 16 + picked % 4 + row_ref[0] % 4 * 4
+    picks = jnp.where(column == wanted, 1.0, 0.0).astype(BF16)
+    near_rows = taps_ref[...].reshape(16 * TAPS, CHAN)
+    kept_ref[...] = jnp.dot(picks, near_rows, preferred_element_type=F32).astype(BF16)
+    sends.append(pltpu.make_async_copy(kept_ref, mine_ref, sems.at[3 + ROWS]))
+    sends[-1].start()
     for send in sends:
         send.wait()
 
 
 def prepare(row, features, labels, weights):
     hbm = pl.BlockSpec(memory_space=pl.ANY)
-    vmem = pl.BlockSpec(memory_space=pltpu.VMEM)
     return pl.pallas_call(
         prepare_kernel,
         in_specs=[pl.BlockSpec(memory_space=pltpu.SMEM), hbm, hbm, hbm],
-        out_specs=[hbm, vmem],
+        out_specs=[hbm, hbm],
         out_shape=[
             jax.ShapeDtypeStruct((ROWS, SENT, CHAN), BF16),
-            jax.ShapeDtypeStruct((4 * TAPS, CHAN), BF16),
+            jax.ShapeDtypeStruct((KEPT, CHAN), BF16),
         ],
         scratch_shapes=[
             pltpu.VMEM((SHARD, CHAN), BF16),
@@ -128,10 +122,9 @@
             pltpu.VMEM((TAPS, 16, CHAN), BF16),
             pltpu.VMEM((SHARD, CHAN), F32),
             pltpu.VMEM((SENT, CHAN), F32),
-            pltpu.VMEM((2, TAPS * 16, LANES), F32),
-            pltpu.VMEM((2, 4 * TAPS, LANES), F32),
             pltpu.VMEM((SENT, CHAN), BF16),
-            pltpu.SemaphoreType.DMA((3 + ROWS,)),
+            pltpu.VMEM((KEPT, CHAN), BF16),
+            pltpu.SemaphoreType.DMA((4 + ROWS,)),
         ],
         compiler_params=compiler_params(60 * 1024 * 1024),
         cost_estimate=pl.CostEstimate(flops=0, bytes_accessed=2 * 9 * SHARD * CHAN, transcendentals=0),
@@ -207,7 +200,24 @@
     return gate_value * (1.0 + values * (1.0 - gate_value))
 
 
-def tail_kernel(parts_ref, proj_ref, classify_ref, classify_t_ref, onehot_ref, out_ref, act_ref, packed_ref):
+def own_labels(part, marks):
+    first = part * 16
+    group = first // UNIT
+    pixel = lax.broadcasted_iota(jnp.int32, (64, UNITS), 0)
+    spot = first - group * UNIT + pixel % 16
+    units = (group + jnp.where(spot >= UNIT, 1, 0)) * 4 + pixel // 16
+    chosen = (units == lax.broadcasted_iota(jnp.int32, (64, UNITS), 1)).astype(BF16)
+    rows = jnp.dot(chosen, marks, preferred_element_type=F32)
+    pixel = lax.broadcasted_iota(jnp.int32, (64, UNIT), 0)
+    spot = first - group * UNIT + pixel % 16
+    spot = jnp.where(spot >= UNIT, spot - UNIT, spot)
+    here = lax.broadcasted_iota(jnp.int32, (64, UNIT), 1) == spot
+    return jnp.sum(jnp.where(here, rows, 0.0), axis=1, keepdims=True)
+
+
+def tail_kernel(
+    part_ref, parts_ref, proj_ref, classify_ref, classify_t_ref, marks_ref, out_ref, act_ref, packed_ref
+):
     pieces = [(row, branch, place) for row in range(ROWS) for branch in range(3) for place in range(4)]
 
     def packed_at(branch, place):
@@ -235,7 +245,8 @@
     lane = lax.broadcasted_iota(jnp.int32, logits.shape, 1)
     exp_logits = jnp.where(lane < 3, jnp.exp(logits), 0.0)
     probabilities = exp_logits / jnp.sum(exp_logits, axis=1, keepdims=True)
-    dlogits = (probabilities - onehot_ref[...]).astype(BF16)
+    onehot = jnp.where(lane.astype(F32) == own_labels(part_ref[0], marks_ref[...]), 1.0, 0.0)
+    dlogits = (probabilities - onehot).astype(BF16)
     grad_hidden = jnp.dot(dlogits, classify_t_ref[...], preferred_element_type=F32)
     grad_mixed = (grad_hidden * swish_grad(mixed_pre, mixed_gate)).astype(BF16)
     act_ref[...] = lax.dot_general(
@@ -250,9 +261,12 @@
             out_ref[part * ROWS + row] = block
 
 
-def tail(parts, proj, classify, classify_t, onehot):
+def tail(part, parts, proj, classify, classify_t, marks):
+    whole = pl.BlockSpec(memory_space=pltpu.VMEM)
     return pl.pallas_call(
         tail_kernel,
+        in_specs=[pl.BlockSpec(memory_space=pltpu.SMEM)] + [whole] * 5,
+        out_specs=whole,
         out_shape=jax.ShapeDtypeStruct((PARTS, SHARE, LANES), BF16),
         scratch_shapes=[
             pltpu.VMEM((64, ROWS * 3 * OUTS), F32),
@@ -263,7 +277,7 @@
             flops=4 * 64 * 768 * CHAN, bytes_accessed=1500000, transcendentals=64 * 2000
         ),
         name="tail",
-    )(parts, proj, classify, classify_t, onehot)
+    )(part, parts, proj, classify, classify_t, marks)
 
 
 def gradient_kernel(
@@ -340,7 +354,7 @@
         weights.transpose(1, 2, 0, 3).reshape(TAPS, OUTS, CHAN),
     )
     gathered = lax.all_to_all(sent, "row", 0, 0).reshape(GRID_J, 2, SENT, CHAN)
-    mine = mine.reshape(TAPS, 4, CHAN)
+    mine = mine[: 4 * TAPS].reshape(TAPS, 4, CHAN)
     theirs = lax.ppermute(mine, "zlo", swap)
     even = lax.axis_index("zlo") == 0
     pairs = jnp.stack([jnp.where(even, mine, theirs), jnp.where(even, theirs, mine)])
@@ -351,11 +365,10 @@
     heads = jnp.pad(classify, ((0, 0), (0, LANES - 3)))
     heads_t = jnp.pad(classify.T, ((0, LANES - 3), (0, 0)))
     marks = lax.dynamic_index_in_dim(gathered[:, :, SHARD : SHARD + GRID_Q, :UNIT], core, 1, keepdims=False)
-    marks = marks.reshape(UNITS // 4, 4, UNIT).transpose(1, 0, 2).reshape(4, HALF // 4)
-    marks = lax.dynamic_slice_in_dim(jnp.pad(marks, ((0, 0), (0, (PARTS - USED) * 16))), part * 16, 16, 1)
-    onehot = (marks.reshape(64, 1) == jnp.arange(LANES, dtype=BF16)[None, :]).astype(F32)
-    kernels, mixing, heads, heads_t, onehot = lax.optimization_barrier(
-        (kernels, mixing, heads, heads_t, onehot)
+    marks = marks.reshape(UNITS, UNIT)
+    part = part.astype(jnp.int32).reshape(1)
+    kernels, mixing, heads, heads_t, marks, part = lax.optimization_barrier(
+        (kernels, mixing, heads, heads_t, marks, part)
     )
 
     parity = core.astype(jnp.int32).reshape(1)
@@ -364,7 +377,7 @@
     pair = (own.astype(F32) + received.astype(F32)).astype(BF16)
 
     parts = lax.all_to_all(pair, ("yhi", "row"), 0, 0)
-    grads = tail(parts, mixing, heads, heads_t, onehot)
+    grads = tail(part, parts, mixing, heads, heads_t, marks)
     grads_own = lax.all_to_all(grads, ("yhi", "row"), 0, 0)
     grads_other = lax.ppermute(grads_own, "core", swap)
     partial = gradient(parity, grads_own, grads_other, gathered)

time: 126 us -> 125 us (level)
  no operation moved by 1% of the time
where the time goes in v7:
time: 125 us; the launch traced here: 124 us
  blocking collectives  88.9 us (71%)
  starting transfers between devices  21.2 us (17%)
  Pallas kernels  7.45 us (6%)
  waiting for transfers between devices  3.57 us (3%)
  local copies, waits for them, and re-layouts  2.21 us (2%)
    all_to_all x1, blocking collectives, shards(): parts = lax.all_to_all(pair, ('yhi', 'row'), 0, 0)  23.1 us
    all_to_all x1, blocking collectives, shards(): over_samples = lax.all_to_all(partial, ('zhi', 'zlo'), 0, 0)  19.3 us
    all_gather x1, blocking collectives, shards(): kernels = lax.all_gather(pairs, 'zhi').reshape(8, TAPS, 4, CHAN)  18.7 us
    all_to_all x1, blocking collectives, shards(): grads_own = lax.all_to_all(grads, ('yhi', 'row'), 0, 0)  17.6 us
    all_to_all x1, blocking collectives, shards(): lax.all_to_all(jnp.broadcast_to(summed[None], (ROWS, TAPS, 4, CHAN)), 'ro...  10.1 us
    all_to_all x1, starting transfers between devices, shards(): gathered = lax.all_to_all(sent, 'row', 0, 0).reshape(GRID_J, 2, SENT, CHAN)  6.01 us
    ppermute x1, starting transfers between devices, shards(): received = lax.ppermute(other, 'core', swap)  5.93 us
    ppermute x1, starting transfers between devices, shards(): grads_other = lax.ppermute(grads_own, 'core', swap)  5.3 us
  transfers between devices with their start and end apart: 4, of which 3 were waited for; matrix products, arithmetic and copies ran while one was open for 1% of the time, Pallas kernels for 0%

profile of v7, /device:TPU:1, one launch (start us, length us, event | category | flops | bytes accessed | tf_op | source)
XLA Modules:
  0.0 124.0 jit_solution(16776048914193785499)
XLA Ops:
  0.0 2.4 %prepare_blocks.1 = (bf16[8,448,256]{2,1,0:T(8,128)(2,1)}, bf16[112,256]{1,0:T(8,128)(2,1)}) custom-call(s32[1]{0:T(128)} %bitcast.1.row_ref, bf16[432,256]{1,0:T(8,128)(2,1)} %bitcast.35, s32[6,1,72]{2,1,0:T(1,128)} %bitcast.38, bf16[27,32,256]{2,1,0:T(8,128)(2,1)} %bitcast.34), custom_call_target="tpu_custom_call" | custom-call | bytes 1990656 | tf_op jit(solution)/shard_map/prepare_blocks/pallas_call | solution.py:111
  2.4 0.0 copy-start.1
  2.5 0.0 copy-start
  2.5 6.0 %all-to-all-start = ((bf16[8,448,256]{2,1,0:T(8,128)(2,1)}), bf16[8,448,256]{2,1,0:T(8,128)(2,1)S(1)}, u32[]{:S(2)}, u32[]{:S(2)}) async-start(bf16[8,448,256]{2,1,0:T(8,128)(2,1)} %get-tuple-element.16), calls=%async_computation | async-start | bytes 3670016 | tf_op jit(solution)/shard_map/all_to_all | solution.py:356
  8.5 0.0 copy-start.2
  8.5 0.0 copy-done.1
  8.5 4.0 %collective-permute-start = (bf16[27,4,256]{2,1,0:T(4,128)(2,1)S(1)}, bf16[27,4,256]{2,1,0:T(4,128)(2,1)S(1)}, u32[]{:S(2)}, u32[]{:S(2)}) collective-permute-start(bf16[27,4,256]{2,1,0:T(4,128)(2,1)S(1)} %reshape.48), channel_id=1, source_target_pairs={{0,1},{1,0},{2,3},{3,2},{4,5},{5,4},{6,7},{7,6},{8,9},{9,8},{10,11... | collective-permute-start | bytes 165896 | tf_op jit(solution)/shard_map/ppermute | solution.py:358
  12.5 0.0 copy-done
  12.5 0.1 reshape.51
  12.7 0.2 copy.24
  12.8 0.1 reshape.52.proj_ref
  13.0 0.0 copy-done.2
  13.0 0.1 copy.18
  13.1 0.9 collective-permute-done
  14.1 0.1 pad_maximum_fusion
  14.2 18.7 %all-gather = bf16[8,27,4,256]{3,2,0,1:T(4,128)(2,1)S(1)} all-gather(bf16[2,27,4,256]{3,2,0,1:T(4,128)(2,1)S(1)} %pad_maximum_fusion), channel_id=2, replica_groups=mesh['row'=8,'yhi'=4,'core'=2,'zhi'=4,'zlo'=2] {'zhi'}, dimensions={0}, use_global_device_ids=true | all-gather | bytes 552960 | tf_op jit(solution)/shard_map/all_gather | solution.py:361
  32.9 0.1 reshape.50.weights_ref
  33.1 0.0 all-to-all-done
  33.1 2.2 %forward_taps.1 = (bf16[32,48,128]{2,1,0:T(8,128)(2,1)S(1)}, bf16[32,48,128]{2,1,0:T(8,128)(2,1)S(1)}) custom-call(s32[1]{0:T(128)} %bitcast.core_ref.parity_ref, bf16[4,2,448,256]{3,2,1,0:T(8,128)(2,1)S(1)} %bitcast.28, bf16[864,256]{1,0:T(8,128)(2,1)S(1)} %reshape.50.weights_ref), custom_call_target="tpu_custom_call" | custom-call | flops 1528823808 | bytes 4000000 | tf_op jit(solution)/shard_map/forward_taps/pallas_call | solution.py:178
  35.3 5.9 %collective-permute-start.1 = (bf16[32,48,128]{2,1,0:T(8,128)(2,1)S(1)}, bf16[32,48,128]{2,1,0:T(8,128)(2,1)S(1)}, u32[]{:S(2)}, u32[]{:S(2)}) collective-permute-start(bf16[32,48,128]{2,1,0:T(8,128)(2,1)S(1)} %get-tuple-element.20), channel_id=1, source_target_pairs={{0,8},{8,0},{1,9},{9,1},{2,10},{10,2},{3,11},{11,3},{4,12},{12,4},... | collective-permute-start | bytes 1179656 | tf_op jit(solution)/shard_map/ppermute | solution.py:376
  41.2 1.3 %collective-permute-done.1 = bf16[32,48,128]{2,1,0:T(8,128)(2,1)S(1)} collective-permute-done((bf16[32,48,128]{2,1,0:T(8,128)(2,1)S(1)}, bf16[32,48,128]{2,1,0:T(8,128)(2,1)S(1)}, u32[]{:S(2)}, u32[]{:S(2)}) %collective-permute-start.1) | collective-permute-done | bytes 393248 | tf_op jit(solution)/shard_map/ppermute | solution.py:376
  42.5 0.1 add_convert_fusion
  42.7 23.1 %all_to_all.25.parts_ref = bf16[32,48,128]{2,1,0:T(8,128)(2,1)S(1)} all-to-all(bf16[32,48,128]{2,1,0:T(8,128)(2,1)S(1)} %add_convert_fusion), channel_id=1, replica_groups=mesh['row'=8,'yhi'=4,'core'=2,'zhi'=4,'zlo'=2] {'yhi','row'}, dimensions={0} | all-to-all | bytes 786432 | tf_op jit(solution)/shard_map/all_to_all | solution.py:379
  65.7 1.1 tail.1
  66.8 17.6 %all_to_all.26.own_ref = bf16[32,48,128]{2,1,0:T(8,128)(2,1)S(1)} all-to-all(bf16[32,48,128]{2,1,0:T(8,128)(2,1)S(1)} %tail.1), channel_id=1, replica_groups=mesh['row'=8,'yhi'=4,'core'=2,'zhi'=4,'zlo'=2] {'yhi','row'}, dimensions={0} | all-to-all | bytes 786432 | tf_op jit(solution)/shard_map/all_to_all | solution.py:381
  84.5 5.3 %collective-permute-start.2 = (bf16[32,48,128]{2,1,0:T(8,128)(2,1)S(1)}, bf16[32,48,128]{2,1,0:T(8,128)(2,1)S(1)}, u32[]{:S(2)}, u32[]{:S(2)}) collective-permute-start(bf16[32,48,128]{2,1,0:T(8,128)(2,1)S(1)} %all_to_all.26.own_ref), channel_id=1, source_target_pairs={{0,8},{8,0},{1,9},{9,1},{2,10},{10,2},{3,11},{11,3},{4,12},{12,4},... | collective-permute-start | bytes 1179656 | tf_op jit(solution)/shard_map/ppermute | solution.py:382
  89.8 1.3 %collective-permute-done.2.other_ref = bf16[32,48,128]{2,1,0:T(8,128)(2,1)S(1)} collective-permute-done((bf16[32,48,128]{2,1,0:T(8,128)(2,1)S(1)}, bf16[32,48,128]{2,1,0:T(8,128)(2,1)S(1)}, u32[]{:S(2)}, u32[]{:S(2)}) %collective-permute-start.2) | collective-permute-done | bytes 393248 | tf_op jit(solution)/shard_map/ppermute | solution.py:382
  91.1 1.8 %gradient_taps.1 = bf16[864,256]{1,0:T(8,128)(2,1)S(1)} custom-call(s32[1]{0:T(128)} %bitcast.core_ref.parity_ref, bf16[32,48,128]{2,1,0:T(8,128)(2,1)S(1)} %all_to_all.26.own_ref, bf16[32,48,128]{2,1,0:T(8,128)(2,1)S(1)} %collective-permute-done.2.other_ref, bf16[4,2,448,256]{3,2,1,0:T(8,128)(2,1)S(1)} %bitcast.29), custom_call_target="tpu_custom_call" | custom-call | flops 1528823808 | bytes 4000000 | tf_op jit(solution)/shard_map/gradient_taps/pallas_call | solution.py:326
  92.9 0.1 reshape.56
  93.0 0.2 copy.23
  93.1 19.3 %all_to_all.27 = bf16[8,27,4,256]{3,2,1,0:T(4,128)(2,1)S(1)} all-to-all(bf16[8,27,4,256]{3,2,1,0:T(4,128)(2,1)S(1)} %bitcast.30), channel_id=1, replica_groups=mesh['row'=8,'yhi'=4,'core'=2,'zhi'=4,'zlo'=2] {'zhi','zlo'}, dimensions={0} | all-to-all | bytes 884736 | tf_op jit(solution)/shard_map/all_to_all | solution.py:385
  112.5 0.2 reduce_sum.12
  112.7 0.1 broadcast_in_dim.2
  112.8 10.1 %all_to_all.28 = bf16[8,27,4,256]{3,2,1,0:T(4,128)(2,1)S(1)} all-to-all(bf16[8,27,4,256]{3,2,1,0:T(4,128)(2,1)S(1)} %broadcast_in_dim.2), channel_id=1, replica_groups=mesh['row'=8,'yhi'=4,'core'=2,'zhi'=4,'zlo'=2] {'row'}, dimensions={0} | all-to-all | bytes 884736 | tf_op jit(solution)/shard_map/all_to_all | solution.py:387
  122.9 0.2 copy.20
  123.1 0.9 reshape.57
  (7 shorter events, 0.1 us)
Async XLA Ops:
  2.4 6.0 %copy-start.1 = (bf16[112,256]{1,0:T(8,128)(2,1)S(1)}, bf16[112,256]{1,0:T(8,128)(2,1)}, u32[]{:S(2)}) copy-start(bf16[112,256]{1,0:T(8,128)(2,1)} %get-tuple-element.15) | copy-start | bytes 172036
  2.5 10.1 %copy-start = (bf16[768,256]{1,0:T(8,128)(2,1)S(1)}, bf16[768,256]{1,0:T(8,128)(2,1)}, u32[]{:S(2)}) copy-start(bf16[768,256]{1,0:T(8,128)(2,1)} %param.7) | copy-start | bytes 1179652
  2.5 30.6 %all-to-all-start = ((bf16[8,448,256]{2,1,0:T(8,128)(2,1)}), bf16[8,448,256]{2,1,0:T(8,128)(2,1)S(1)}, u32[]{:S(2)}, u32[]{:S(2)}) async-start(bf16[8,448,256]{2,1,0:T(8,128)(2,1)} %get-tuple-element.16), calls=%async_computation | async-start | bytes 3670016 | tf_op jit(solution)/shard_map/all_to_all | solution.py:356
  8.5 4.5 %copy-start.2 = (bf16[256,3]{0,1:T(4,128)(2,1)S(1)}, bf16[256,3]{0,1:T(4,128)(2,1)}, u32[]{:S(2)}) copy-start(bf16[256,3]{0,1:T(4,128)(2,1)} %param.8) | copy-start | bytes 4612
  8.5 5.5 %collective-permute-start = (bf16[27,4,256]{2,1,0:T(4,128)(2,1)S(1)}, bf16[27,4,256]{2,1,0:T(4,128)(2,1)S(1)}, u32[]{:S(2)}, u32[]{:S(2)}) collective-permute-start(bf16[27,4,256]{2,1,0:T(4,128)(2,1)S(1)} %reshape.48), channel_id=1, source_target_pairs={{0,1},{1,0},{2,3},{3,2},{4,5},{5,4},{6,7},{7,6},{8,9},{9,8},{10,11... | collective-permute-start | bytes 165896 | tf_op jit(solution)/shard_map/ppermute | solution.py:358
  35.3 7.3 %collective-permute-start.1 = (bf16[32,48,128]{2,1,0:T(8,128)(2,1)S(1)}, bf16[32,48,128]{2,1,0:T(8,128)(2,1)S(1)}, u32[]{:S(2)}, u32[]{:S(2)}) collective-permute-start(bf16[32,48,128]{2,1,0:T(8,128)(2,1)S(1)} %get-tuple-element.20), channel_id=1, source_target_pairs={{0,8},{8,0},{1,9},{9,1},{2,10},{10,2},{3,11},{11,3},{4,12},{12,4},... | collective-permute-start | bytes 1179656 | tf_op jit(solution)/shard_map/ppermute | solution.py:376
  84.5 6.6 %collective-permute-start.2 = (bf16[32,48,128]{2,1,0:T(8,128)(2,1)S(1)}, bf16[32,48,128]{2,1,0:T(8,128)(2,1)S(1)}, u32[]{:S(2)}, u32[]{:S(2)}) collective-permute-start(bf16[32,48,128]{2,1,0:T(8,128)(2,1)S(1)} %all_to_all.26.own_ref), channel_id=1, source_target_pairs={{0,8},{8,0},{1,9},{9,1},{2,10},{10,2},{3,11},{11,3},{4,12},{12,4},... | collective-permute-start | bytes 1179656 | tf_op jit(solution)/shard_map/ppermute | solution.py:382

commit v8 on v7

--- a/solution.py
+++ b/solution.py
@@ -15,7 +15,7 @@
 UNITS = GRID_J * GRID_Q
 HALF = UNITS * UNIT
 SHARD = 432
-SENT = 448
+SENT = 440
 PARTS = 32
 USED = 27
 SHARE = 48

time: 125 us -> 125 us (level)
  no operation moved by 1% of the time
where the time goes in v8:
time: 125 us; the launch traced here: 124 us
  blocking collectives  88.9 us (71%)
  starting transfers between devices  21.2 us (17%)
  Pallas kernels  7.46 us (6%)
  waiting for transfers between devices  3.57 us (3%)
  local copies, waits for them, and re-layouts  2.21 us (2%)
    all_to_all x1, blocking collectives, shards(): parts = lax.all_to_all(pair, ('yhi', 'row'), 0, 0)  23.1 us
    all_to_all x1, blocking collectives, shards(): over_samples = lax.all_to_all(partial, ('zhi', 'zlo'), 0, 0)  19.3 us
    all_gather x1, blocking collectives, shards(): kernels = lax.all_gather(pairs, 'zhi').reshape(8, TAPS, 4, CHAN)  18.7 us
    all_to_all x1, blocking collectives, shards(): grads_own = lax.all_to_all(grads, ('yhi', 'row'), 0, 0)  17.6 us
    all_to_all x1, blocking collectives, shards(): lax.all_to_all(jnp.broadcast_to(summed[None], (ROWS, TAPS, 4, CHAN)), 'ro...  10.1 us
    all_to_all x1, starting transfers between devices, shards(): gathered = lax.all_to_all(sent, 'row', 0, 0).reshape(GRID_J, 2, SENT, CHAN)  6.01 us
    ppermute x1, starting transfers between devices, shards(): received = lax.ppermute(other, 'core', swap)  5.93 us
    ppermute x1, starting transfers between devices, shards(): grads_other = lax.ppermute(grads_own, 'core', swap)  5.3 us
  transfers between devices with their start and end apart: 4, of which 3 were waited for; matrix products, arithmetic and copies ran while one was open for 1% of the time, Pallas kernels for 0%

profile of v8, /device:TPU:1, one launch (start us, length us, event | category | flops | bytes accessed | tf_op | source)
XLA Modules:
  0.0 124.0 jit_solution(6575600500496559939)
XLA Ops:
  0.0 2.4 %prepare_blocks.1 = (bf16[8,440,256]{2,1,0:T(8,128)(2,1)}, bf16[112,256]{1,0:T(8,128)(2,1)}) custom-call(s32[1]{0:T(128)} %bitcast.1.row_ref, bf16[432,256]{1,0:T(8,128)(2,1)} %bitcast.35, s32[6,1,72]{2,1,0:T(1,128)} %bitcast.38, bf16[27,32,256]{2,1,0:T(8,128)(2,1)} %bitcast.34), custom_call_target="tpu_custom_call" | custom-call | bytes 1990656 | tf_op jit(solution)/shard_map/prepare_blocks/pallas_call | solution.py:111
  2.4 0.0 copy-start.1
  2.5 0.0 copy-start
  2.5 6.0 %all-to-all-start = ((bf16[8,440,256]{2,1,0:T(8,128)(2,1)}), bf16[8,440,256]{2,1,0:T(8,128)(2,1)S(1)}, u32[]{:S(2)}, u32[]{:S(2)}) async-start(bf16[8,440,256]{2,1,0:T(8,128)(2,1)} %get-tuple-element.16), calls=%async_computation | async-start | bytes 3604480 | tf_op jit(solution)/shard_map/all_to_all | solution.py:356
  8.5 0.0 copy-start.2
  8.5 0.0 copy-done.1
  8.5 4.0 %collective-permute-start = (bf16[27,4,256]{2,1,0:T(4,128)(2,1)S(1)}, bf16[27,4,256]{2,1,0:T(4,128)(2,1)S(1)}, u32[]{:S(2)}, u32[]{:S(2)}) collective-permute-start(bf16[27,4,256]{2,1,0:T(4,128)(2,1)S(1)} %reshape.48), channel_id=1, source_target_pairs={{0,1},{1,0},{2,3},{3,2},{4,5},{5,4},{6,7},{7,6},{8,9},{9,8},{10,11... | collective-permute-start | bytes 165896 | tf_op jit(solution)/shard_map/ppermute | solution.py:358
  12.5 0.0 copy-done
  12.5 0.1 reshape.51
  12.6 0.2 copy.24
  12.8 0.1 reshape.52.proj_ref
  13.0 0.0 copy-done.2
  13.0 0.1 copy.18
  13.1 0.9 collective-permute-done
  14.1 0.1 pad_maximum_fusion
  14.2 18.7 %all-gather = bf16[8,27,4,256]{3,2,0,1:T(4,128)(2,1)S(1)} all-gather(bf16[2,27,4,256]{3,2,0,1:T(4,128)(2,1)S(1)} %pad_maximum_fusion), channel_id=2, replica_groups=mesh['row'=8,'yhi'=4,'core'=2,'zhi'=4,'zlo'=2] {'zhi'}, dimensions={0}, use_global_device_ids=true | all-gather | bytes 552960 | tf_op jit(solution)/shard_map/all_gather | solution.py:361
  32.9 0.1 reshape.50.weights_ref
  33.1 0.0 all-to-all-done
  33.1 2.2 %forward_taps.1 = (bf16[32,48,128]{2,1,0:T(8,128)(2,1)S(1)}, bf16[32,48,128]{2,1,0:T(8,128)(2,1)S(1)}) custom-call(s32[1]{0:T(128)} %bitcast.core_ref.parity_ref, bf16[4,2,440,256]{3,2,1,0:T(8,128)(2,1)S(1)} %bitcast.28, bf16[864,256]{1,0:T(8,128)(2,1)S(1)} %reshape.50.weights_ref), custom_call_target="tpu_custom_call" | custom-call | flops 1528823808 | bytes 4000000 | tf_op jit(solution)/shard_map/forward_taps/pallas_call | solution.py:178
  35.3 5.9 %collective-permute-start.1 = (bf16[32,48,128]{2,1,0:T(8,128)(2,1)S(1)}, bf16[32,48,128]{2,1,0:T(8,128)(2,1)S(1)}, u32[]{:S(2)}, u32[]{:S(2)}) collective-permute-start(bf16[32,48,128]{2,1,0:T(8,128)(2,1)S(1)} %get-tuple-element.20), channel_id=1, source_target_pairs={{0,8},{8,0},{1,9},{9,1},{2,10},{10,2},{3,11},{11,3},{4,12},{12,4},... | collective-permute-start | bytes 1179656 | tf_op jit(solution)/shard_map/ppermute | solution.py:376
  41.2 1.3 %collective-permute-done.1 = bf16[32,48,128]{2,1,0:T(8,128)(2,1)S(1)} collective-permute-done((bf16[32,48,128]{2,1,0:T(8,128)(2,1)S(1)}, bf16[32,48,128]{2,1,0:T(8,128)(2,1)S(1)}, u32[]{:S(2)}, u32[]{:S(2)}) %collective-permute-start.1) | collective-permute-done | bytes 393248 | tf_op jit(solution)/shard_map/ppermute | solution.py:376
  42.5 0.1 add_convert_fusion
  42.6 23.1 %all_to_all.25.parts_ref = bf16[32,48,128]{2,1,0:T(8,128)(2,1)S(1)} all-to-all(bf16[32,48,128]{2,1,0:T(8,128)(2,1)S(1)} %add_convert_fusion), channel_id=1, replica_groups=mesh['row'=8,'yhi'=4,'core'=2,'zhi'=4,'zlo'=2] {'yhi','row'}, dimensions={0} | all-to-all | bytes 786432 | tf_op jit(solution)/shard_map/all_to_all | solution.py:379
  65.7 1.1 tail.1
  66.8 17.6 %all_to_all.26.own_ref = bf16[32,48,128]{2,1,0:T(8,128)(2,1)S(1)} all-to-all(bf16[32,48,128]{2,1,0:T(8,128)(2,1)S(1)} %tail.1), channel_id=1, replica_groups=mesh['row'=8,'yhi'=4,'core'=2,'zhi'=4,'zlo'=2] {'yhi','row'}, dimensions={0} | all-to-all | bytes 786432 | tf_op jit(solution)/shard_map/all_to_all | solution.py:381
  84.5 5.3 %collective-permute-start.2 = (bf16[32,48,128]{2,1,0:T(8,128)(2,1)S(1)}, bf16[32,48,128]{2,1,0:T(8,128)(2,1)S(1)}, u32[]{:S(2)}, u32[]{:S(2)}) collective-permute-start(bf16[32,48,128]{2,1,0:T(8,128)(2,1)S(1)} %all_to_all.26.own_ref), channel_id=1, source_target_pairs={{0,8},{8,0},{1,9},{9,1},{2,10},{10,2},{3,11},{11,3},{4,12},{12,4},... | collective-permute-start | bytes 1179656 | tf_op jit(solution)/shard_map/ppermute | solution.py:382
  89.8 1.3 %collective-permute-done.2.other_ref = bf16[32,48,128]{2,1,0:T(8,128)(2,1)S(1)} collective-permute-done((bf16[32,48,128]{2,1,0:T(8,128)(2,1)S(1)}, bf16[32,48,128]{2,1,0:T(8,128)(2,1)S(1)}, u32[]{:S(2)}, u32[]{:S(2)}) %collective-permute-start.2) | collective-permute-done | bytes 393248 | tf_op jit(solution)/shard_map/ppermute | solution.py:382
  91.1 1.8 %gradient_taps.1 = bf16[864,256]{1,0:T(8,128)(2,1)S(1)} custom-call(s32[1]{0:T(128)} %bitcast.core_ref.parity_ref, bf16[32,48,128]{2,1,0:T(8,128)(2,1)S(1)} %all_to_all.26.own_ref, bf16[32,48,128]{2,1,0:T(8,128)(2,1)S(1)} %collective-permute-done.2.other_ref, bf16[4,2,440,256]{3,2,1,0:T(8,128)(2,1)S(1)} %bitcast.29), custom_call_target="tpu_custom_call" | custom-call | flops 1528823808 | bytes 4000000 | tf_op jit(solution)/shard_map/gradient_taps/pallas_call | solution.py:326
  92.9 0.1 reshape.56
  93.0 0.2 copy.23
  93.1 19.3 %all_to_all.27 = bf16[8,27,4,256]{3,2,1,0:T(4,128)(2,1)S(1)} all-to-all(bf16[8,27,4,256]{3,2,1,0:T(4,128)(2,1)S(1)} %bitcast.30), channel_id=1, replica_groups=mesh['row'=8,'yhi'=4,'core'=2,'zhi'=4,'zlo'=2] {'zhi','zlo'}, dimensions={0} | all-to-all | bytes 884736 | tf_op jit(solution)/shard_map/all_to_all | solution.py:385
  112.5 0.2 reduce_sum.12
  112.7 0.1 broadcast_in_dim.2
  112.8 10.1 %all_to_all.28 = bf16[8,27,4,256]{3,2,1,0:T(4,128)(2,1)S(1)} all-to-all(bf16[8,27,4,256]{3,2,1,0:T(4,128)(2,1)S(1)} %broadcast_in_dim.2), channel_id=1, replica_groups=mesh['row'=8,'yhi'=4,'core'=2,'zhi'=4,'zlo'=2] {'row'}, dimensions={0} | all-to-all | bytes 884736 | tf_op jit(solution)/shard_map/all_to_all | solution.py:387
  122.9 0.2 copy.20
  123.1 0.9 reshape.57
  (7 shorter events, 0.1 us)
Async XLA Ops:
  2.4 6.0 %copy-start.1 = (bf16[112,256]{1,0:T(8,128)(2,1)S(1)}, bf16[112,256]{1,0:T(8,128)(2,1)}, u32[]{:S(2)}) copy-start(bf16[112,256]{1,0:T(8,128)(2,1)} %get-tuple-element.15) | copy-start | bytes 172036
  2.5 10.1 %copy-start = (bf16[768,256]{1,0:T(8,128)(2,1)S(1)}, bf16[768,256]{1,0:T(8,128)(2,1)}, u32[]{:S(2)}) copy-start(bf16[768,256]{1,0:T(8,128)(2,1)} %param.7) | copy-start | bytes 1179652
  2.5 30.6 %all-to-all-start = ((bf16[8,440,256]{2,1,0:T(8,128)(2,1)}), bf16[8,440,256]{2,1,0:T(8,128)(2,1)S(1)}, u32[]{:S(2)}, u32[]{:S(2)}) async-start(bf16[8,440,256]{2,1,0:T(8,128)(2,1)} %get-tuple-element.16), calls=%async_computation | async-start | bytes 3604480 | tf_op jit(solution)/shard_map/all_to_all | solution.py:356
  8.5 4.5 %copy-start.2 = (bf16[256,3]{0,1:T(4,128)(2,1)S(1)}, bf16[256,3]{0,1:T(4,128)(2,1)}, u32[]{:S(2)}) copy-start(bf16[256,3]{0,1:T(4,128)(2,1)} %param.8) | copy-start | bytes 4612
  8.5 5.5 %collective-permute-start = (bf16[27,4,256]{2,1,0:T(4,128)(2,1)S(1)}, bf16[27,4,256]{2,1,0:T(4,128)(2,1)S(1)}, u32[]{:S(2)}, u32[]{:S(2)}) collective-permute-start(bf16[27,4,256]{2,1,0:T(4,128)(2,1)S(1)} %reshape.48), channel_id=1, source_target_pairs={{0,1},{1,0},{2,3},{3,2},{4,5},{5,4},{6,7},{7,6},{8,9},{9,8},{10,11... | collective-permute-start | bytes 165896 | tf_op jit(solution)/shard_map/ppermute | solution.py:358
  35.3 7.3 %collective-permute-start.1 = (bf16[32,48,128]{2,1,0:T(8,128)(2,1)S(1)}, bf16[32,48,128]{2,1,0:T(8,128)(2,1)S(1)}, u32[]{:S(2)}, u32[]{:S(2)}) collective-permute-start(bf16[32,48,128]{2,1,0:T(8,128)(2,1)S(1)} %get-tuple-element.20), channel_id=1, source_target_pairs={{0,8},{8,0},{1,9},{9,1},{2,10},{10,2},{3,11},{11,3},{4,12},{12,4},... | collective-permute-start | bytes 1179656 | tf_op jit(solution)/shard_map/ppermute | solution.py:376
  84.5 6.6 %collective-permute-start.2 = (bf16[32,48,128]{2,1,0:T(8,128)(2,1)S(1)}, bf16[32,48,128]{2,1,0:T(8,128)(2,1)S(1)}, u32[]{:S(2)}, u32[]{:S(2)}) collective-permute-start(bf16[32,48,128]{2,1,0:T(8,128)(2,1)S(1)} %all_to_all.26.own_ref), channel_id=1, source_target_pairs={{0,8},{8,0},{1,9},{9,1},{2,10},{10,2},{3,11},{11,3},{4,12},{12,4},... | collective-permute-start | bytes 1179656 | tf_op jit(solution)/shard_map/ppermute | solution.py:382

commit v9 on v7

--- a/solution.py
+++ b/solution.py
@@ -229,9 +229,10 @@
 
     preact, gate = [], []
     for row in range(ROWS):
-        total = parts_ref[row].astype(F32)
+        first = row * (PARTS // ROWS)
+        total = parts_ref[first].astype(F32)
         for part in range(1, PARTS // ROWS):
-            total = total + parts_ref[part * ROWS + row].astype(F32)
+            total = total + parts_ref[first + part].astype(F32)
         preact.append(total)
         gate.append(sigmoid(total))
         packed_ref[row] = total * gate[row]
@@ -258,7 +259,7 @@
     for row in range(ROWS):
         block = (packed_ref[row] * swish_grad(preact[row], gate[row])).astype(BF16)
         for part in range(PARTS // ROWS):
-            out_ref[part * ROWS + row] = block
+            out_ref[row * (PARTS // ROWS) + part] = block
 
 
 def tail(part, parts, proj, classify, classify_t, marks):
@@ -344,7 +345,7 @@
 def shards(features, weights, proj, classify, labels):
     row = lax.axis_index("row")
     core = lax.axis_index("core")
-    part = lax.axis_index("yhi") * ROWS + row
+    part = row * (PARTS // ROWS) + lax.axis_index("yhi")
     swap = [(0, 1), (1, 0)]
 
     sent, mine = prepare(
@@ -376,9 +377,9 @@
     received = lax.ppermute(other, "core", swap)
     pair = (own.astype(F32) + received.astype(F32)).astype(BF16)
 
-    parts = lax.all_to_all(pair, ("yhi", "row"), 0, 0)
+    parts = lax.all_to_all(pair, ("row", "yhi"), 0, 0)
     grads = tail(part, parts, mixing, heads, heads_t, marks)
-    grads_own = lax.all_to_all(grads, ("yhi", "row"), 0, 0)
+    grads_own = lax.all_to_all(grads, ("row", "yhi"), 0, 0)
     grads_other = lax.ppermute(grads_own, "core", swap)
     partial = gradient(parity, grads_own, grads_other, gathered)
     partial = partial.reshape(TAPS, 8, 4, CHAN).transpose(1, 0, 2, 3)

time: 125 us -> 125 us (level)
  no operation moved by 1% of the time
where the time goes in v9:
time: 125 us; the launch traced here: 124 us
  blocking collectives  87.8 us (70%)
  starting transfers between devices  22.2 us (18%)
  Pallas kernels  7.45 us (6%)
  waiting for transfers between devices  3.56 us (3%)
  local copies, waits for them, and re-layouts  2.21 us (2%)
    all_to_all x1, blocking collectives, shards(): parts = lax.all_to_all(pair, ('row', 'yhi'), 0, 0)  23 us
    all_to_all x1, blocking collectives, shards(): over_samples = lax.all_to_all(partial, ('zhi', 'zlo'), 0, 0)  19.3 us
    all_gather x1, blocking collectives, shards(): kernels = lax.all_gather(pairs, 'zhi').reshape(8, TAPS, 4, CHAN)  18.7 us
    all_to_all x1, blocking collectives, shards(): grads_own = lax.all_to_all(grads, ('row', 'yhi'), 0, 0)  16.5 us
    all_to_all x1, blocking collectives, shards(): lax.all_to_all(jnp.broadcast_to(summed[None], (ROWS, TAPS, 4, CHAN)), 'ro...  10.2 us
    ppermute x1, starting transfers between devices, shards(): grads_other = lax.ppermute(grads_own, 'core', swap)  6.23 us
    all_to_all x1, starting transfers between devices, shards(): gathered = lax.all_to_all(sent, 'row', 0, 0).reshape(GRID_J, 2, SENT, CHAN)  6.01 us
    ppermute x1, starting transfers between devices, shards(): received = lax.ppermute(other, 'core', swap)  5.93 us
  transfers between devices with their start and end apart: 4, of which 3 were waited for; matrix products, arithmetic and copies ran while one was open for 1% of the time, Pallas kernels for 0%

profile of v9, /device:TPU:1, one launch (start us, length us, event | category | flops | bytes accessed | tf_op | source)
XLA Modules:
  0.0 123.8 jit_solution(9815918619889294195)
XLA Ops:
  0.0 2.4 %prepare_blocks.1 = (bf16[8,448,256]{2,1,0:T(8,128)(2,1)}, bf16[112,256]{1,0:T(8,128)(2,1)}) custom-call(s32[1]{0:T(128)} %bitcast.1.row_ref, bf16[432,256]{1,0:T(8,128)(2,1)} %bitcast.35, s32[6,1,72]{2,1,0:T(1,128)} %bitcast.38, bf16[27,32,256]{2,1,0:T(8,128)(2,1)} %bitcast.34), custom_call_target="tpu_custom_call" | custom-call | bytes 1990656 | tf_op jit(solution)/shard_map/prepare_blocks/pallas_call | solution.py:111
  2.4 0.0 copy-start.1
  2.5 0.0 copy-start
  2.5 6.0 %all-to-all-start = ((bf16[8,448,256]{2,1,0:T(8,128)(2,1)}), bf16[8,448,256]{2,1,0:T(8,128)(2,1)S(1)}, u32[]{:S(2)}, u32[]{:S(2)}) async-start(bf16[8,448,256]{2,1,0:T(8,128)(2,1)} %get-tuple-element.16), calls=%async_computation | async-start | bytes 3670016 | tf_op jit(solution)/shard_map/all_to_all | solution.py:357
  8.5 0.0 copy-start.2
  8.5 0.0 copy-done.1
  8.5 4.0 %collective-permute-start = (bf16[27,4,256]{2,1,0:T(4,128)(2,1)S(1)}, bf16[27,4,256]{2,1,0:T(4,128)(2,1)S(1)}, u32[]{:S(2)}, u32[]{:S(2)}) collective-permute-start(bf16[27,4,256]{2,1,0:T(4,128)(2,1)S(1)} %reshape.48), channel_id=1, source_target_pairs={{0,1},{1,0},{2,3},{3,2},{4,5},{5,4},{6,7},{7,6},{8,9},{9,8},{10,11... | collective-permute-start | bytes 165896 | tf_op jit(solution)/shard_map/ppermute | solution.py:359
  12.5 0.0 copy-done
  12.5 0.1 reshape.51
  12.6 0.2 copy.24
  12.8 0.1 reshape.52.proj_ref
  12.9 0.0 copy-done.2
  13.0 0.1 copy.18
  13.1 0.9 collective-permute-done
  14.1 0.1 pad_maximum_fusion
  14.2 18.7 %all-gather = bf16[8,27,4,256]{3,2,0,1:T(4,128)(2,1)S(1)} all-gather(bf16[2,27,4,256]{3,2,0,1:T(4,128)(2,1)S(1)} %pad_maximum_fusion), channel_id=2, replica_groups=mesh['row'=8,'yhi'=4,'core'=2,'zhi'=4,'zlo'=2] {'zhi'}, dimensions={0}, use_global_device_ids=true | all-gather | bytes 552960 | tf_op jit(solution)/shard_map/all_gather | solution.py:362
  32.9 0.1 reshape.50.weights_ref
  33.1 0.0 all-to-all-done
  33.1 2.2 %forward_taps.1 = (bf16[32,48,128]{2,1,0:T(8,128)(2,1)S(1)}, bf16[32,48,128]{2,1,0:T(8,128)(2,1)S(1)}) custom-call(s32[1]{0:T(128)} %bitcast.core_ref.parity_ref, bf16[4,2,448,256]{3,2,1,0:T(8,128)(2,1)S(1)} %bitcast.28, bf16[864,256]{1,0:T(8,128)(2,1)S(1)} %reshape.50.weights_ref), custom_call_target="tpu_custom_call" | custom-call | flops 1528823808 | bytes 4000000 | tf_op jit(solution)/shard_map/forward_taps/pallas_call | solution.py:178
  35.3 5.9 %collective-permute-start.1 = (bf16[32,48,128]{2,1,0:T(8,128)(2,1)S(1)}, bf16[32,48,128]{2,1,0:T(8,128)(2,1)S(1)}, u32[]{:S(2)}, u32[]{:S(2)}) collective-permute-start(bf16[32,48,128]{2,1,0:T(8,128)(2,1)S(1)} %get-tuple-element.20), channel_id=1, source_target_pairs={{0,8},{8,0},{1,9},{9,1},{2,10},{10,2},{3,11},{11,3},{4,12},{12,4},... | collective-permute-start | bytes 1179656 | tf_op jit(solution)/shard_map/ppermute | solution.py:377
  41.2 1.3 %collective-permute-done.1 = bf16[32,48,128]{2,1,0:T(8,128)(2,1)S(1)} collective-permute-done((bf16[32,48,128]{2,1,0:T(8,128)(2,1)S(1)}, bf16[32,48,128]{2,1,0:T(8,128)(2,1)S(1)}, u32[]{:S(2)}, u32[]{:S(2)}) %collective-permute-start.1) | collective-permute-done | bytes 393248 | tf_op jit(solution)/shard_map/ppermute | solution.py:377
  42.5 0.1 add_convert_fusion
  42.7 23.0 %all_to_all.25.parts_ref = bf16[32,48,128]{2,1,0:T(8,128)(2,1)S(1)} all-to-all(bf16[32,48,128]{2,1,0:T(8,128)(2,1)S(1)} %add_convert_fusion), channel_id=1, replica_groups=mesh['row'=8,'yhi'=4,'core'=2,'zhi'=4,'zlo'=2] {'row','yhi'}, dimensions={0} | all-to-all | bytes 786432 | tf_op jit(solution)/shard_map/all_to_all | solution.py:380
  65.7 1.1 tail.1
  66.8 16.5 %all_to_all.26.own_ref = bf16[32,48,128]{2,1,0:T(8,128)(2,1)S(1)} all-to-all(bf16[32,48,128]{2,1,0:T(8,128)(2,1)S(1)} %tail.1), channel_id=1, replica_groups=mesh['row'=8,'yhi'=4,'core'=2,'zhi'=4,'zlo'=2] {'row','yhi'}, dimensions={0} | all-to-all | bytes 786432 | tf_op jit(solution)/shard_map/all_to_all | solution.py:382
  83.3 6.2 %collective-permute-start.2 = (bf16[32,48,128]{2,1,0:T(8,128)(2,1)S(1)}, bf16[32,48,128]{2,1,0:T(8,128)(2,1)S(1)}, u32[]{:S(2)}, u32[]{:S(2)}) collective-permute-start(bf16[32,48,128]{2,1,0:T(8,128)(2,1)S(1)} %all_to_all.26.own_ref), channel_id=1, source_target_pairs={{0,8},{8,0},{1,9},{9,1},{2,10},{10,2},{3,11},{11,3},{4,12},{12,4},... | collective-permute-start | bytes 1179656 | tf_op jit(solution)/shard_map/ppermute | solution.py:383
  89.5 1.3 %collective-permute-done.2.other_ref = bf16[32,48,128]{2,1,0:T(8,128)(2,1)S(1)} collective-permute-done((bf16[32,48,128]{2,1,0:T(8,128)(2,1)S(1)}, bf16[32,48,128]{2,1,0:T(8,128)(2,1)S(1)}, u32[]{:S(2)}, u32[]{:S(2)}) %collective-permute-start.2) | collective-permute-done | bytes 393248 | tf_op jit(solution)/shard_map/ppermute | solution.py:383
  90.9 1.8 %gradient_taps.1 = bf16[864,256]{1,0:T(8,128)(2,1)S(1)} custom-call(s32[1]{0:T(128)} %bitcast.core_ref.parity_ref, bf16[32,48,128]{2,1,0:T(8,128)(2,1)S(1)} %all_to_all.26.own_ref, bf16[32,48,128]{2,1,0:T(8,128)(2,1)S(1)} %collective-permute-done.2.other_ref, bf16[4,2,448,256]{3,2,1,0:T(8,128)(2,1)S(1)} %bitcast.29), custom_call_target="tpu_custom_call" | custom-call | flops 1528823808 | bytes 4000000 | tf_op jit(solution)/shard_map/gradient_taps/pallas_call | solution.py:327
  92.6 0.1 reshape.56
  92.7 0.2 copy.23
  92.9 19.3 %all_to_all.27 = bf16[8,27,4,256]{3,2,1,0:T(4,128)(2,1)S(1)} all-to-all(bf16[8,27,4,256]{3,2,1,0:T(4,128)(2,1)S(1)} %bitcast.30), channel_id=1, replica_groups=mesh['row'=8,'yhi'=4,'core'=2,'zhi'=4,'zlo'=2] {'zhi','zlo'}, dimensions={0} | all-to-all | bytes 884736 | tf_op jit(solution)/shard_map/all_to_all | solution.py:386
  112.2 0.2 reduce_sum.12
  112.4 0.1 broadcast_in_dim.2
  112.5 10.2 %all_to_all.28 = bf16[8,27,4,256]{3,2,1,0:T(4,128)(2,1)S(1)} all-to-all(bf16[8,27,4,256]{3,2,1,0:T(4,128)(2,1)S(1)} %broadcast_in_dim.2), channel_id=1, replica_groups=mesh['row'=8,'yhi'=4,'core'=2,'zhi'=4,'zlo'=2] {'row'}, dimensions={0} | all-to-all | bytes 884736 | tf_op jit(solution)/shard_map/all_to_all | solution.py:388
  122.7 0.2 copy.20
  123.0 0.9 reshape.57
  (7 shorter events, 0.1 us)
Async XLA Ops:
  2.4 6.0 %copy-start.1 = (bf16[112,256]{1,0:T(8,128)(2,1)S(1)}, bf16[112,256]{1,0:T(8,128)(2,1)}, u32[]{:S(2)}) copy-start(bf16[112,256]{1,0:T(8,128)(2,1)} %get-tuple-element.15) | copy-start | bytes 172036
  2.5 10.1 %copy-start = (bf16[768,256]{1,0:T(8,128)(2,1)S(1)}, bf16[768,256]{1,0:T(8,128)(2,1)}, u32[]{:S(2)}) copy-start(bf16[768,256]{1,0:T(8,128)(2,1)} %param.7) | copy-start | bytes 1179652
  2.5 30.6 %all-to-all-start = ((bf16[8,448,256]{2,1,0:T(8,128)(2,1)}), bf16[8,448,256]{2,1,0:T(8,128)(2,1)S(1)}, u32[]{:S(2)}, u32[]{:S(2)}) async-start(bf16[8,448,256]{2,1,0:T(8,128)(2,1)} %get-tuple-element.16), calls=%async_computation | async-start | bytes 3670016 | tf_op jit(solution)/shard_map/all_to_all | solution.py:357
  8.5 4.5 %copy-start.2 = (bf16[256,3]{0,1:T(4,128)(2,1)S(1)}, bf16[256,3]{0,1:T(4,128)(2,1)}, u32[]{:S(2)}) copy-start(bf16[256,3]{0,1:T(4,128)(2,1)} %param.8) | copy-start | bytes 4612
  8.5 5.5 %collective-permute-start = (bf16[27,4,256]{2,1,0:T(4,128)(2,1)S(1)}, bf16[27,4,256]{2,1,0:T(4,128)(2,1)S(1)}, u32[]{:S(2)}, u32[]{:S(2)}) collective-permute-start(bf16[27,4,256]{2,1,0:T(4,128)(2,1)S(1)} %reshape.48), channel_id=1, source_target_pairs={{0,1},{1,0},{2,3},{3,2},{4,5},{5,4},{6,7},{7,6},{8,9},{9,8},{10,11... | collective-permute-start | bytes 165896 | tf_op jit(solution)/shard_map/ppermute | solution.py:359
  35.3 7.3 %collective-permute-start.1 = (bf16[32,48,128]{2,1,0:T(8,128)(2,1)S(1)}, bf16[32,48,128]{2,1,0:T(8,128)(2,1)S(1)}, u32[]{:S(2)}, u32[]{:S(2)}) collective-permute-start(bf16[32,48,128]{2,1,0:T(8,128)(2,1)S(1)} %get-tuple-element.20), channel_id=1, source_target_pairs={{0,8},{8,0},{1,9},{9,1},{2,10},{10,2},{3,11},{11,3},{4,12},{12,4},... | collective-permute-start | bytes 1179656 | tf_op jit(solution)/shard_map/ppermute | solution.py:377
  83.3 7.6 %collective-permute-start.2 = (bf16[32,48,128]{2,1,0:T(8,128)(2,1)S(1)}, bf16[32,48,128]{2,1,0:T(8,128)(2,1)S(1)}, u32[]{:S(2)}, u32[]{:S(2)}) collective-permute-start(bf16[32,48,128]{2,1,0:T(8,128)(2,1)S(1)} %all_to_all.26.own_ref), channel_id=1, source_target_pairs={{0,8},{8,0},{1,9},{9,1},{2,10},{10,2},{3,11},{11,3},{4,12},{12,4},... | collective-permute-start | bytes 1179656 | tf_op jit(solution)/shard_map/ppermute | solution.py:383

commit v10 on v7

--- a/solution.py
+++ b/solution.py
@@ -381,8 +381,8 @@
     grads_own = lax.all_to_all(grads, ("yhi", "row"), 0, 0)
     grads_other = lax.ppermute(grads_own, "core", swap)
     partial = gradient(parity, grads_own, grads_other, gathered)
-    partial = partial.reshape(TAPS, 8, 4, CHAN).transpose(1, 0, 2, 3)
-    over_samples = lax.all_to_all(partial, ("zhi", "zlo"), 0, 0)
+    partial = partial.reshape(TAPS, 4, 2, 4, CHAN).transpose(2, 1, 0, 3, 4).reshape(8, TAPS, 4, CHAN)
+    over_samples = lax.all_to_all(partial, ("zlo", "zhi"), 0, 0)
     summed = jnp.sum(over_samples.astype(F32), axis=0).astype(BF16)
     final = lax.all_to_all(jnp.broadcast_to(summed[None], (ROWS, TAPS, 4, CHAN)), "row", 0, 0)
     return final.transpose(0, 2, 1, 3).reshape(OUTS, 3, 9, CHAN)

time: 125 us -> 124 us (level)
  the two profiles are of different devices: /device:TPU:1 before, /device:TPU:64 now
where the time goes in v10:
time: 124 us
  blocking collectives  94 us (76%)
  starting transfers between devices  14.5 us (12%)
  Pallas kernels  7.46 us (6%)
  waiting for transfers between devices  4.88 us (4%)
  local copies, waits for them, and re-layouts  2.21 us (2%)
    all_to_all x1, blocking collectives, shards(): parts = lax.all_to_all(pair, ('yhi', 'row'), 0, 0)  24.9 us
    all_to_all x1, blocking collectives, shards(): over_samples = lax.all_to_all(partial, ('zlo', 'zhi'), 0, 0)  20 us
    all_gather x1, blocking collectives, shards(): kernels = lax.all_gather(pairs, 'zhi').reshape(8, TAPS, 4, CHAN)  19.1 us
    all_to_all x1, blocking collectives, shards(): grads_own = lax.all_to_all(grads, ('yhi', 'row'), 0, 0)  18.7 us
    all_to_all x1, blocking collectives, shards(): lax.all_to_all(jnp.broadcast_to(summed[None], (ROWS, TAPS, 4, CHAN)), 'ro...  11.4 us
    all_to_all x1, starting transfers between devices, shards(): gathered = lax.all_to_all(sent, 'row', 0, 0).reshape(GRID_J, 2, SENT, CHAN)  5.46 us
    ppermute x1, starting transfers between devices, shards(): theirs = lax.ppermute(mine, 'zlo', swap)  5.23 us
  transfers between devices with their start and end apart: 4, of which 3 were waited for; matrix products, arithmetic and copies ran while one was open for 1% of the time, Pallas kernels for 0%

profile of v10, /device:TPU:64, one launch (start us, length us, event | category | flops | bytes accessed | tf_op | source)
XLA Modules:
  0.0 123.7 jit_solution(15148038546831796670)
XLA Ops:
  0.0 2.4 %prepare_blocks.1 = (bf16[8,448,256]{2,1,0:T(8,128)(2,1)}, bf16[112,256]{1,0:T(8,128)(2,1)}) custom-call(s32[1]{0:T(128)} %bitcast.1.row_ref, bf16[432,256]{1,0:T(8,128)(2,1)} %bitcast.35, s32[6,1,72]{2,1,0:T(1,128)} %bitcast.38, bf16[27,32,256]{2,1,0:T(8,128)(2,1)} %bitcast.34), custom_call_target="tpu_custom_call" | custom-call | bytes 1990656 | tf_op jit(solution)/shard_map/prepare_blocks/pallas_call | solution.py:111
  2.4 0.0 copy-start.1
  2.5 0.0 copy-start
  2.5 5.5 %all-to-all-start = ((bf16[8,448,256]{2,1,0:T(8,128)(2,1)}), bf16[8,448,256]{2,1,0:T(8,128)(2,1)S(1)}, u32[]{:S(2)}, u32[]{:S(2)}) async-start(bf16[8,448,256]{2,1,0:T(8,128)(2,1)} %get-tuple-element.16), calls=%async_computation | async-start | bytes 3670016 | tf_op jit(solution)/shard_map/all_to_all | solution.py:356
  7.9 0.0 copy-start.2
  7.9 0.0 copy-done.1
  8.0 5.2 %collective-permute-start = (bf16[27,4,256]{2,1,0:T(4,128)(2,1)S(1)}, bf16[27,4,256]{2,1,0:T(4,128)(2,1)S(1)}, u32[]{:S(2)}, u32[]{:S(2)}) collective-permute-start(bf16[27,4,256]{2,1,0:T(4,128)(2,1)S(1)} %reshape.51), channel_id=1, source_target_pairs={{0,1},{1,0},{2,3},{3,2},{4,5},{5,4},{6,7},{7,6},{8,9},{9,8},{10,11... | collective-permute-start | bytes 165896 | tf_op jit(solution)/shard_map/ppermute | solution.py:358
  13.2 0.0 copy-done
  13.2 0.1 reshape.54
  13.3 0.2 copy.23
  13.5 0.1 reshape.55.proj_ref
  13.6 0.0 copy-done.2
  13.6 0.1 copy.19
  13.8 1.5 %collective-permute-done = bf16[27,4,256]{2,1,0:T(4,128)(2,1)S(1)} collective-permute-done((bf16[27,4,256]{2,1,0:T(4,128)(2,1)S(1)}, bf16[27,4,256]{2,1,0:T(4,128)(2,1)S(1)}, u32[]{:S(2)}, u32[]{:S(2)}) %collective-permute-start) | collective-permute-done | bytes 55328 | tf_op jit(solution)/shard_map/ppermute | solution.py:358
  15.4 0.1 pad_maximum_fusion
  15.5 19.1 %all-gather = bf16[8,27,4,256]{3,2,0,1:T(4,128)(2,1)S(1)} all-gather(bf16[2,27,4,256]{3,2,0,1:T(4,128)(2,1)S(1)} %pad_maximum_fusion), channel_id=2, replica_groups=mesh['row'=8,'yhi'=4,'core'=2,'zhi'=4,'zlo'=2] {'zhi'}, dimensions={0}, use_global_device_ids=true | all-gather | bytes 552960 | tf_op jit(solution)/shard_map/all_gather | solution.py:361
  34.5 0.1 reshape.53.weights_ref
  34.6 0.0 all-to-all-done
  34.7 2.2 %forward_taps.1 = (bf16[32,48,128]{2,1,0:T(8,128)(2,1)S(1)}, bf16[32,48,128]{2,1,0:T(8,128)(2,1)S(1)}) custom-call(s32[1]{0:T(128)} %bitcast.core_ref.parity_ref, bf16[4,2,448,256]{3,2,1,0:T(8,128)(2,1)S(1)} %bitcast.28, bf16[864,256]{1,0:T(8,128)(2,1)S(1)} %reshape.53.weights_ref), custom_call_target="tpu_custom_call" | custom-call | flops 1528823808 | bytes 4000000 | tf_op jit(solution)/shard_map/forward_taps/pallas_call | solution.py:178
  36.9 1.9 %collective-permute-start.1 = (bf16[32,48,128]{2,1,0:T(8,128)(2,1)S(1)}, bf16[32,48,128]{2,1,0:T(8,128)(2,1)S(1)}, u32[]{:S(2)}, u32[]{:S(2)}) collective-permute-start(bf16[32,48,128]{2,1,0:T(8,128)(2,1)S(1)} %get-tuple-element.20), channel_id=1, source_target_pairs={{0,8},{8,0},{1,9},{9,1},{2,10},{10,2},{3,11},{11,3},{4,12},{12,4},... | collective-permute-start | bytes 1179656 | tf_op jit(solution)/shard_map/ppermute | solution.py:376
  38.8 1.7 %collective-permute-done.1 = bf16[32,48,128]{2,1,0:T(8,128)(2,1)S(1)} collective-permute-done((bf16[32,48,128]{2,1,0:T(8,128)(2,1)S(1)}, bf16[32,48,128]{2,1,0:T(8,128)(2,1)S(1)}, u32[]{:S(2)}, u32[]{:S(2)}) %collective-permute-start.1) | collective-permute-done | bytes 393248 | tf_op jit(solution)/shard_map/ppermute | solution.py:376
  40.5 0.1 add_convert_fusion
  40.6 24.9 %all_to_all.25.parts_ref = bf16[32,48,128]{2,1,0:T(8,128)(2,1)S(1)} all-to-all(bf16[32,48,128]{2,1,0:T(8,128)(2,1)S(1)} %add_convert_fusion), channel_id=1, replica_groups=mesh['row'=8,'yhi'=4,'core'=2,'zhi'=4,'zlo'=2] {'yhi','row'}, dimensions={0} | all-to-all | bytes 786432 | tf_op jit(solution)/shard_map/all_to_all | solution.py:379
  65.5 1.1 tail.1
  66.6 18.7 %all_to_all.26.own_ref = bf16[32,48,128]{2,1,0:T(8,128)(2,1)S(1)} all-to-all(bf16[32,48,128]{2,1,0:T(8,128)(2,1)S(1)} %tail.1), channel_id=1, replica_groups=mesh['row'=8,'yhi'=4,'core'=2,'zhi'=4,'zlo'=2] {'yhi','row'}, dimensions={0} | all-to-all | bytes 786432 | tf_op jit(solution)/shard_map/all_to_all | solution.py:381
  85.3 1.9 %collective-permute-start.2 = (bf16[32,48,128]{2,1,0:T(8,128)(2,1)S(1)}, bf16[32,48,128]{2,1,0:T(8,128)(2,1)S(1)}, u32[]{:S(2)}, u32[]{:S(2)}) collective-permute-start(bf16[32,48,128]{2,1,0:T(8,128)(2,1)S(1)} %all_to_all.26.own_ref), channel_id=1, source_target_pairs={{0,8},{8,0},{1,9},{9,1},{2,10},{10,2},{3,11},{11,3},{4,12},{12,4},... | collective-permute-start | bytes 1179656 | tf_op jit(solution)/shard_map/ppermute | solution.py:382
  87.2 1.7 %collective-permute-done.2.other_ref = bf16[32,48,128]{2,1,0:T(8,128)(2,1)S(1)} collective-permute-done((bf16[32,48,128]{2,1,0:T(8,128)(2,1)S(1)}, bf16[32,48,128]{2,1,0:T(8,128)(2,1)S(1)}, u32[]{:S(2)}, u32[]{:S(2)}) %collective-permute-start.2) | collective-permute-done | bytes 393248 | tf_op jit(solution)/shard_map/ppermute | solution.py:382
  88.9 1.8 %gradient_taps.1 = bf16[864,256]{1,0:T(8,128)(2,1)S(1)} custom-call(s32[1]{0:T(128)} %bitcast.core_ref.parity_ref, bf16[32,48,128]{2,1,0:T(8,128)(2,1)S(1)} %all_to_all.26.own_ref, bf16[32,48,128]{2,1,0:T(8,128)(2,1)S(1)} %collective-permute-done.2.other_ref, bf16[4,2,448,256]{3,2,1,0:T(8,128)(2,1)S(1)} %bitcast.29), custom_call_target="tpu_custom_call" | custom-call | flops 1528823808 | bytes 4000000 | tf_op jit(solution)/shard_map/gradient_taps/pallas_call | solution.py:326
  90.7 0.1 reshape.59
  90.8 0.2 copy.20
  90.9 20.0 %all_to_all.27 = bf16[8,27,4,256]{3,2,1,0:T(4,128)(2,1)S(1)} all-to-all(bf16[8,27,4,256]{3,2,1,0:T(4,128)(2,1)S(1)} %bitcast.30), channel_id=1, replica_groups=mesh['row'=8,'yhi'=4,'core'=2,'zhi'=4,'zlo'=2] {'zlo','zhi'}, dimensions={0} | all-to-all | bytes 884736 | tf_op jit(solution)/shard_map/all_to_all | solution.py:385
  110.9 0.2 reduce_sum.12
  111.1 0.1 broadcast_in_dim.2
  111.2 11.4 %all_to_all.28 = bf16[8,27,4,256]{3,2,1,0:T(4,128)(2,1)S(1)} all-to-all(bf16[8,27,4,256]{3,2,1,0:T(4,128)(2,1)S(1)} %broadcast_in_dim.2), channel_id=1, replica_groups=mesh['row'=8,'yhi'=4,'core'=2,'zhi'=4,'zlo'=2] {'row'}, dimensions={0} | all-to-all | bytes 884736 | tf_op jit(solution)/shard_map/all_to_all | solution.py:387
  122.6 0.2 copy.21
  122.8 0.9 reshape.61
  (7 shorter events, 0.1 us)
Async XLA Ops:
  2.4 5.5 %copy-start.1 = (bf16[112,256]{1,0:T(8,128)(2,1)S(1)}, bf16[112,256]{1,0:T(8,128)(2,1)}, u32[]{:S(2)}) copy-start(bf16[112,256]{1,0:T(8,128)(2,1)} %get-tuple-element.15) | copy-start | bytes 172036
  2.5 10.8 %copy-start = (bf16[768,256]{1,0:T(8,128)(2,1)S(1)}, bf16[768,256]{1,0:T(8,128)(2,1)}, u32[]{:S(2)}) copy-start(bf16[768,256]{1,0:T(8,128)(2,1)} %param.7) | copy-start | bytes 1179652
  2.5 32.2 %all-to-all-start = ((bf16[8,448,256]{2,1,0:T(8,128)(2,1)}), bf16[8,448,256]{2,1,0:T(8,128)(2,1)S(1)}, u32[]{:S(2)}, u32[]{:S(2)}) async-start(bf16[8,448,256]{2,1,0:T(8,128)(2,1)} %get-tuple-element.16), calls=%async_computation | async-start | bytes 3670016 | tf_op jit(solution)/shard_map/all_to_all | solution.py:356
  7.9 5.7 %copy-start.2 = (bf16[256,3]{0,1:T(4,128)(2,1)S(1)}, bf16[256,3]{0,1:T(4,128)(2,1)}, u32[]{:S(2)}) copy-start(bf16[256,3]{0,1:T(4,128)(2,1)} %param.8) | copy-start | bytes 4612
  8.0 7.4 %collective-permute-start = (bf16[27,4,256]{2,1,0:T(4,128)(2,1)S(1)}, bf16[27,4,256]{2,1,0:T(4,128)(2,1)S(1)}, u32[]{:S(2)}, u32[]{:S(2)}) collective-permute-start(bf16[27,4,256]{2,1,0:T(4,128)(2,1)S(1)} %reshape.51), channel_id=1, source_target_pairs={{0,1},{1,0},{2,3},{3,2},{4,5},{5,4},{6,7},{7,6},{8,9},{9,8},{10,11... | collective-permute-start | bytes 165896 | tf_op jit(solution)/shard_map/ppermute | solution.py:358
  36.9 3.6 %collective-permute-start.1 = (bf16[32,48,128]{2,1,0:T(8,128)(2,1)S(1)}, bf16[32,48,128]{2,1,0:T(8,128)(2,1)S(1)}, u32[]{:S(2)}, u32[]{:S(2)}) collective-permute-start(bf16[32,48,128]{2,1,0:T(8,128)(2,1)S(1)} %get-tuple-element.20), channel_id=1, source_target_pairs={{0,8},{8,0},{1,9},{9,1},{2,10},{10,2},{3,11},{11,3},{4,12},{12,4},... | collective-permute-start | bytes 1179656 | tf_op jit(solution)/shard_map/ppermute | solution.py:376
  85.3 3.6 %collective-permute-start.2 = (bf16[32,48,128]{2,1,0:T(8,128)(2,1)S(1)}, bf16[32,48,128]{2,1,0:T(8,128)(2,1)S(1)}, u32[]{:S(2)}, u32[]{:S(2)}) collective-permute-start(bf16[32,48,128]{2,1,0:T(8,128)(2,1)S(1)} %all_to_all.26.own_ref), channel_id=1, source_target_pairs={{0,8},{8,0},{1,9},{9,1},{2,10},{10,2},{3,11},{11,3},{4,12},{12,4},... | collective-permute-start | bytes 1179656 | tf_op jit(solution)/shard_map/ppermute | solution.py:382

commit v11 on v10

--- a/solution.py
+++ b/solution.py
@@ -342,7 +342,7 @@
 
 
 def shards(features, weights, proj, classify, labels):
-    row = lax.axis_index("row")
+    row = lax.axis_index(("step", "parity"))
     core = lax.axis_index("core")
     part = lax.axis_index("yhi") * ROWS + row
     swap = [(0, 1), (1, 0)]
@@ -353,7 +353,7 @@
         labels.transpose(1, 0, 2),
         weights.transpose(1, 2, 0, 3).reshape(TAPS, OUTS, CHAN),
     )
-    gathered = lax.all_to_all(sent, "row", 0, 0).reshape(GRID_J, 2, SENT, CHAN)
+    gathered = lax.all_to_all(sent, ("step", "parity"), 0, 0).reshape(GRID_J, 2, SENT, CHAN)
     mine = mine[: 4 * TAPS].reshape(TAPS, 4, CHAN)
     theirs = lax.ppermute(mine, "zlo", swap)
     even = lax.axis_index("zlo") == 0
@@ -376,27 +376,28 @@
     received = lax.ppermute(other, "core", swap)
     pair = (own.astype(F32) + received.astype(F32)).astype(BF16)
 
-    parts = lax.all_to_all(pair, ("yhi", "row"), 0, 0)
+    parts = lax.all_to_all(pair, ("yhi", "step", "parity"), 0, 0)
     grads = tail(part, parts, mixing, heads, heads_t, marks)
-    grads_own = lax.all_to_all(grads, ("yhi", "row"), 0, 0)
+    grads_own = lax.all_to_all(grads, ("yhi", "step", "parity"), 0, 0)
     grads_other = lax.ppermute(grads_own, "core", swap)
     partial = gradient(parity, grads_own, grads_other, gathered)
     partial = partial.reshape(TAPS, 4, 2, 4, CHAN).transpose(2, 1, 0, 3, 4).reshape(8, TAPS, 4, CHAN)
     over_samples = lax.all_to_all(partial, ("zlo", "zhi"), 0, 0)
     summed = jnp.sum(over_samples.astype(F32), axis=0).astype(BF16)
-    final = lax.all_to_all(jnp.broadcast_to(summed[None], (ROWS, TAPS, 4, CHAN)), "row", 0, 0)
-    return final.transpose(0, 2, 1, 3).reshape(OUTS, 3, 9, CHAN)
+    final = lax.all_to_all(jnp.broadcast_to(summed[None], (ROWS, TAPS, 4, CHAN)), ("parity", "step"), 0, 0)
+    final = final.reshape(2, GRID_J, TAPS, 4, CHAN).transpose(1, 0, 3, 2, 4)
+    return final.reshape(OUTS, 3, 9, CHAN)
 
 
 def solution(mesh):
-    split = Mesh(mesh.devices.reshape(8, 4, 2, 4, 2), ("row", "yhi", "core", "zhi", "zlo"))
+    split = Mesh(mesh.devices.reshape(4, 2, 4, 2, 4, 2), ("step", "parity", "yhi", "core", "zhi", "zlo"))
     sample, channel = ("zhi", "zlo"), ("yhi", "core")
     in_specs = (
-        P(sample, "row", None, channel),
+        P(sample, ("step", "parity"), None, channel),
         P(sample, None, None, channel),
         P(),
         P(),
-        P(sample, "row", None),
+        P(sample, ("step", "parity"), None),
     )
     out_specs = P(sample, None, None, channel)
     return jax.shard_map(shards, mesh=split, in_specs=in_specs, out_specs=out_specs, check_vma=False)

time: 124 us -> 124 us (level)
  no operation moved by 1% of the time
where the time goes in v11:
time: 124 us
  blocking collectives  94.2 us (76%)
  starting transfers between devices  14.5 us (12%)
  Pallas kernels  7.46 us (6%)
  waiting for transfers between devices  4.88 us (4%)
  local copies, waits for them, and re-layouts  2.21 us (2%)
    all_to_all x1, blocking collectives, shards(): parts = lax.all_to_all(pair, ('yhi', 'step', 'parity'), 0, 0)  24.9 us
    all_to_all x1, blocking collectives, shards(): over_samples = lax.all_to_all(partial, ('zlo', 'zhi'), 0, 0)  20 us
    all_gather x1, blocking collectives, shards(): kernels = lax.all_gather(pairs, 'zhi').reshape(8, TAPS, 4, CHAN)  19.1 us
    all_to_all x1, blocking collectives, shards(): grads_own = lax.all_to_all(grads, ('yhi', 'step', 'parity'), 0, 0)  18.7 us
    all_to_all x1, blocking collectives, shards(): lax.all_to_all(jnp.broadcast_to(summed[None], (ROWS, TAPS, 4, CHAN)), ('p...  11.6 us
    all_to_all x1, starting transfers between devices, shards(): lax.all_to_all(sent, ('step', 'parity'), 0, 0)  5.46 us
    ppermute x1, starting transfers between devices, shards(): theirs = lax.ppermute(mine, 'zlo', swap)  5.23 us
  transfers between devices with their start and end apart: 4, of which 3 were waited for; matrix products, arithmetic and copies ran while one was open for 1% of the time, Pallas kernels for 0%

profile of v11, /device:TPU:64, one launch (start us, length us, event | category | flops | bytes accessed | tf_op | source)
XLA Modules:
  0.0 123.9 jit_solution(911597967849088525)
XLA Ops:
  0.0 2.4 %prepare_blocks.1 = (bf16[8,448,256]{2,1,0:T(8,128)(2,1)}, bf16[112,256]{1,0:T(8,128)(2,1)}) custom-call(s32[1]{0:T(128)} %bitcast.1.row_ref, bf16[432,256]{1,0:T(8,128)(2,1)} %bitcast.37, s32[6,1,72]{2,1,0:T(1,128)} %bitcast.40, bf16[27,32,256]{2,1,0:T(8,128)(2,1)} %bitcast.36), custom_call_target="tpu_custom_call" | custom-call | bytes 1990656 | tf_op jit(solution)/shard_map/prepare_blocks/pallas_call | solution.py:111
  2.4 0.0 copy-start.1
  2.5 0.0 copy-start
  2.5 5.5 %all-to-all-start = ((bf16[8,448,256]{2,1,0:T(8,128)(2,1)}), bf16[8,448,256]{2,1,0:T(8,128)(2,1)S(1)}, u32[]{:S(2)}, u32[]{:S(2)}) async-start(bf16[8,448,256]{2,1,0:T(8,128)(2,1)} %get-tuple-element.16), calls=%async_computation | async-start | bytes 3670016 | tf_op jit(solution)/shard_map/all_to_all | solution.py:356
  7.9 0.0 copy-start.2
  7.9 0.0 copy-done.1
  8.0 5.2 %collective-permute-start = (bf16[27,4,256]{2,1,0:T(4,128)(2,1)S(1)}, bf16[27,4,256]{2,1,0:T(4,128)(2,1)S(1)}, u32[]{:S(2)}, u32[]{:S(2)}) collective-permute-start(bf16[27,4,256]{2,1,0:T(4,128)(2,1)S(1)} %reshape.54), channel_id=1, source_target_pairs={{0,1},{1,0},{2,3},{3,2},{4,5},{5,4},{6,7},{7,6},{8,9},{9,8},{10,11... | collective-permute-start | bytes 165896 | tf_op jit(solution)/shard_map/ppermute | solution.py:358
  13.2 0.0 copy-done
  13.2 0.1 reshape.57
  13.3 0.2 copy.19
  13.5 0.1 reshape.58.proj_ref
  13.6 0.0 copy-done.2
  13.6 0.1 copy.15
  13.8 1.5 %collective-permute-done = bf16[27,4,256]{2,1,0:T(4,128)(2,1)S(1)} collective-permute-done((bf16[27,4,256]{2,1,0:T(4,128)(2,1)S(1)}, bf16[27,4,256]{2,1,0:T(4,128)(2,1)S(1)}, u32[]{:S(2)}, u32[]{:S(2)}) %collective-permute-start) | collective-permute-done | bytes 55328 | tf_op jit(solution)/shard_map/ppermute | solution.py:358
  15.4 0.1 pad_maximum_fusion
  15.5 19.1 %all-gather = bf16[8,27,4,256]{3,2,0,1:T(4,128)(2,1)S(1)} all-gather(bf16[2,27,4,256]{3,2,0,1:T(4,128)(2,1)S(1)} %pad_maximum_fusion), channel_id=2, replica_groups=mesh['step'=4,'parity'=2,'yhi'=4,'core'=2,'zhi'=4,'zlo'=2] {'zhi'}, dimensions={0}, use_global_device_ids=true | all-gather | bytes 552960 | tf_op jit(solution)/shard_map/all_gather | solution.py:361
  34.5 0.1 reshape.56.weights_ref
  34.6 0.0 all-to-all-done
  34.7 2.2 %forward_taps.1 = (bf16[32,48,128]{2,1,0:T(8,128)(2,1)S(1)}, bf16[32,48,128]{2,1,0:T(8,128)(2,1)S(1)}) custom-call(s32[1]{0:T(128)} %bitcast.core_ref.parity_ref, bf16[4,2,448,256]{3,2,1,0:T(8,128)(2,1)S(1)} %bitcast.30, bf16[864,256]{1,0:T(8,128)(2,1)S(1)} %reshape.56.weights_ref), custom_call_target="tpu_custom_call" | custom-call | flops 1528823808 | bytes 4000000 | tf_op jit(solution)/shard_map/forward_taps/pallas_call | solution.py:178
  36.9 1.9 %collective-permute-start.1 = (bf16[32,48,128]{2,1,0:T(8,128)(2,1)S(1)}, bf16[32,48,128]{2,1,0:T(8,128)(2,1)S(1)}, u32[]{:S(2)}, u32[]{:S(2)}) collective-permute-start(bf16[32,48,128]{2,1,0:T(8,128)(2,1)S(1)} %get-tuple-element.20), channel_id=1, source_target_pairs={{0,8},{8,0},{1,9},{9,1},{2,10},{10,2},{3,11},{11,3},{4,12},{12,4},... | collective-permute-start | bytes 1179656 | tf_op jit(solution)/shard_map/ppermute | solution.py:376
  38.8 1.7 %collective-permute-done.1 = bf16[32,48,128]{2,1,0:T(8,128)(2,1)S(1)} collective-permute-done((bf16[32,48,128]{2,1,0:T(8,128)(2,1)S(1)}, bf16[32,48,128]{2,1,0:T(8,128)(2,1)S(1)}, u32[]{:S(2)}, u32[]{:S(2)}) %collective-permute-start.1) | collective-permute-done | bytes 393248 | tf_op jit(solution)/shard_map/ppermute | solution.py:376
  40.5 0.1 add_convert_fusion
  40.6 24.9 %all_to_all.25.parts_ref = bf16[32,48,128]{2,1,0:T(8,128)(2,1)S(1)} all-to-all(bf16[32,48,128]{2,1,0:T(8,128)(2,1)S(1)} %add_convert_fusion), channel_id=1, replica_groups=mesh['step'=4,'parity'=2,'yhi'=4,'core'=2,'zhi'=4,'zlo'=2] {'yhi','step'..., dimensions={0} | all-to-all | bytes 786432 | tf_op jit(solution)/shard_map/all_to_all | solution.py:379
  65.5 1.1 tail.1
  66.6 18.7 %all_to_all.26.own_ref = bf16[32,48,128]{2,1,0:T(8,128)(2,1)S(1)} all-to-all(bf16[32,48,128]{2,1,0:T(8,128)(2,1)S(1)} %tail.1), channel_id=1, replica_groups=mesh['step'=4,'parity'=2,'yhi'=4,'core'=2,'zhi'=4,'zlo'=2] {'yhi','step'..., dimensions={0} | all-to-all | bytes 786432 | tf_op jit(solution)/shard_map/all_to_all | solution.py:381
  85.3 1.9 %collective-permute-start.2 = (bf16[32,48,128]{2,1,0:T(8,128)(2,1)S(1)}, bf16[32,48,128]{2,1,0:T(8,128)(2,1)S(1)}, u32[]{:S(2)}, u32[]{:S(2)}) collective-permute-start(bf16[32,48,128]{2,1,0:T(8,128)(2,1)S(1)} %all_to_all.26.own_ref), channel_id=1, source_target_pairs={{0,8},{8,0},{1,9},{9,1},{2,10},{10,2},{3,11},{11,3},{4,12},{12,4},... | collective-permute-start | bytes 1179656 | tf_op jit(solution)/shard_map/ppermute | solution.py:382
  87.2 1.7 %collective-permute-done.2.other_ref = bf16[32,48,128]{2,1,0:T(8,128)(2,1)S(1)} collective-permute-done((bf16[32,48,128]{2,1,0:T(8,128)(2,1)S(1)}, bf16[32,48,128]{2,1,0:T(8,128)(2,1)S(1)}, u32[]{:S(2)}, u32[]{:S(2)}) %collective-permute-start.2) | collective-permute-done | bytes 393248 | tf_op jit(solution)/shard_map/ppermute | solution.py:382
  88.9 1.8 %gradient_taps.1 = bf16[864,256]{1,0:T(8,128)(2,1)S(1)} custom-call(s32[1]{0:T(128)} %bitcast.core_ref.parity_ref, bf16[32,48,128]{2,1,0:T(8,128)(2,1)S(1)} %all_to_all.26.own_ref, bf16[32,48,128]{2,1,0:T(8,128)(2,1)S(1)} %collective-permute-done.2.other_ref, bf16[4,2,448,256]{3,2,1,0:T(8,128)(2,1)S(1)} %bitcast.31), custom_call_target="tpu_custom_call" | custom-call | flops 1528823808 | bytes 4000000 | tf_op jit(solution)/shard_map/gradient_taps/pallas_call | solution.py:326
  90.7 0.1 reshape.62
  90.8 0.2 copy.16
  90.9 20.0 %all_to_all.27 = bf16[8,27,4,256]{3,2,1,0:T(4,128)(2,1)S(1)} all-to-all(bf16[8,27,4,256]{3,2,1,0:T(4,128)(2,1)S(1)} %bitcast.32), channel_id=1, replica_groups=mesh['step'=4,'parity'=2,'yhi'=4,'core'=2,'zhi'=4,'zlo'=2] {'zlo','zhi'}, dimensions={0} | all-to-all | bytes 884736 | tf_op jit(solution)/shard_map/all_to_all | solution.py:385
  110.9 0.2 reduce_sum.12
  111.1 0.1 broadcast_in_dim.2
  111.2 11.6 %all_to_all.28 = bf16[8,27,4,256]{3,2,1,0:T(4,128)(2,1)S(1)} all-to-all(bf16[8,27,4,256]{3,2,1,0:T(4,128)(2,1)S(1)} %broadcast_in_dim.2), channel_id=1, replica_groups=mesh['step'=4,'parity'=2,'yhi'=4,'core'=2,'zhi'=4,'zlo'=2] {'parity','st..., dimensions={0} | all-to-all | bytes 884736 | tf_op jit(solution)/shard_map/all_to_all | solution.py:387
  122.8 0.2 copy.17
  123.1 0.9 reshape.65
  (7 shorter events, 0.1 us)
Async XLA Ops:
  2.4 5.5 %copy-start.1 = (bf16[112,256]{1,0:T(8,128)(2,1)S(1)}, bf16[112,256]{1,0:T(8,128)(2,1)}, u32[]{:S(2)}) copy-start(bf16[112,256]{1,0:T(8,128)(2,1)} %get-tuple-element.15) | copy-start | bytes 172036
  2.5 10.8 %copy-start = (bf16[768,256]{1,0:T(8,128)(2,1)S(1)}, bf16[768,256]{1,0:T(8,128)(2,1)}, u32[]{:S(2)}) copy-start(bf16[768,256]{1,0:T(8,128)(2,1)} %param.7) | copy-start | bytes 1179652
  2.5 32.2 %all-to-all-start = ((bf16[8,448,256]{2,1,0:T(8,128)(2,1)}), bf16[8,448,256]{2,1,0:T(8,128)(2,1)S(1)}, u32[]{:S(2)}, u32[]{:S(2)}) async-start(bf16[8,448,256]{2,1,0:T(8,128)(2,1)} %get-tuple-element.16), calls=%async_computation | async-start | bytes 3670016 | tf_op jit(solution)/shard_map/all_to_all | solution.py:356
  7.9 5.7 %copy-start.2 = (bf16[256,3]{0,1:T(4,128)(2,1)S(1)}, bf16[256,3]{0,1:T(4,128)(2,1)}, u32[]{:S(2)}) copy-start(bf16[256,3]{0,1:T(4,128)(2,1)} %param.8) | copy-start | bytes 4612
  8.0 7.4 %collective-permute-start = (bf16[27,4,256]{2,1,0:T(4,128)(2,1)S(1)}, bf16[27,4,256]{2,1,0:T(4,128)(2,1)S(1)}, u32[]{:S(2)}, u32[]{:S(2)}) collective-permute-start(bf16[27,4,256]{2,1,0:T(4,128)(2,1)S(1)} %reshape.54), channel_id=1, source_target_pairs={{0,1},{1,0},{2,3},{3,2},{4,5},{5,4},{6,7},{7,6},{8,9},{9,8},{10,11... | collective-permute-start | bytes 165896 | tf_op jit(solution)/shard_map/ppermute | solution.py:358
  36.9 3.6 %collective-permute-start.1 = (bf16[32,48,128]{2,1,0:T(8,128)(2,1)S(1)}, bf16[32,48,128]{2,1,0:T(8,128)(2,1)S(1)}, u32[]{:S(2)}, u32[]{:S(2)}) collective-permute-start(bf16[32,48,128]{2,1,0:T(8,128)(2,1)S(1)} %get-tuple-element.20), channel_id=1, source_target_pairs={{0,8},{8,0},{1,9},{9,1},{2,10},{10,2},{3,11},{11,3},{4,12},{12,4},... | collective-permute-start | bytes 1179656 | tf_op jit(solution)/shard_map/ppermute | solution.py:376
  85.3 3.6 %collective-permute-start.2 = (bf16[32,48,128]{2,1,0:T(8,128)(2,1)S(1)}, bf16[32,48,128]{2,1,0:T(8,128)(2,1)S(1)}, u32[]{:S(2)}, u32[]{:S(2)}) collective-permute-start(bf16[32,48,128]{2,1,0:T(8,128)(2,1)S(1)} %all_to_all.26.own_ref), channel_id=1, source_target_pairs={{0,8},{8,0},{1,9},{9,1},{2,10},{10,2},{3,11},{11,3},{4,12},{12,4},... | collective-permute-start | bytes 1179656 | tf_op jit(solution)/shard_map/ppermute | solution.py:382
